TPU v7x, 32 devices: a whole 2x2x4 slice. The times are simulated.
32 devices in a mesh: group: 2 (over y), ep: 4 (over z), pd: 4 (over x, core).
Axes of the slice: x: 2, y: 2, z: 4, core: 2. Of those that a mesh axis runs over, the one named last changes fastest.
Arguments:
- tokens: bfloat16 [2048, 7168], P(('group', 'ep'), 'pd'), parts along dimension 0, may hold values from -6 to 6
- expert_ids: int32 [2048, 8], P(('group', 'ep')), parts along dimension 0, may hold values from 0 to 255, all different within a row; in each aligned block of 256 rows (0 to 255, 256 to 511, ...) at most 16 rows name the same one
- gate_scores: float32 [2048, 8], P(('group', 'ep')), parts along dimension 0, may hold values from 0.1 to 1
- gate_weight: bfloat16 [4, 7168, 1024], P('ep', None, 'pd'), may hold values from -0.0625 to 0.0625
- up_weight: bfloat16 [4, 7168, 1024], P('ep', None, 'pd'), may hold values from -0.0625 to 0.0625
- down_weight: bfloat16 [4, 1024, 7168], P('ep', 'pd'), may hold values from -0.1875 to 0.1875
- cache_rows: bfloat16 [32, 32, 576], P(('group', 'ep'), 'pd'), parts along dimension 0, may hold values from -6 to 6
- lengths: int32 [32], P('group'), parts along dimension 0, may hold values from 1 to 32, 256 in all
- destination: int32 [8, 4], P('group'), parts along dimension 0, may hold values from 0 to 3, as said below
- decode_query: bfloat16 [8, 4, 64, 576], P(('group', 'ep'), None, 'pd'), parts along dimension 0, may hold values from -450 to 450
Outputs:
- mixed: bfloat16 [2048, 7168], P(('group', 'ep'), 'pd'), parts along dimension 0
- attended: bfloat16 [8, 4, 64, 512], P(('group', 'ep'), None, 'pd'), parts along dimension 0
There are 2 independent parts, one for each index of `group`. A program takes and returns all parts, laid end to end along the dimension named above; an argument that names none is the same for every part. Nothing has to cross between parts.
Inputs may be any that keep to these rules, and one draw needn't show every extreme that they name: `expert_ids`: each row names 8 different experts; within each aligned block of 256 rows, the rows of one ep index, no expert is named by more than 16 rows. `destination`: each row is a permutation: every decode index receives exactly one request from each ep index.
All inputs are finite; a program needn't handle non-finite values.
Results may differ from a plain program's by a relative error of at most 0.012.
Values may be sent and summed in bfloat16 or wider, within the bound.
No kernel may reach another device: no remote copies, remote signals or barrier semaphores. Data moves between devices by JAX's collectives and lax.ppermute only.
A program may use at most 128 MiB of HBM per device.

v0:
```python
import jax
import jax.numpy as jnp
from jax import lax
from jax.sharding import PartitionSpec as P

TOPK = 8
LATC = 512
CAP = 16


score_scale = 192.0 ** (-0.5)


def window_targets(block_ids, ep_count):
    flat_ids = block_ids.reshape(-1)
    in_window = flat_ids < ep_count
    matches = (flat_ids[:, None] == jnp.arange(ep_count, dtype=jnp.int32)[None, :]) & in_window[
        :, None
    ]
    earlier = jnp.cumsum(matches.astype(jnp.int32), axis=0) - 1
    within = jnp.sum(jnp.where(matches, earlier, 0), axis=1)
    return jnp.where(in_window, flat_ids * CAP + within, ep_count * CAP)


def on_device(
    tokens,
    expert_ids,
    gate_scores,
    gate_weight,
    up_weight,
    down_weight,
    cache_rows,
    lengths,
    destination,
    decode_query,
):
    ep_count = lax.axis_size("ep")
    own_index = lax.axis_index("ep")
    token_count = tokens.shape[0]
    slot_count = ep_count * CAP
    targets = window_targets(expert_ids, ep_count).reshape(token_count, TOPK)
    placement = targets[:, :, None] == jnp.arange(slot_count, dtype=jnp.int32)[None, None, :]
    dispatch = jnp.any(placement, axis=1).astype(jnp.bfloat16)
    own_routes = lax.dynamic_index_in_dim(destination, own_index, 0, keepdims=False)
    routing = (own_routes[None, :] == jnp.arange(ep_count, dtype=jnp.int32)[:, None]).astype(
        jnp.bfloat16
    )
    outgoing = jnp.einsum(
        "dk,kpc->dpc", routing, cache_rows, preferred_element_type=jnp.float32
    ).astype(jnp.bfloat16)
    slot_lengths = jnp.sum(
        jnp.where(destination == own_index, lengths.reshape(ep_count, ep_count), 0), axis=1
    )
    payload = jnp.einsum("ts,td->sd", dispatch, tokens, preferred_element_type=jnp.float32)
    payload = payload.astype(jnp.bfloat16).reshape(ep_count, CAP, -1)
    cache_in = lax.all_to_all(outgoing, "ep", split_axis=0, concat_axis=0, tiled=True)
    arrived = lax.all_to_all(payload, "ep", split_axis=0, concat_axis=0, tiled=True)
    expert_rows = arrived.reshape(slot_count, -1)
    w_gate = gate_weight[0]
    w_up = up_weight[0]
    w_down = down_weight[0]
    shard_piece = lax.all_gather(expert_rows, "pd", axis=1, tiled=True)
    gate_sums = jnp.dot(shard_piece, w_gate, preferred_element_type=jnp.float32)
    up_sums = jnp.dot(shard_piece, w_up, preferred_element_type=jnp.float32)
    hidden = (jax.nn.silu(gate_sums) * up_sums).astype(jnp.bfloat16)
    partial_out = jnp.dot(hidden, w_down, preferred_element_type=jnp.float32)
    expert_out = lax.psum_scatter(
        partial_out.astype(jnp.bfloat16), "pd", scatter_dimension=1, tiled=True
    )
    returned = lax.all_to_all(
        expert_out.reshape(ep_count, CAP, -1), "ep", split_axis=0, concat_axis=0, tiled=True
    )
    returned_rows = returned.reshape(slot_count, -1)
    padded_rows = jnp.concatenate(
        [returned_rows, jnp.zeros((1, returned_rows.shape[1]), returned_rows.dtype)], axis=0
    )
    picked = padded_rows[targets].astype(jnp.float32)
    mixed = jnp.sum(picked * gate_scores[:, :, None], axis=1).astype(jnp.bfloat16)
    queries = decode_query[0]
    head_count = queries.shape[1]
    shard_piece = lax.all_gather(cache_in, "pd", axis=1, tiled=True)
    run_max = jnp.full((ep_count, head_count), -1e30, jnp.float32)
    scores = (
        jnp.einsum("jhc,jtc->jht", queries, shard_piece, preferred_element_type=jnp.float32)
        * score_scale
    )
    positions = jnp.arange(shard_piece.shape[1], dtype=jnp.int32)
    usable = (positions[None, :] < slot_lengths[:, None])[:, None, :]
    piece_max = jnp.max(jnp.where(usable, scores, -1e30), axis=2)
    new_max = jnp.maximum(run_max, piece_max)
    weights = jnp.where(usable, jnp.exp(scores - new_max[:, :, None]), 0.0)
    new_sum = jnp.sum(weights, axis=2)
    latent = shard_piece[:, :, :LATC]
    new_acc = jnp.einsum(
        "jht,jtc->jhc", weights.astype(jnp.bfloat16), latent, preferred_element_type=jnp.float32
    )
    attended = (new_acc / new_sum[:, :, None]).astype(jnp.bfloat16)[None]
    return (mixed, attended)


def solution(mesh):
    in_specs = (
        P(("group", "ep"), "pd"),
        P(("group", "ep"), None),
        P(("group", "ep"), None),
        P("ep", None, "pd"),
        P("ep", None, "pd"),
        P("ep", "pd", None),
        P(("group", "ep"), "pd", None),
        P("group"),
        P("group", None),
        P(("group", "ep"), None, "pd", None),
    )
    out_specs = (P(("group", "ep"), "pd"), P(("group", "ep"), None, "pd", None))
    return jax.shard_map(
        on_device, mesh=mesh, in_specs=in_specs, out_specs=out_specs, check_vma=False
    )
```

profile of v0, /device:TPU:0, one launch (start us, length us, event | category | flops | bytes accessed | tf_op | source)
XLA Modules:
  0.0 108.2 jit_solution(3077413289696763679)
XLA Ops:
  7.2 0.0 copy-start
  7.2 0.0 reduce-scatter.2.cloned.1.call-start
  7.2 0.9 copy.52
  8.1 0.1 eq.63
  8.2 0.1 eq.59
  8.4 1.2 %reduce-window.6 = s32[4,16,128]{2,1,0:T(8,128)S(1)} reduce-window(s32[4,16,128]{2,1,0:T(8,128)S(1)} %fusion.30, s32[]{:T(128)} %constant.17.clone.1), window={size=1x1x128 pad=0_0x0_0x127_0}, to_apply=%region_0.0 | reduce-window | flops 1040384 | bytes 65540 | tf_op jit(solution)/shard_map/reduce-window
  9.5 0.2 slice_reduce_fusion
  9.7 0.2 reduce-window.9
  9.9 0.1 add_bitcast_fusion
  10.1 0.1 reduce_sum.39
  10.2 0.1 copy.54
  10.2 0.7 compare_select_fusion
  11.0 0.1 fusion.16
  11.0 0.0 copy-done
  11.0 0.3 convolution_convert_fusion.1
  11.3 14.3 %all_to_all.15 = bf16[4,16,1792]{2,1,0:T(8,128)(2,1)S(1)} all-to-all(bf16[4,16,1792]{2,1,0:T(8,128)(2,1)S(1)} %bitcast.58), channel_id=1, replica_groups=mesh['group'=2,'ep'=4,'pd'=4] {'ep'}, dimensions={0} | all-to-all | bytes 458752 | tf_op jit(solution)/shard_map/all_to_all | solution.py:57
  25.6 9.3 %all_gather.6 = bf16[64,7168]{1,0:T(8,128)(2,1)S(1)} all-gather(bf16[64,1792]{1,0:T(8,128)(2,1)S(1)} %bitcast.59), channel_id=1, replica_groups=mesh['group'=2,'ep'=4,'pd'=4] {'pd'}, dimensions={1}, use_global_device_ids=true | all-gather | bytes 1146880 | tf_op jit(solution)/shard_map/all_gather | solution.py:62
  34.9 2.7 %fusion.4 = f32[64,256]{1,0:T(8,128)S(1)} fusion(bf16[64,7168]{1,0:T(8,128)(2,1)S(1)} %all_gather.6, bf16[1,7168,256]{2,1,0:T(8,128)(2,1)} %param.13), kind=kOutput, calls=%fused_computation.7 | convolution fusion | flops 234881024 | bytes 4653056 | tf_op jit(solution)/shard_map/dot_general | solution.py:63
  37.7 0.0 copy-start.2
  37.7 0.0 copy-start.5
  37.7 0.0 copy-start.3
  37.7 0.0 copy-start.1
  37.7 0.0 copy-start.4
  37.7 6.4 %convolution_convert_fusion = bf16[64,7168]{1,0:T(8,128)(2,1)} fusion(bf16[1,256,7168]{2,1,0:T(8,128)(2,1)} %param.15, bf16[64,7168]{1,0:T(8,128)(2,1)S(1)} %all_gather.6, bf16[1,7168,256]{2,1,0:T(8,128)(2,1)} %param.14, f32[64,256]{1,0:T(8,128)S(1)} %fusion.4), kind=kOutput, calls=%fused_computation.3 | convolution fusion | flops 470319104 | bytes 9240576 | tf_op jit(solution)/shard_map/dot_general | solution.py:66
  44.1 0.0 reduce-scatter.2.cloned.1.call-update
  44.2 0.0 copy-done.2
  44.2 0.0 copy-done.5
  44.2 0.1 convolution_convert_fusion.2
  44.3 0.6 copy.58
  45.0 3.3 %all-to-all-start.2 = ((bf16[4,8,576]{2,1,0:T(8,128)(2,1)}), bf16[4,8,576]{2,1,0:T(8,128)(2,1)S(1)}, u32[]{:S(2)}, u32[]{:S(2)}) async-start(bf16[4,8,576]{2,1,0:T(8,128)(2,1)} %copy.58), calls=%async_computation.3 | async-start | bytes 81920 | tf_op jit(solution)/shard_map/all_to_all | solution.py:56
  48.2 0.1 copy.55
  48.4 0.1 reshape.90
  48.5 0.0 copy-done.3
  48.5 0.1 reshape.87
  48.6 0.1 select_reduce_fusion.1
  48.7 0.1 iota_compare_fusion.4
  48.8 0.0 copy-done.1
  48.8 0.1 copy.56
  48.9 5.0 %all-to-all-done.2 = bf16[4,8,576]{2,1,0:T(8,128)(2,1)S(1)} async-done(((bf16[4,8,576]{2,1,0:T(8,128)(2,1)}), bf16[4,8,576]{2,1,0:T(8,128)(2,1)S(1)}, u32[]{:S(2)}, u32[]{:S(2)}) %all-to-all-start.2) | async-done | bytes 36896 | tf_op jit(solution)/shard_map/all_to_all | solution.py:56
  53.9 5.5 %all_gather.7 = bf16[4,32,576]{2,0,1:T(4,128)(2,1)S(1)} all-gather(bf16[4,8,576]{2,0,1:T(4,128)(2,1)S(1)} %copy.59), channel_id=1, replica_groups=mesh['group'=2,'ep'=4,'pd'=4] {'pd'}, dimensions={1}, use_global_device_ids=true | all-gather | bytes 184320 | tf_op jit(solution)/shard_map/all_gather | solution.py:81
  59.4 0.0 copy-done.4
  59.4 0.2 select_reduce_fusion
  59.7 7.0 %reduce-scatter.2.cloned.1.call-done = bf16[64,1792]{1,0:T(8,128)(2,1)} async-done(((bf16[64,7168]{1,0:T(8,128)(2,1)}), bf16[64,1792]{1,0:T(8,128)(2,1)}) %reduce-scatter.2.cloned.1.call-update) | async-done | bytes 229392 | tf_op jit(solution)/shard_map/reduce_scatter | solution.py:67
  66.7 4.6 %all-to-all-start.1 = ((bf16[4,16,1792]{2,1,0:T(8,128)(2,1)}), bf16[4,16,1792]{2,1,0:T(8,128)(2,1)S(1)}, u32[]{:S(2)}, u32[]{:S(2)}) async-start(bf16[4,16,1792]{2,1,0:T(8,128)(2,1)} %bitcast.60), calls=%async_computation.2 | async-start | bytes 458752 | tf_op jit(solution)/shard_map/all_to_all | solution.py:70
  71.3 0.2 bitcast_reduce_fusion
  71.5 0.9 fusion.7
  72.4 7.2 %all-to-all-done.1 = bf16[4,16,1792]{2,1,0:T(8,128)(2,1)S(1)} async-done(((bf16[4,16,1792]{2,1,0:T(8,128)(2,1)}), bf16[4,16,1792]{2,1,0:T(8,128)(2,1)S(1)}, u32[]{:S(2)}, u32[]{:S(2)}) %all-to-all-start.1) | async-done | bytes 229408 | tf_op jit(solution)/shard_map/all_to_all | solution.py:70
  79.6 10.6 %gather_fusion = bf16[2048,1792]{1,0:T(8,128)(2,1)} fusion(bf16[65,1792]{1,0:T(8,128)(2,1)S(1)} %concatenate.3, s32[2048]{0:T(1024)S(1)} %broadcast_clamp_fusion), kind=kCustom, calls=%fused_computation | custom fusion | bytes 14688256 | tf_op jit(solution)/shard_map/gather | solution.py:77
  90.2 11.2 %fusion = bf16[256,1792]{1,0:T(8,128)(2,1)} fusion(bf16[2048,1792]{1,0:T(8,128)(2,1)} %gather_fusion, f32[256,8]{1,0:T(8,128)S(1)} %copy.56), kind=kLoop, calls=%fused_computation.2 | loop fusion | flops 10551296 | bytes 8265728 | tf_op jit(solution)/shard_map/reduce_sum | solution.py:78
  (10 shorter events, 0.1 us)
Async XLA Ops:
  7.2 3.9 %copy-start = (bf16[256,1792]{1,0:T(8,128)(2,1)S(1)}, bf16[256,1792]{1,0:T(8,128)(2,1)}, u32[]{:S(2)}) copy-start(bf16[256,1792]{1,0:T(8,128)(2,1)} %param.10) | copy-start | bytes 2752516
  7.2 59.5 %reduce-scatter.2.cloned.1.call-start = ((), (), s32[]{:S(2)}) async-start(), calls=%async_computation.4 | async-start | bytes 1146880 | tf_op jit(solution)/shard_map/reduce_scatter | solution.py:67
  37.7 6.5 %copy-start.2 = (s32[4,4]{1,0:T(4,128)S(1)}, s32[4,4]{1,0:T(4,128)}, u32[]{:S(2)}) copy-start(s32[4,4]{1,0:T(4,128)} %param.18) | copy-start | bytes 196
  37.7 6.5 %copy-start.5 = (bf16[4,8,576]{2,1,0:T(8,128)(2,1)S(1)}, bf16[4,8,576]{2,1,0:T(8,128)(2,1)}, u32[]{:S(2)}) copy-start(bf16[4,8,576]{2,1,0:T(8,128)(2,1)} %param.16) | copy-start | bytes 110596
  37.7 10.8 %copy-start.3 = (s32[16]{0:T(128)S(1)}, s32[16]{0:T(128)}, u32[]{:S(2)}) copy-start(s32[16]{0:T(128)} %param.17) | copy-start | bytes 196
  37.7 11.1 %copy-start.1 = (f32[256,8]{0,1:T(8,128)S(1)}, f32[256,8]{0,1:T(8,128)}, u32[]{:S(2)}) copy-start(f32[256,8]{0,1:T(8,128)} %param.12) | copy-start | bytes 24580
  37.7 21.7 %copy-start.4 = (bf16[1,4,16,576]{3,2,1,0:T(8,128)(2,1)S(1)}, bf16[1,4,16,576]{3,2,1,0:T(8,128)(2,1)}, u32[]{:S(2)}) copy-start(bf16[1,4,16,576]{3,2,1,0:T(8,128)(2,1)} %param.19) | copy-start | bytes 221188
  45.0 8.9 %all-to-all-start.2 = ((bf16[4,8,576]{2,1,0:T(8,128)(2,1)}), bf16[4,8,576]{2,1,0:T(8,128)(2,1)S(1)}, u32[]{:S(2)}, u32[]{:S(2)}) async-start(bf16[4,8,576]{2,1,0:T(8,128)(2,1)} %copy.58), calls=%async_computation.3 | async-start | bytes 81920 | tf_op jit(solution)/shard_map/all_to_all | solution.py:56
  66.7 12.8 %all-to-all-start.1 = ((bf16[4,16,1792]{2,1,0:T(8,128)(2,1)}), bf16[4,16,1792]{2,1,0:T(8,128)(2,1)S(1)}, u32[]{:S(2)}, u32[]{:S(2)}) async-start(bf16[4,16,1792]{2,1,0:T(8,128)(2,1)} %bitcast.60), calls=%async_computation.2 | async-start | bytes 458752 | tf_op jit(solution)/shard_map/all_to_all | solution.py:70
Sparse Core Ops, SparseCore 0:
  44.3 22.4 reduce-scatter.1
where the time goes:
time: 109 us; the launch traced here: 108 us
  blocking collectives  29.1 us (27%)
  waiting for transfers between devices  19.2 us (18%)
  between operations  14.2 us (13%)
  other arithmetic  13.8 us (13%)
  local copies, waits for them, and re-layouts  13.3 us (12%)
  matrix products  10.7 us (10%)
  starting transfers between devices  7.89 us (7%)
    all_to_all x1, blocking collectives, on_device(): lax.all_to_all(payload, 'ep', split_axis=0, concat_axis=0, tiled=True)  14.3 us
    reduce_sum x1, other arithmetic, on_device(): jnp.sum(picked * gate_scores[:, :, None], axis=1).astype(jnp.bfloat16)  11.2 us
    gather x1, local copies, waits for them, and re-layouts, on_device(): picked = padded_rows[targets].astype(jnp.float32)  10.6 us
    all_gather x1, blocking collectives, on_device(): shard_piece = lax.all_gather(expert_rows, 'pd', axis=1, tiled=True)  9.3 us
    all_to_all x1, waiting for transfers between devices, on_device(): lax.all_to_all(expert_out.reshape(ep_count, CAP, -1), 'ep', split_axis=0,...  7.19 us
    reduce_scatter x1, waiting for transfers between devices, on_device(): lax.psum_scatter(partial_out.astype(jnp.bfloat16), 'pd', scatter_dimensio...  7.04 us
    dot_general x1, matrix products, on_device(): partial_out = jnp.dot(hidden, w_down, preferred_element_type=jnp.float32)  6.41 us
    all_gather x1, blocking collectives, on_device(): shard_piece = lax.all_gather(cache_in, 'pd', axis=1, tiled=True)  5.52 us
  transfers between devices with their start and end apart: 3, of which 3 were waited for; matrix products, arithmetic and copies ran while one was open for 3% of the time, Pallas kernels for 0%

commit v1 on v0

v1 whole, which is shorter than its diff:
```python
import jax
import jax.numpy as jnp
from jax import lax
from jax.sharding import PartitionSpec as P

LATC = 512
CAP = 16

score_scale = 192.0 ** (-0.5)


def swap(value, axis, mask):
    count = lax.axis_size(axis)
    return lax.ppermute(value, axis, [(i, i ^ mask) for i in range(count)])


def on_device(
    tokens,
    expert_ids,
    gate_scores,
    gate_weight,
    up_weight,
    down_weight,
    cache_rows,
    lengths,
    destination,
    decode_query,
):
    ep_count = lax.axis_size("ep")
    own = lax.axis_index("ep")
    pd_count = lax.axis_size("pd")
    me = lax.axis_index("pd")
    token_count, width = tokens.shape
    bf16, f32 = jnp.bfloat16, jnp.float32
    partners = own ^ jnp.arange(ep_count, dtype=jnp.int32)

    ids = expert_ids.T
    gates = gate_scores.T
    named = ids[None] == partners[:, None, None]
    served = jnp.any(named, axis=1)
    gate = jnp.sum(jnp.where(named, gates[None], 0.0), axis=1)
    steps = jnp.arange(token_count, dtype=jnp.int32)
    earlier = (steps[:, None] < steps[None, :]).astype(bf16)
    rank = jnp.dot(served.astype(bf16), earlier, preferred_element_type=f32).astype(jnp.int32)
    slots = jnp.arange(CAP, dtype=jnp.int32)
    chosen = served[:, None, :] & (rank[:, None, :] == slots[None, :, None])
    dispatch = chosen.astype(bf16).reshape(ep_count * CAP, token_count)
    combine = jnp.where(chosen, gate[:, None, :], 0.0).reshape(ep_count * CAP, token_count)

    payload = jnp.dot(dispatch, tokens, preferred_element_type=f32).astype(bf16)
    payload = payload.reshape(ep_count, CAP, width)

    routes = lax.dynamic_index_in_dim(destination, own, 0, keepdims=False)
    pick = (routes[None, :] == partners[:, None]).astype(bf16)
    outgoing = jnp.einsum("dk,kpc->dpc", pick, cache_rows, preferred_element_type=f32).astype(bf16)

    rows = [payload[0]] + [swap(payload[d], "ep", d) for d in range(1, ep_count)]
    kept = [outgoing[0]] + [swap(outgoing[d], "ep", d) for d in range(1, ep_count)]
    rows = jnp.concatenate(rows, axis=0)
    kept = jnp.stack(kept, axis=0)

    pieces, caches = {0: rows}, {0: kept}
    bit = pd_count // 2
    while bit:
        for m in list(pieces):
            pieces[m ^ bit] = swap(pieces[m], "pd", bit)
            caches[m ^ bit] = swap(caches[m], "pd", bit)
        bit //= 2

    w_gate, w_up, w_down = gate_weight[0], up_weight[0], down_weight[0]
    gate_sums = up_sums = 0.0
    for m in sorted(pieces):
        start = (me ^ m) * width
        gate_sums += jnp.dot(
            pieces[m],
            lax.dynamic_slice_in_dim(w_gate, start, width, 0),
            preferred_element_type=f32,
        )
        up_sums += jnp.dot(
            pieces[m], lax.dynamic_slice_in_dim(w_up, start, width, 0), preferred_element_type=f32
        )
    hidden = (jax.nn.silu(gate_sums) * up_sums).astype(bf16)
    parts = {}
    for m in sorted(pieces):
        start = (me ^ m) * width
        parts[m] = jnp.dot(
            hidden,
            lax.dynamic_slice_in_dim(w_down, start, width, 1),
            preferred_element_type=f32,
        ).astype(bf16)
    bit = 1
    while bit < pd_count:
        for m in list(parts):
            if m & bit:
                arrived = swap(parts.pop(m), "pd", bit)
                kept_part = parts[m ^ bit].astype(f32) + arrived.astype(f32)
                parts[m ^ bit] = kept_part.astype(bf16)
        bit *= 2
    expert_out = parts[0].reshape(ep_count, CAP, width)
    returned = [expert_out[0]] + [swap(expert_out[d], "ep", d) for d in range(1, ep_count)]
    returned = jnp.concatenate(returned, axis=0)
    high = combine.astype(bf16)
    low = (combine - high.astype(f32)).astype(bf16)
    mixed = jnp.einsum("st,sd->td", high, returned, preferred_element_type=f32)
    mixed += jnp.einsum("st,sd->td", low, returned, preferred_element_type=f32)
    mixed = mixed.astype(bf16)

    order = partners
    queries = decode_query[0][order]
    keys = jnp.concatenate([caches[m] for m in sorted(caches)], axis=1)
    part_rows = cache_rows.shape[1]
    positions = jnp.concatenate(
        [(me ^ m) * part_rows + jnp.arange(part_rows, dtype=jnp.int32) for m in sorted(caches)]
    )
    slot_lengths = jnp.sum(
        jnp.where(destination == own, lengths.reshape(ep_count, ep_count), 0), axis=1
    )[order]
    scores = jnp.einsum("jhc,jtc->jht", queries, keys, preferred_element_type=f32) * score_scale
    usable = (positions[None, :] < slot_lengths[:, None])[:, None, :]
    top = jnp.max(jnp.where(usable, scores, -1e30), axis=2, keepdims=True)
    weights = jnp.where(usable, jnp.exp(scores - top), 0.0)
    total = jnp.sum(weights, axis=2, keepdims=True)
    summed = jnp.einsum(
        "jht,jtc->jhc", weights.astype(bf16), keys[:, :, :LATC], preferred_element_type=f32
    )
    attended = (summed / total).astype(bf16)[order][None]
    return (mixed, attended)


def solution(mesh):
    in_specs = (
        P(("group", "ep"), "pd"),
        P(("group", "ep"), None),
        P(("group", "ep"), None),
        P("ep", None, "pd"),
        P("ep", None, "pd"),
        P("ep", "pd", None),
        P(("group", "ep"), "pd", None),
        P("group"),
        P("group", None),
        P(("group", "ep"), None, "pd", None),
    )
    out_specs = (P(("group", "ep"), "pd"), P(("group", "ep"), None, "pd", None))
    return jax.shard_map(
        on_device, mesh=mesh, in_specs=in_specs, out_specs=out_specs, check_vma=False
    )
```

time: 109 us -> 56.1 us (0.51)
  blocking collectives: 29.1 us -> 0 us
  between operations: 14.2 us -> 1.07 us
  starting transfers between devices: 7.89 us -> 20.1 us
  other arithmetic: 13.8 us -> 3.45 us
  local copies, waits for them, and re-layouts: 13.3 us -> 5 us
  waiting for transfers between devices: 19.2 us -> 15.3 us
    ppermute x0 -> x18, starting transfers between devices: none -> 20.1 us  [swap(): return lax.ppermute(value, axis, [(i, i ^ mask) for i in range(count)])]
    ppermute x0 -> x18, waiting for transfers between devices: none -> 15.3 us  [swap(): return lax.ppermute(value, axis, [(i, i ^ mask) for i in range(count)])]
    all_gather x2 -> x0, blocking collectives: 14.8 us -> none  [the longest x1 9.3 us: on_device(): shard_piece = lax.all_gather(expert_rows, 'pd', axis=1, tiled=True)]
    all_to_all x1 -> x0, blocking collectives: 14.3 us -> none  [on_device(): lax.all_to_all(payload, 'ep', split_axis=0, concat_axis=0, tiled=True)]
    all_to_all x2 -> x0, waiting for transfers between devices: 12.2 us -> none  [the longest x1 7.19 us: on_device(): lax.all_to_all(expert_out.reshape(ep_count, CAP, -1), 'ep', split_axis=0,...]
    reduce_sum x4 -> x2, other arithmetic: 11.5 us -> 1.6 us  [the longest x1 0.8 us: on_device(): gate = jnp.sum(jnp.where(named, gates[None], 0.0), axis=1)]
    all_to_all x2 -> x0, starting transfers between devices: 7.85 us -> none  [the longest x1 4.58 us: on_device(): lax.all_to_all(expert_out.reshape(ep_count, CAP, -1), 'ep', split_axis=0,...]
    gather x1 -> x3, local copies, waits for them, and re-layouts: 10.6 us -> 3.28 us  [the longest x1 1.45 us: on_device(): queries = decode_query[0][order]]
  transfers between devices with their start and end apart: 3 -> 18, of which waited for: 3 -> 5; matrix products, arithmetic and copies ran while one was open for 3% -> 27% of each run, Pallas kernels for 0% -> 0%
where the time goes in v1:
time: 56.1 us; the launch traced here: 55.7 us
  starting transfers between devices  20.1 us (36%)
  waiting for transfers between devices  15.3 us (27%)
  matrix products  10.7 us (19%)
  local copies, waits for them, and re-layouts  5 us (9%)
  other arithmetic  3.45 us (6%)
  between operations  1.07 us (2%)
    ppermute x18, starting transfers between devices, swap(): return lax.ppermute(value, axis, [(i, i ^ mask) for i in range(count)])  20.1 us
    ppermute x18, waiting for transfers between devices, swap(): return lax.ppermute(value, axis, [(i, i ^ mask) for i in range(count)])  15.3 us
    dot_general x4, matrix products, on_device(): jnp.dot(pieces[m], lax.dynamic_slice_in_dim(w_up, start, width, 0), prefe...  3.67 us
    dot_general x4, matrix products, on_device(): jnp.dot(pieces[m], lax.dynamic_slice_in_dim(w_gate, start, width, 0), pre...  2.31 us
    gather x1, local copies, waits for them, and re-layouts, on_device(): queries = decode_query[0][order]  1.45 us
    dot_general x1, matrix products, on_device(): mixed = jnp.einsum('st,sd->td', high, returned, preferred_element_type=f32)  1.35 us
    gather x1, local copies, waits for them, and re-layouts, on_device(): attended = (summed / total).astype(bf16)[order][None]  1.19 us
    dot_general x4, matrix products, on_device(): jnp.dot(hidden, lax.dynamic_slice_in_dim(w_down, start, width, 1), prefer...  1.17 us
  transfers between devices with their start and end apart: 18, of which 5 were waited for; matrix products, arithmetic and copies ran while one was open for 27% of the time, Pallas kernels for 0%

profile of v1, /device:TPU:0, one launch (start us, length us, event | category | flops | bytes accessed | tf_op | source)
XLA Modules:
  0.0 55.7 jit_solution(4491097232670049832)
XLA Ops:
  0.6 0.0 copy-start
  0.7 0.1 eq.61
  0.8 0.9 %compare_reduce_fusion = pred[4,256]{1,0:T(4,128)(4,1)S(1)} fusion(s32[8,256]{1,0:T(8,128)} %bitcast.105, s32[4]{0:T(128)S(1)} %iota_xor_fusion), kind=kLoop, calls=%fused_computation.74 | loop fusion | flops 15360 | bytes 9232 | tf_op jit(solution)/shard_map/reduce_or | solution.py:40
  1.6 0.1 convolution_convert_fusion.6
  1.8 0.1 fusion.43
  1.9 0.3 convolution_convert_fusion.4
  2.2 5.1 %collective-permute-start.2 = (bf16[16,1792]{1,0:T(8,128)(2,1)S(1)}, bf16[16,1792]{1,0:T(8,128)(2,1)S(1)}, u32[]{:S(2)}, u32[]{:S(2)}) collective-permute-start(bf16[16,1792]{1,0:T(8,128)(2,1)S(1)} %get-tuple-element.7), channel_id=1, source_target_pairs={{0,12},{4,8},{8,4},{12,0},{1,13},{5,9},{9,5},{13,1},{2,14},{6,10},... | collective-permute-start | bytes 172040 | tf_op jit(solution)/shard_map/ppermute | solution.py:14
  7.3 0.7 %fusion.76 = s32[4]{0:T(128)S(1)} fusion(s32[4,4]{1,0:T(4,128)} %param.18, s32[]{:T(128)S(6)} %select_n.64), kind=kLoop, calls=%fused_computation.107 | loop fusion | bytes 36 | tf_op jit(solution)/shard_map/eq | solution.py:54
  8.0 1.0 %convolution_convert_fusion.5 = bf16[4,8,576]{2,0,1:T(4,128)(2,1)S(1)} fusion(bf16[4,8,576]{2,1,0:T(8,128)(2,1)} %param.16, s32[4]{0:T(128)S(1)} %fusion.76, s32[4]{0:T(128)S(1)} %iota_xor_fusion), kind=kOutput, calls=%fused_computation.21 | convolution fusion | flops 165904 | bytes 73760 | tf_op jit(solution)/shard_map/dk,kpc->dpc/dot_general | solution.py:55
  9.0 0.1 fusion.86
  9.1 2.0 %collective-permute-start.14 = (bf16[8,576]{1,0:T(8,128)(2,1)S(1)}, bf16[8,576]{1,0:T(8,128)(2,1)S(1)}, u32[]{:S(2)}, u32[]{:S(2)}) collective-permute-start(bf16[8,576]{1,0:T(8,128)(2,1)S(1)} %bitcast.112), channel_id=1, source_target_pairs={{0,12},{4,8},{8,4},{12,0},{1,13},{5,9},{9,5},{13,1},{2,14},{6,10},... | collective-permute-start | bytes 27656 | tf_op jit(solution)/shard_map/ppermute | solution.py:14
  11.0 1.1 %collective-permute-start.13 = (bf16[8,576]{1,0:T(8,128)(2,1)S(1)}, bf16[8,576]{1,0:T(8,128)(2,1)S(1)}, u32[]{:S(2)}, u32[]{:S(2)}) collective-permute-start(bf16[8,576]{1,0:T(8,128)(2,1)S(1)} %bitcast.108), channel_id=1, source_target_pairs={{0,8},{4,12},{8,0},{12,4},{1,9},{5,13},{9,1},{13,5},{2,10},{6,14},... | collective-permute-start | bytes 27656 | tf_op jit(solution)/shard_map/ppermute | solution.py:14
  12.1 1.4 %collective-permute-start.12 = (bf16[8,576]{1,0:T(8,128)(2,1)S(1)}, bf16[8,576]{1,0:T(8,128)(2,1)S(1)}, u32[]{:S(2)}, u32[]{:S(2)}) collective-permute-start(bf16[8,576]{1,0:T(8,128)(2,1)S(1)} %bitcast.110), channel_id=1, source_target_pairs={{0,4},{4,0},{8,12},{12,8},{1,5},{5,1},{9,13},{13,9},{2,6},{6,2},{1... | collective-permute-start | bytes 27656 | tf_op jit(solution)/shard_map/ppermute | solution.py:14
  13.6 0.7 %reshape.98 = s32[4,4]{1,0:T(4,128)S(1)} reshape(s32[16]{0:T(128)} %param.17) | data formatting | bytes 128 | tf_op jit(solution)/shard_map/reshape | solution.py:116
  14.3 0.8 %select_reduce_fusion.1 = s32[4]{0:T(128)S(1)} fusion(s32[4,4]{1,0:T(4,128)S(1)} %reshape.98, s32[4,4]{1,0:T(4,128)} %param.18, s32[]{:T(128)S(6)} %axis_index.23), kind=kLoop, calls=%fused_computation.100 | loop fusion | flops 44 | bytes 148 | tf_op jit(solution)/shard_map/reduce_sum | solution.py:115
  15.1 0.6 %gather_fusion = s32[4]{0:T(128)S(1)} fusion(s32[4]{0:T(128)S(1)} %select_reduce_fusion.1, s32[1024]{0:T(1024)S(1)} %pad_clamp_fusion), kind=kCustom, calls=%fused_computation | custom fusion | bytes 48 | tf_op jit(solution)/shard_map/gather | solution.py:115
  15.8 0.1 pad_add_fusion
  15.8 0.1 broadcast_compare_fusion
  15.9 0.7 %collective-permute-start = (bf16[16,1792]{1,0:T(8,128)(2,1)S(1)}, bf16[16,1792]{1,0:T(8,128)(2,1)S(1)}, u32[]{:S(2)}, u32[]{:S(2)}) collective-permute-start(bf16[16,1792]{1,0:T(8,128)(2,1)S(1)} %get-tuple-element.9), channel_id=1, source_target_pairs={{0,4},{4,0},{8,12},{12,8},{1,5},{5,1},{9,13},{13,9},{2,6},{6,2},{1... | collective-permute-start | bytes 172040 | tf_op jit(solution)/shard_map/ppermute | solution.py:14
  16.7 0.1 pad_maximum_fusion.3
  16.8 1.6 %collective-permute-start.16 = (bf16[4,8,576]{2,0,1:T(4,128)(2,1)S(1)}, bf16[4,8,576]{2,0,1:T(4,128)(2,1)S(1)}, u32[]{:S(2)}, u32[]{:S(2)}) collective-permute-start(bf16[4,8,576]{2,0,1:T(4,128)(2,1)S(1)} %pad_maximum_fusion.3), channel_id=1, source_target_pairs={{0,2},{1,3},{2,0},{3,1},{4,6},{5,7},{6,4},{7,5},{8,10},{9,11},{10,... | collective-permute-start | bytes 110600 | tf_op jit(solution)/shard_map/ppermute | solution.py:14
  18.3 0.8 %fusion.47 = f32[4,256]{1,0:T(4,128)S(1)} fusion(f32[8,256]{1,0:T(8,128)} %bitcast.113, s32[8,256]{1,0:T(8,128)} %bitcast.106, s32[4]{0:T(128)S(1)} %iota_xor_fusion), kind=kLoop, calls=%fused_computation.78 | loop fusion | flops 23552 | bytes 20496 | tf_op jit(solution)/shard_map/reduce_sum | solution.py:41
  19.2 0.1 fusion.42
  19.3 0.1 fusion.41
  19.3 1.5 %gather_fusion.1 = bf16[4,16,576]{2,1,0:T(8,128)(2,1)S(1)} fusion(bf16[4,16,576]{2,1,0:T(8,128)(2,1)} %bitcast.103, s32[1024]{0:T(1024)S(1)} %pad_clamp_fusion), kind=kCustom, calls=%fused_computation.1 | custom fusion | bytes 147472 | tf_op jit(solution)/shard_map/gather | solution.py:109
  20.8 0.0 copy-start.2
  20.8 0.1 collective-permute-start.15
  20.9 0.5 collective-permute-start.17
  21.4 0.0 copy-start.3
  21.5 1.0 %collective-permute-start.4 = (bf16[64,1792]{1,0:T(8,128)(2,1)S(1)}, bf16[64,1792]{1,0:T(8,128)(2,1)S(1)}, u32[]{:S(2)}, u32[]{:S(2)}) collective-permute-start(bf16[64,1792]{1,0:T(8,128)(2,1)S(1)} %pad_maximum_fusion), channel_id=1, source_target_pairs={{0,2},{1,3},{2,0},{3,1},{4,6},{5,7},{6,4},{7,5},{8,10},{9,11},{10,... | collective-permute-start | bytes 688136 | tf_op jit(solution)/shard_map/ppermute | solution.py:14
  22.5 0.2 collective-permute-start.3
  22.7 0.2 pad_maximum_fusion.2
  22.9 0.2 convolution_multiply_fusion
  23.0 0.2 fusion.87
  23.2 5.9 %collective-permute-done.4 = bf16[64,1792]{1,0:T(8,128)(2,1)S(1)} collective-permute-done((bf16[64,1792]{1,0:T(8,128)(2,1)S(1)}, bf16[64,1792]{1,0:T(8,128)(2,1)S(1)}, u32[]{:S(2)}, u32[]{:S(2)}) %collective-permute-start.4) | collective-permute-done | bytes 229408 | tf_op jit(solution)/shard_map/ppermute | solution.py:14
  29.1 1.4 %fusion.21 = f32[64,256]{1,0:T(8,128)S(1)} fusion(bf16[64,1792]{1,0:T(8,128)(2,1)S(1)} %collective-permute-done.4, bf16[1,7168,256]{2,1,0:T(8,128)(2,1)} %param.13, s32[]{:T(128)S(6)} %select_n.60), kind=kOutput, calls=%fused_computation.38 | convolution fusion | flops 58720256 | bytes 1212420 | tf_op jit(solution)/shard_map/dot_general | solution.py:74
  30.6 1.5 %fusion.15 = f32[64,256]{1,0:T(8,128)S(1)} fusion(bf16[64,1792]{1,0:T(8,128)(2,1)S(1)} %collective-permute-done.4, bf16[1,7168,256]{2,1,0:T(8,128)(2,1)} %param.14, s32[]{:T(128)S(6)} %select_n.60), kind=kOutput, calls=%fused_computation.32 | convolution fusion | flops 58720256 | bytes 1212420 | tf_op jit(solution)/shard_map/dot_general | solution.py:79
  32.1 0.0 collective-permute-done.3
  32.1 0.3 fusion.23
  32.4 0.0 copy-start.1
  32.4 1.6 %fusion.17 = f32[64,256]{1,0:T(8,128)S(1)} fusion(bf16[64,1792]{1,0:T(8,128)(2,1)S(1)} %collective-permute-done.3, bf16[1,7168,256]{2,1,0:T(8,128)(2,1)} %param.14, s32[]{:T(128)S(6)} %select_n.59), kind=kOutput, calls=%fused_computation.34 | convolution fusion | flops 58720256 | bytes 1212420 | tf_op jit(solution)/shard_map/dot_general | solution.py:79
  34.0 0.3 fusion.6
  34.3 0.3 fusion.5
  34.7 0.3 convolution_add_fusion.3
  35.0 0.3 multiply_convert_fusion
  35.3 0.0 slice-start
  35.3 0.3 convolution_convert_fusion
  35.6 0.6 %collective-permute-start.7 = (bf16[64,1792]{1,0:T(8,128)(2,1)S(1)}, bf16[64,1792]{1,0:T(8,128)(2,1)S(1)}, u32[]{:S(2)}, u32[]{:S(2)}) collective-permute-start(bf16[64,1792]{1,0:T(8,128)(2,1)S(1)} %convolution_convert_fusion), channel_id=1, source_target_pairs={{0,1},{1,0},{2,3},{3,2},{4,5},{5,4},{6,7},{7,6},{8,9},{9,8},{10,11... | collective-permute-start | bytes 688136 | tf_op jit(solution)/shard_map/ppermute | solution.py:14
  36.1 0.3 convolution_convert_fusion.2
  36.4 0.1 collective-permute-start.6
  36.5 0.7 %collective-permute-done.7 = bf16[64,1792]{1,0:T(8,128)(2,1)S(1)} collective-permute-done((bf16[64,1792]{1,0:T(8,128)(2,1)S(1)}, bf16[64,1792]{1,0:T(8,128)(2,1)S(1)}, u32[]{:S(2)}, u32[]{:S(2)}) %collective-permute-start.7) | collective-permute-done | bytes 229408 | tf_op jit(solution)/shard_map/ppermute | solution.py:14
  37.3 0.3 add_convert_fusion.1
  37.6 1.4 %collective-permute-start.8 = (bf16[64,1792]{1,0:T(8,128)(2,1)S(1)}, bf16[64,1792]{1,0:T(8,128)(2,1)S(1)}, u32[]{:S(2)}, u32[]{:S(2)}) collective-permute-start(bf16[64,1792]{1,0:T(8,128)(2,1)S(1)} %add_convert_fusion.1), channel_id=1, source_target_pairs={{0,2},{1,3},{2,0},{3,1},{4,6},{5,7},{6,4},{7,5},{8,10},{9,11},{10,... | collective-permute-start | bytes 688136 | tf_op jit(solution)/shard_map/ppermute | solution.py:14
  39.0 0.3 fusion.3
  39.3 6.2 %collective-permute-done.8 = bf16[64,1792]{1,0:T(8,128)(2,1)S(1)} collective-permute-done((bf16[64,1792]{1,0:T(8,128)(2,1)S(1)}, bf16[64,1792]{1,0:T(8,128)(2,1)S(1)}, u32[]{:S(2)}, u32[]{:S(2)}) %collective-permute-start.8) | collective-permute-done | bytes 229408 | tf_op jit(solution)/shard_map/ppermute | solution.py:14
  45.5 0.1 add_convert_fusion
  45.6 2.9 %collective-permute-start.11 = (bf16[16,1792]{1,0:T(8,128)(2,1)S(1)}, bf16[16,1792]{1,0:T(8,128)(2,1)S(1)}, u32[]{:S(2)}, u32[]{:S(2)}) collective-permute-start(bf16[16,1792]{1,0:T(8,128)(2,1)S(1)} %get-tuple-element.3), channel_id=1, source_target_pairs={{0,12},{4,8},{8,4},{12,0},{1,13},{5,9},{9,5},{13,1},{2,14},{6,10},... | collective-permute-start | bytes 172040 | tf_op jit(solution)/shard_map/ppermute | solution.py:14
  48.5 1.5 %collective-permute-start.9 = (bf16[16,1792]{1,0:T(8,128)(2,1)S(1)}, bf16[16,1792]{1,0:T(8,128)(2,1)S(1)}, u32[]{:S(2)}, u32[]{:S(2)}) collective-permute-start(bf16[16,1792]{1,0:T(8,128)(2,1)S(1)} %get-tuple-element.5), channel_id=1, source_target_pairs={{0,4},{4,0},{8,12},{12,8},{1,5},{5,1},{9,13},{13,9},{2,6},{6,2},{1... | collective-permute-start | bytes 172040 | tf_op jit(solution)/shard_map/ppermute | solution.py:14
  50.1 0.2 fusion.4
  50.3 1.2 %gather_fusion.2 = bf16[4,16,512]{2,1,0:T(8,128)(2,1)} fusion(bf16[4,16,512]{2,1,0:T(8,128)(2,1)S(1)} %fusion.4, s32[1024]{0:T(1024)S(1)} %pad_clamp_fusion), kind=kCustom, calls=%fused_computation.2 | custom fusion | bytes 131088 | tf_op jit(solution)/shard_map/gather | solution.py:126
  51.5 0.2 collective-permute-done.11
  51.7 2.2 %collective-permute-done.10 = bf16[16,1792]{1,0:T(8,128)(2,1)S(1)} collective-permute-done((bf16[16,1792]{1,0:T(8,128)(2,1)S(1)}, bf16[16,1792]{1,0:T(8,128)(2,1)S(1)}, u32[]{:S(2)}, u32[]{:S(2)}) %collective-permute-start.10) | collective-permute-done | bytes 57376 | tf_op jit(solution)/shard_map/ppermute | solution.py:14
  53.9 0.4 fusion.46
  54.3 1.3 %fusion.1 = bf16[256,1792]{1,0:T(8,128)(2,1)} fusion(f32[256,1792]{1,0:T(8,128)S(1)} %fusion.46, bf16[64,256]{1,0:T(8,128)(2,1)S(1)} %fusion.41, bf16[16,1792]{1,0:T(8,128)(2,1)S(1)} %collective-permute-done.11, bf16[16,1792]{1,0:T(8,128)(2,1)S(1)} %collective-permute-done.10, bf16[16,1792]{1,0:T(8,128)(2,1)S(1)} %collective-permute-done.9, ...), kind=kOutput, calls=%fused_computation.5 | convolution fusion | flops 60555264 | bytes 3014656 | tf_op jit(solution)/shard_map/st,sd->td/dot_general | solution.py:104
  (39 shorter events, 0.2 us)
Async XLA Ops:
  0.6 1.2 %copy-start = (bf16[256,1792]{1,0:T(8,128)(2,1)S(1)}, bf16[256,1792]{1,0:T(8,128)(2,1)}, u32[]{:S(2)}) copy-start(bf16[256,1792]{1,0:T(8,128)(2,1)} %param.10) | copy-start | bytes 2752516
  2.2 19.2 %collective-permute-start.2 = (bf16[16,1792]{1,0:T(8,128)(2,1)S(1)}, bf16[16,1792]{1,0:T(8,128)(2,1)S(1)}, u32[]{:S(2)}, u32[]{:S(2)}) collective-permute-start(bf16[16,1792]{1,0:T(8,128)(2,1)S(1)} %get-tuple-element.7), channel_id=1, source_target_pairs={{0,12},{4,8},{8,4},{12,0},{1,13},{5,9},{9,5},{13,1},{2,14},{6,10},... | collective-permute-start | bytes 172040 | tf_op jit(solution)/shard_map/ppermute | solution.py:14
  7.3 14.1 %collective-permute-start.1 = (bf16[16,1792]{1,0:T(8,128)(2,1)S(1)}, bf16[16,1792]{1,0:T(8,128)(2,1)S(1)}, u32[]{:S(2)}, u32[]{:S(2)}) collective-permute-start(bf16[16,1792]{1,0:T(8,128)(2,1)S(1)} %get-tuple-element.8), channel_id=1, source_target_pairs={{0,8},{4,12},{8,0},{12,4},{1,9},{5,13},{9,1},{13,5},{2,10},{6,14},... | collective-permute-start | bytes 172040 | tf_op jit(solution)/shard_map/ppermute | solution.py:14
  9.1 6.9 %collective-permute-start.14 = (bf16[8,576]{1,0:T(8,128)(2,1)S(1)}, bf16[8,576]{1,0:T(8,128)(2,1)S(1)}, u32[]{:S(2)}, u32[]{:S(2)}) collective-permute-start(bf16[8,576]{1,0:T(8,128)(2,1)S(1)} %bitcast.112), channel_id=1, source_target_pairs={{0,12},{4,8},{8,4},{12,0},{1,13},{5,9},{9,5},{13,1},{2,14},{6,10},... | collective-permute-start | bytes 27656 | tf_op jit(solution)/shard_map/ppermute | solution.py:14
  11.0 5.6 %collective-permute-start.13 = (bf16[8,576]{1,0:T(8,128)(2,1)S(1)}, bf16[8,576]{1,0:T(8,128)(2,1)S(1)}, u32[]{:S(2)}, u32[]{:S(2)}) collective-permute-start(bf16[8,576]{1,0:T(8,128)(2,1)S(1)} %bitcast.108), channel_id=1, source_target_pairs={{0,8},{4,12},{8,0},{12,4},{1,9},{5,13},{9,1},{13,5},{2,10},{6,14},... | collective-permute-start | bytes 27656 | tf_op jit(solution)/shard_map/ppermute | solution.py:14
  12.1 4.5 %collective-permute-start.12 = (bf16[8,576]{1,0:T(8,128)(2,1)S(1)}, bf16[8,576]{1,0:T(8,128)(2,1)S(1)}, u32[]{:S(2)}, u32[]{:S(2)}) collective-permute-start(bf16[8,576]{1,0:T(8,128)(2,1)S(1)} %bitcast.110), channel_id=1, source_target_pairs={{0,4},{4,0},{8,12},{12,8},{1,5},{5,1},{9,13},{13,9},{2,6},{6,2},{1... | collective-permute-start | bytes 27656 | tf_op jit(solution)/shard_map/ppermute | solution.py:14
  15.9 5.5 %collective-permute-start = (bf16[16,1792]{1,0:T(8,128)(2,1)S(1)}, bf16[16,1792]{1,0:T(8,128)(2,1)S(1)}, u32[]{:S(2)}, u32[]{:S(2)}) collective-permute-start(bf16[16,1792]{1,0:T(8,128)(2,1)S(1)} %get-tuple-element.9), channel_id=1, source_target_pairs={{0,4},{4,0},{8,12},{12,8},{1,5},{5,1},{9,13},{13,9},{2,6},{6,2},{1... | collective-permute-start | bytes 172040 | tf_op jit(solution)/shard_map/ppermute | solution.py:14
  16.8 4.1 %collective-permute-start.16 = (bf16[4,8,576]{2,0,1:T(4,128)(2,1)S(1)}, bf16[4,8,576]{2,0,1:T(4,128)(2,1)S(1)}, u32[]{:S(2)}, u32[]{:S(2)}) collective-permute-start(bf16[4,8,576]{2,0,1:T(4,128)(2,1)S(1)} %pad_maximum_fusion.3), channel_id=1, source_target_pairs={{0,2},{1,3},{2,0},{3,1},{4,6},{5,7},{6,4},{7,5},{8,10},{9,11},{10,... | collective-permute-start | bytes 110600 | tf_op jit(solution)/shard_map/ppermute | solution.py:14
  20.8 11.3 %copy-start.2 = (bf16[1,7168,256]{2,1,0:T(8,128)(2,1)S(1)}, bf16[1,7168,256]{2,1,0:T(8,128)(2,1)}, u32[]{:S(2)}) copy-start(bf16[1,7168,256]{2,1,0:T(8,128)(2,1)} %param.13) | copy-start | bytes 11010052
  20.8 1.9 %collective-permute-start.15 = (bf16[4,8,576]{2,0,1:T(4,128)(2,1)S(1)}, bf16[4,8,576]{2,0,1:T(4,128)(2,1)S(1)}, u32[]{:S(2)}, u32[]{:S(2)}) collective-permute-start(bf16[4,8,576]{2,0,1:T(4,128)(2,1)S(1)} %pad_maximum_fusion.3), channel_id=1, source_target_pairs={{0,1},{1,0},{2,3},{3,2},{4,5},{5,4},{6,7},{7,6},{8,9},{9,8},{10,11... | collective-permute-start | bytes 110600 | tf_op jit(solution)/shard_map/ppermute | solution.py:14
  20.9 1.8 %collective-permute-start.17 = (bf16[4,8,576]{2,0,1:T(4,128)(2,1)S(1)}, bf16[4,8,576]{2,0,1:T(4,128)(2,1)S(1)}, u32[]{:S(2)}, u32[]{:S(2)}) collective-permute-start(bf16[4,8,576]{2,0,1:T(4,128)(2,1)S(1)} %collective-permute-done.16), channel_id=1, source_target_pairs={{0,1},{1,0},{2,3},{3,2},{4,5},{5,4},{6,7},{7,6},{8,9},{9,8},{10,11... | collective-permute-start | bytes 110600 | tf_op jit(solution)/shard_map/ppermute | solution.py:14
  21.4 12.9 %copy-start.3 = (bf16[1,7168,256]{2,1,0:T(8,128)(2,1)S(1)}, bf16[1,7168,256]{2,1,0:T(8,128)(2,1)}, u32[]{:S(2)}) copy-start(bf16[1,7168,256]{2,1,0:T(8,128)(2,1)} %param.14) | copy-start | bytes 11010052
  21.5 7.7 %collective-permute-start.4 = (bf16[64,1792]{1,0:T(8,128)(2,1)S(1)}, bf16[64,1792]{1,0:T(8,128)(2,1)S(1)}, u32[]{:S(2)}, u32[]{:S(2)}) collective-permute-start(bf16[64,1792]{1,0:T(8,128)(2,1)S(1)} %pad_maximum_fusion), channel_id=1, source_target_pairs={{0,2},{1,3},{2,0},{3,1},{4,6},{5,7},{6,4},{7,5},{8,10},{9,11},{10,... | collective-permute-start | bytes 688136 | tf_op jit(solution)/shard_map/ppermute | solution.py:14
  22.5 9.6 %collective-permute-start.3 = (bf16[64,1792]{1,0:T(8,128)(2,1)S(1)}, bf16[64,1792]{1,0:T(8,128)(2,1)S(1)}, u32[]{:S(2)}, u32[]{:S(2)}) collective-permute-start(bf16[64,1792]{1,0:T(8,128)(2,1)S(1)} %pad_maximum_fusion), channel_id=1, source_target_pairs={{0,1},{1,0},{2,3},{3,2},{4,5},{5,4},{6,7},{7,6},{8,9},{9,8},{10,11... | collective-permute-start | bytes 688136 | tf_op jit(solution)/shard_map/ppermute | solution.py:14
  22.9 11.8 %copy-start.4 = (bf16[4,32,576]{2,0,1:T(4,128)(2,1)}, bf16[4,32,576]{2,0,1:T(4,128)(2,1)S(1)}, u32[]{:S(2)}) copy-start(bf16[4,32,576]{2,0,1:T(4,128)(2,1)S(1)} %pad_maximum_fusion.2) | copy-start | bytes 442372
  29.1 5.5 %collective-permute-start.5 = (bf16[64,1792]{1,0:T(8,128)(2,1)S(1)}, bf16[64,1792]{1,0:T(8,128)(2,1)S(1)}, u32[]{:S(2)}, u32[]{:S(2)}) collective-permute-start(bf16[64,1792]{1,0:T(8,128)(2,1)S(1)} %collective-permute-done.4), channel_id=1, source_target_pairs={{0,1},{1,0},{2,3},{3,2},{4,5},{5,4},{6,7},{7,6},{8,9},{9,8},{10,11... | collective-permute-start | bytes 688136 | tf_op jit(solution)/shard_map/ppermute | solution.py:14
  32.4 2.9 %copy-start.1 = (bf16[1,256,7168]{2,1,0:T(8,128)(2,1)S(1)}, bf16[1,256,7168]{2,1,0:T(8,128)(2,1)}, u32[]{:S(2)}) copy-start(bf16[1,256,7168]{2,1,0:T(8,128)(2,1)} %param.15) | copy-start | bytes 11010052
  35.3 14.8 %slice-start = ((bf16[4,32,576]{2,0,1:T(4,128)(2,1)}), bf16[4,32,512]{2,0,1:T(4,128)(2,1)S(1)}, s32[]{:S(2)}) async-start(bf16[4,32,576]{2,0,1:T(4,128)(2,1)} %copy-done.4), calls=%async_computation | async-start | bytes 262144 | tf_op jit(solution)/shard_map/slice | solution.py:124
  35.6 1.7 %collective-permute-start.7 = (bf16[64,1792]{1,0:T(8,128)(2,1)S(1)}, bf16[64,1792]{1,0:T(8,128)(2,1)S(1)}, u32[]{:S(2)}, u32[]{:S(2)}) collective-permute-start(bf16[64,1792]{1,0:T(8,128)(2,1)S(1)} %convolution_convert_fusion), channel_id=1, source_target_pairs={{0,1},{1,0},{2,3},{3,2},{4,5},{5,4},{6,7},{7,6},{8,9},{9,8},{10,11... | collective-permute-start | bytes 688136 | tf_op jit(solution)/shard_map/ppermute | solution.py:14
  36.4 2.8 %collective-permute-start.6 = (bf16[64,1792]{1,0:T(8,128)(2,1)S(1)}, bf16[64,1792]{1,0:T(8,128)(2,1)S(1)}, u32[]{:S(2)}, u32[]{:S(2)}) collective-permute-start(bf16[64,1792]{1,0:T(8,128)(2,1)S(1)} %convolution_convert_fusion.2), channel_id=1, source_target_pairs={{0,1},{1,0},{2,3},{3,2},{4,5},{5,4},{6,7},{7,6},{8,9},{9,8},{10,11... | collective-permute-start | bytes 688136 | tf_op jit(solution)/shard_map/ppermute | solution.py:14
  37.6 7.9 %collective-permute-start.8 = (bf16[64,1792]{1,0:T(8,128)(2,1)S(1)}, bf16[64,1792]{1,0:T(8,128)(2,1)S(1)}, u32[]{:S(2)}, u32[]{:S(2)}) collective-permute-start(bf16[64,1792]{1,0:T(8,128)(2,1)S(1)} %add_convert_fusion.1), channel_id=1, source_target_pairs={{0,2},{1,3},{2,0},{3,1},{4,6},{5,7},{6,4},{7,5},{8,10},{9,11},{10,... | collective-permute-start | bytes 688136 | tf_op jit(solution)/shard_map/ppermute | solution.py:14
  45.6 6.1 %collective-permute-start.11 = (bf16[16,1792]{1,0:T(8,128)(2,1)S(1)}, bf16[16,1792]{1,0:T(8,128)(2,1)S(1)}, u32[]{:S(2)}, u32[]{:S(2)}) collective-permute-start(bf16[16,1792]{1,0:T(8,128)(2,1)S(1)} %get-tuple-element.3), channel_id=1, source_target_pairs={{0,12},{4,8},{8,4},{12,0},{1,13},{5,9},{9,5},{13,1},{2,14},{6,10},... | collective-permute-start | bytes 172040 | tf_op jit(solution)/shard_map/ppermute | solution.py:14
  48.5 5.4 %collective-permute-start.10 = (bf16[16,1792]{1,0:T(8,128)(2,1)S(1)}, bf16[16,1792]{1,0:T(8,128)(2,1)S(1)}, u32[]{:S(2)}, u32[]{:S(2)}) collective-permute-start(bf16[16,1792]{1,0:T(8,128)(2,1)S(1)} %get-tuple-element.4), channel_id=1, source_target_pairs={{0,8},{4,12},{8,0},{12,4},{1,9},{5,13},{9,1},{13,5},{2,10},{6,14},... | collective-permute-start | bytes 172040 | tf_op jit(solution)/shard_map/ppermute | solution.py:14
  48.5 5.4 %collective-permute-start.9 = (bf16[16,1792]{1,0:T(8,128)(2,1)S(1)}, bf16[16,1792]{1,0:T(8,128)(2,1)S(1)}, u32[]{:S(2)}, u32[]{:S(2)}) collective-permute-start(bf16[16,1792]{1,0:T(8,128)(2,1)S(1)} %get-tuple-element.5), channel_id=1, source_target_pairs={{0,4},{4,0},{8,12},{12,8},{1,5},{5,1},{9,13},{13,9},{2,6},{6,2},{1... | collective-permute-start | bytes 172040 | tf_op jit(solution)/shard_map/ppermute | solution.py:14

commit v2 on v0

v2 whole, which is shorter than its diff:
```python
import functools

import jax
import jax.numpy as jnp
from jax import lax
from jax.experimental import pallas as pl
from jax.experimental.pallas import tpu as pltpu
from jax.sharding import PartitionSpec as P

LATC = 512
CAP = 16

score_scale = 192.0 ** (-0.5)

bf16, f32, i32 = jnp.bfloat16, jnp.float32, jnp.int32
VMEM = pl.BlockSpec(memory_space=pltpu.VMEM)
SMEM = pl.BlockSpec(memory_space=pltpu.SMEM)
HBM = pl.BlockSpec(memory_space=pltpu.HBM)
ANY = pl.BlockSpec(memory_space=pl.ANY)


def swap(value, axis, mask):
    count = lax.axis_size(axis)
    return lax.ppermute(value, axis, [(i, i ^ mask) for i in range(count)])


def in_hbm(value):
    return pltpu.with_memory_space_constraint(value, pltpu.HBM)


def params(arrays, extra=6 << 20):
    held = sum(a.size * a.dtype.itemsize for a in arrays)
    return pltpu.CompilerParams(vmem_limit_bytes=min(held + extra, 60 << 20))


def cost(flops, moved=0):
    return pl.CostEstimate(flops=flops, bytes_accessed=moved, transcendentals=0)


def fold_widths(latr):
    first = latr // 2 // 128 * 128
    return first, latr - first, -(-(latr - first) // 128) * 128


def route_kernel(ep_count, ids_ref, gates_ref, tokens_ref, cache_ref, dest_ref, *outs):
    blocks, combine_ref = outs[:-1], outs[-1]
    own = lax.axis_index("ep")
    token_count, width = tokens_ref.shape
    ids, gates = ids_ref[...], gates_ref[...]
    served, gate = [], []
    for d in range(ep_count):
        named = ids == (own ^ d)
        served.append(jnp.sum(jnp.where(named, 1.0, 0.0), axis=0, keepdims=True))
        gate.append(jnp.sum(jnp.where(named, gates, 0.0), axis=0, keepdims=True))
    shape = (token_count, token_count)
    before = lax.broadcasted_iota(i32, shape, 0) < lax.broadcasted_iota(i32, shape, 1)
    before = jnp.where(before, 1.0, 0.0).astype(bf16)
    marks = jnp.concatenate(served, axis=0)
    rank = jnp.dot(marks.astype(bf16), before, preferred_element_type=f32)
    rank = jnp.where(marks > 0.5, rank, -1.0)
    slots = lax.broadcasted_iota(i32, (CAP, token_count), 0).astype(f32)
    chosen = [slots == rank[d : d + 1] for d in range(ep_count)]
    dispatch = jnp.concatenate([jnp.where(c, 1.0, 0.0) for c in chosen], axis=0).astype(bf16)
    rows = jnp.dot(dispatch, tokens_ref[...], preferred_element_type=f32)
    first, second, wide = fold_widths(cache_ref.shape[2])
    part = cache_ref.shape[1]
    for d in range(ep_count):
        combine_ref[d * CAP : (d + 1) * CAP, :] = jnp.where(chosen[d], gate[d], 0.0)
        blocks[d][:, :width] = rows[d * CAP : (d + 1) * CAP].astype(bf16)
        pick = i32(0)
        for k in range(ep_count):
            pick = jnp.where(dest_ref[own, k] == (own ^ d), k, pick)
        kept = cache_ref[pick].astype(f32)
        above = jnp.concatenate([kept[:, :first], jnp.zeros((part, wide - first), f32)], axis=1)
        below = jnp.concatenate([kept[:, first:], jnp.zeros((part, wide - second), f32)], axis=1)
        blocks[d][:, width:] = jnp.concatenate([above, below], axis=0).astype(bf16)


def route(ids, gates, tokens, cache_rows, destination, ep_count):
    token_count, width = tokens.shape
    wide = fold_widths(cache_rows.shape[2])[2]
    out_shape = [jax.ShapeDtypeStruct((CAP, width + wide), bf16)] * ep_count
    out_shape += [jax.ShapeDtypeStruct((ep_count * CAP, token_count), f32)]
    outs = pl.pallas_call(
        functools.partial(route_kernel, ep_count),
        out_shape=out_shape,
        in_specs=[VMEM, VMEM, VMEM, VMEM, SMEM],
        out_specs=[VMEM] * (ep_count + 1),
        compiler_params=params([tokens, ids, gates, cache_rows] + out_shape * 2),
        cost_estimate=cost(4 * ep_count * CAP * tokens.size, 2 * tokens.size),
        name="route",
    )(*map(in_hbm, (ids, gates, tokens, cache_rows, destination)))
    return outs[:-1], outs[-1]


def fetch_kernel(cuts, after_ref, *refs):
    count = (len(refs) - 2) // 2
    sems, mark_ref = refs[-1], refs[-2]
    copies = []
    for i in range(count):
        rows = refs[i].shape[0] // cuts
        for c in range(cuts):
            at = pl.ds(c * rows, rows)
            copies.append(
                pltpu.make_async_copy(refs[i].at[at], refs[count + i].at[at], sems.at[i, c])
            )
    for copy in copies:
        copy.start()
    mark_ref[...] = jnp.zeros(mark_ref.shape, mark_ref.dtype)
    for copy in copies:
        copy.wait()


def fetch(after, *arrays):
    out_shape = [pltpu.VMEM(a.shape, a.dtype) for a in arrays]
    cuts = 4
    outs = pl.pallas_call(
        functools.partial(fetch_kernel, cuts),
        out_shape=out_shape + [jax.ShapeDtypeStruct((8, 128), f32)],
        in_specs=[ANY] + [HBM] * len(arrays),
        out_specs=[VMEM] * (len(arrays) + 1),
        scratch_shapes=[pltpu.SemaphoreType.DMA((len(arrays), cuts))],
        compiler_params=pltpu.CompilerParams(vmem_limit_bytes=1 << 20),
        cost_estimate=cost(0, 0),
        name="fetch",
    )(after, *map(in_hbm, arrays))
    return outs[:-1], outs[-1]


def join_kernel(count, *refs):
    out_ref, at = refs[-1], 0
    for ref in refs[:count]:
        out_ref[at : at + ref.shape[0], :] = ref[...]
        at += ref.shape[0]


def join(blocks, after=(), weight=0):
    rows = sum(b.shape[0] for b in blocks)
    out_shape = jax.ShapeDtypeStruct((rows, blocks[0].shape[1]), blocks[0].dtype)
    return pl.pallas_call(
        functools.partial(join_kernel, len(blocks)),
        out_shape=out_shape,
        in_specs=[VMEM] * len(blocks) + [ANY] * len(after),
        out_specs=VMEM,
        compiler_params=params([out_shape] * 3, 1 << 20),
        cost_estimate=cost(0, weight),
        name="join",
    )(*blocks, *after)


def tie_kernel(*refs):
    pass


def tie(value, after):
    return pl.pallas_call(
        tie_kernel,
        out_shape=jax.ShapeDtypeStruct(value.shape, value.dtype),
        in_specs=[ANY] * (1 + len(after)),
        out_specs=ANY,
        input_output_aliases={0: 0},
        compiler_params=pltpu.CompilerParams(vmem_limit_bytes=1 << 20),
        cost_estimate=cost(0, 0),
        name="tie",
    )(value, *after)


def total_kernel(kept_ref, arrived_ref, *outs):
    at = 0
    for out in outs:
        rows = pl.ds(at, out.shape[0])
        out[...] = (kept_ref[rows, :] + arrived_ref[rows, :].astype(f32)).astype(out.dtype)
        at += out.shape[0]


def total(kept, arrived, count, dtype=bf16):
    rows, columns = kept.shape
    out_shape = [jax.ShapeDtypeStruct((rows // count, columns), dtype)] * count
    return pl.pallas_call(
        total_kernel,
        out_shape=out_shape,
        in_specs=[VMEM, VMEM],
        out_specs=[VMEM] * count,
        compiler_params=params([kept] * 4, 1 << 20),
        cost_estimate=cost(kept.size, 8 * kept.size),
        name="total",
    )(kept, arrived)


def piece_sums(piece_refs, masks, me, width, gate_ref, up_ref):
    gate_sums = up_sums = None
    for refs, m in zip(piece_refs, masks):
        rows = jnp.concatenate([r[:, :width] for r in refs], axis=0)
        at = pl.ds(pl.multiple_of((me ^ m) * width, width), width)
        g = jnp.dot(rows, gate_ref[at, :], preferred_element_type=f32)
        u = jnp.dot(rows, up_ref[at, :], preferred_element_type=f32)
        gate_sums = g if gate_sums is None else gate_sums + g
        up_sums = u if up_sums is None else up_sums + u
    return gate_sums, up_sums


def first_kernel(masks, width, gate_ref, up_ref, *refs):
    pieces, (gate_out, up_out) = refs[:-2], refs[-2:]
    per = len(pieces) // len(masks)
    groups = [pieces[i * per : (i + 1) * per] for i in range(len(masks))]
    gate_out[...], up_out[...] = piece_sums(
        groups, masks, lax.axis_index("pd"), width, gate_ref, up_ref
    )


def second_kernel(
    masks, targets, width, gate_ref, up_ref, down_ref, gsum_ref, usum_ref, *refs
):
    outs = refs[len(refs) - len(targets) - 1 :]
    pieces, hidden_out = refs[: len(refs) - len(targets) - 1], outs[-1]
    per = len(pieces) // len(masks)
    groups = [pieces[i * per : (i + 1) * per] for i in range(len(masks))]
    me = lax.axis_index("pd")
    gate_sums, up_sums = piece_sums(groups, masks, me, width, gate_ref, up_ref)
    gate_sums, up_sums = gate_sums + gsum_ref[...], up_sums + usum_ref[...]
    hidden = (gate_sums / (1.0 + jnp.exp(-gate_sums)) * up_sums).astype(bf16)
    hidden_out[...] = hidden
    for out, m in zip(outs, targets):
        at = pl.ds(pl.multiple_of((me ^ m) * width, width), width)
        out[...] = jnp.dot(hidden, down_ref[:, at], preferred_element_type=f32).astype(bf16)


def third_kernel(targets, width, hidden_ref, down_ref, *outs):
    me = lax.axis_index("pd")
    for out, m in zip(outs, targets):
        at = pl.ds(pl.multiple_of((me ^ m) * width, width), width)
        out[...] = jnp.dot(hidden_ref[...], down_ref[:, at], preferred_element_type=f32)


def attend_kernel(
    ep_count, pd_count, width, dest_ref, len_ref, query_ref, *refs
):
    pieces, out_ref = refs[:-1], refs[-1]
    per = len(pieces) // pd_count
    own, me = lax.axis_index("ep"), lax.axis_index("pd")
    latr, heads = query_ref.shape[2], query_ref.shape[1]
    first, second, wide = fold_widths(latr)
    part = CAP // 2
    shape = (heads, part * pd_count)
    column = lax.broadcasted_iota(i32, shape, 1)
    position = (me ^ (column // part)) * part + column % part
    sizes = [pieces[g].shape[0] // CAP for g in range(per)]
    where = [(g, i) for g in range(per) for i in range(sizes[g])]
    for d in range(ep_count):
        j = own ^ d
        length = i32(0)
        for k in range(ep_count):
            length = jnp.where(dest_ref[j, k] == own, len_ref[j * ep_count + k], length)
        keys = []
        for m in range(pd_count):
            ref = pieces[m * per + where[d][0]]
            at = where[d][1] * CAP
            folded = ref[at : at + CAP, width:].astype(f32)
            keys.append(
                jnp.concatenate([folded[:part, :first], folded[part:, :second]], axis=1)
            )
        keys = jnp.concatenate(keys, axis=0).astype(bf16)
        scores = lax.dot_general(
            query_ref[j], keys, (((1,), (1,)), ((), ())), preferred_element_type=f32
        )
        scores = scores * score_scale
        usable = position < length
        top = jnp.max(jnp.where(usable, scores, -1e30), axis=1, keepdims=True)
        weights = jnp.where(usable, jnp.exp(scores - top), 0.0)
        total = jnp.sum(weights, axis=1, keepdims=True)
        summed = jnp.dot(weights.astype(bf16), keys[:, :LATC], preferred_element_type=f32)
        out_ref[j] = (summed / total).astype(bf16)


def combine_kernel(combine_ref, *refs):
    blocks, out_ref = refs[:-1], refs[-1]
    combine = combine_ref[...]
    high = combine.astype(bf16)
    low = (combine - high.astype(f32)).astype(bf16)
    rows = jnp.concatenate([b[...] for b in blocks], axis=0)
    dims = (((0,), (0,)), ((), ()))
    mixed = lax.dot_general(high, rows, dims, preferred_element_type=f32)
    mixed += lax.dot_general(low, rows, dims, preferred_element_type=f32)
    out_ref[...] = mixed.astype(bf16)


def spread(pieces, m, bit):
    have = [m]
    while bit:
        for k in list(have):
            pieces[k ^ bit] = [swap(g, "pd", bit) for g in pieces[k]]
            have.append(k ^ bit)
        bit //= 2


def on_device(
    tokens,
    expert_ids,
    gate_scores,
    gate_weight,
    up_weight,
    down_weight,
    cache_rows,
    lengths,
    destination,
    decode_query,
):
    ep_count = lax.axis_size("ep")
    pd_count = lax.axis_size("pd")
    token_count, width = tokens.shape
    hidden_units = gate_weight.shape[2]
    slot_count = ep_count * CAP
    half = ep_count // 2

    blocks, combine = route(
        expert_ids.T, gate_scores.T, tokens, cache_rows, destination, ep_count
    )
    arrived = [blocks[0]] + [swap(blocks[d], "ep", d) for d in range(1, ep_count)]
    bit = pd_count // 2
    over = swap(blocks[0], "pd", bit)
    (w_gate,), mark = fetch(combine, gate_weight[0])
    rest = join(arrived[1:], [mark, over])
    (w_up, w_down), mark = fetch(rest, up_weight[0], down_weight[0])

    pieces = {0: [blocks[0], rest]}
    pieces[bit] = [over, swap(rest, "pd", bit)]
    early = list(range(bit))
    late = [m ^ bit for m in early]
    spread(pieces, 0, bit // 2)
    sums = jax.ShapeDtypeStruct((slot_count, hidden_units), f32)
    operands = [g for m in early for g in pieces[m]]
    gate_sums, up_sums = pl.pallas_call(
        functools.partial(first_kernel, early, width),
        out_shape=[sums, sums],
        in_specs=[VMEM] * (2 + len(operands)),
        out_specs=[VMEM, VMEM],
        compiler_params=params(operands * 2),
        cost_estimate=cost(4 * slot_count * w_gate.size * 2, 2 * w_gate.size),
        name="gate_up_first",
    )(w_gate, w_up, *operands)
    pieces[bit][1] = tie(pieces[bit][1], [mark, gate_sums])
    spread(pieces, bit, bit // 2)
    others = sorted([m for m in range(pd_count) if m & 1], reverse=True)
    stay = sorted([m for m in range(pd_count) if not m & 1], reverse=True)
    operands = [g for m in late for g in pieces[m]]
    out_shape = [jax.ShapeDtypeStruct((slot_count, width), bf16)] * len(others)
    out_shape += [jax.ShapeDtypeStruct((slot_count, hidden_units), bf16)]
    outs = pl.pallas_call(
        functools.partial(second_kernel, late, others, width),
        out_shape=out_shape,
        in_specs=[VMEM] * (5 + len(operands)),
        out_specs=[VMEM] * len(out_shape),
        compiler_params=params(operands * 2 + out_shape * 2),
        cost_estimate=cost(6 * slot_count * w_gate.size * 2, 2 * w_gate.size),
        name="gate_up_down",
    )(w_gate, w_up, w_down, gate_sums, up_sums, *operands)
    parts = dict(zip(others, outs[:-1]))
    out_shape = [jax.ShapeDtypeStruct((slot_count, width), f32)] * len(stay)
    outs = pl.pallas_call(
        functools.partial(third_kernel, stay, width),
        out_shape=out_shape,
        in_specs=[VMEM, VMEM],
        out_specs=[VMEM] * len(out_shape),
        compiler_params=params(out_shape * 2),
        cost_estimate=cost(2 * slot_count * w_down.size, w_down.size),
        name="down_rest",
    )(outs[-1], w_down)
    kept = dict(zip(stay, outs))
    cut = half * CAP
    kept = {m: dict(zip((0, cut), total(kept[m], swap(parts[m ^ 1], "pd", 1), 2, f32))) for m in stay}
    returned = [None] * ep_count
    for low in (cut, 0):
        rows = {m: kept[m][low] for m in stay}
        bit = 2
        while bit < pd_count:
            for m in sorted(rows, reverse=True):
                if m & bit:
                    over = swap(rows.pop(m).astype(bf16), "pd", bit)
                    final = bit * 2 == pd_count
                    rows[m ^ bit] = total(rows[m ^ bit], over, half if final else 1, bf16 if final else f32)
                    rows[m ^ bit] = rows[m ^ bit] if final else rows[m ^ bit][0]
            bit *= 2
        for i, block in enumerate(rows[0]):
            d = low // CAP + i
            returned[d] = swap(block, "ep", d) if d else block
    mixed = jax.ShapeDtypeStruct((token_count, width), bf16)
    mixed = pl.pallas_call(
        combine_kernel,
        out_shape=mixed,
        in_specs=[VMEM] * (1 + ep_count),
        out_specs=VMEM,
        compiler_params=params([mixed] * 4),
        cost_estimate=cost(4 * slot_count * tokens.size, 2 * tokens.size),
        name="combine",
    )(combine, *returned)

    operands = [g for m in range(pd_count) for g in pieces[m]]
    attended = jax.ShapeDtypeStruct(decode_query.shape[1:3] + (LATC,), bf16)
    attended = pl.pallas_call(
        functools.partial(attend_kernel, ep_count, pd_count, width),
        out_shape=attended,
        in_specs=[SMEM, SMEM, VMEM] + [VMEM] * len(operands),
        out_specs=VMEM,
        compiler_params=params(operands + [decode_query, attended]),
        cost_estimate=cost(8 * slot_count * tokens.size, 8 * tokens.size),
        name="attend",
    )(destination, lengths, decode_query[0], *operands)
    return (mixed, attended[None])


def solution(mesh):
    in_specs = (
        P(("group", "ep"), "pd"),
        P(("group", "ep"), None),
        P(("group", "ep"), None),
        P("ep", None, "pd"),
        P("ep", None, "pd"),
        P("ep", "pd", None),
        P(("group", "ep"), "pd", None),
        P("group"),
        P("group", None),
        P(("group", "ep"), None, "pd", None),
    )
    out_specs = (P(("group", "ep"), "pd"), P(("group", "ep"), None, "pd", None))
    return jax.shard_map(
        on_device, mesh=mesh, in_specs=in_specs, out_specs=out_specs, check_vma=False
    )
```

time: 109 us -> 43.1 us (0.40)
  blocking collectives: 29.1 us -> 0 us
  other arithmetic: 13.8 us -> 0.03 us
  between operations: 14.2 us -> 0.77 us
  local copies, waits for them, and re-layouts: 13.3 us -> 0.02 us
  Pallas kernels: 0 us -> 13.2 us
  matrix products: 10.7 us -> 0 us
  starting transfers between devices: 7.89 us -> 15.1 us
  waiting for transfers between devices: 19.2 us -> 13.8 us
    ppermute x0 -> x16, starting transfers between devices: none -> 15.1 us  [swap(): return lax.ppermute(value, axis, [(i, i ^ mask) for i in range(count)])]
    all_gather x2 -> x0, blocking collectives: 14.8 us -> none  [the longest x1 9.3 us: on_device(): shard_piece = lax.all_gather(expert_rows, 'pd', axis=1, tiled=True)]
    all_to_all x1 -> x0, blocking collectives: 14.3 us -> none  [on_device(): lax.all_to_all(payload, 'ep', split_axis=0, concat_axis=0, tiled=True)]
    ppermute x0 -> x16, waiting for transfers between devices: none -> 13.8 us  [swap(): return lax.ppermute(value, axis, [(i, i ^ mask) for i in range(count)])]
    pallas_call x0 -> x14, Pallas kernels: none -> 13.2 us  [the longest x2 5.21 us: fetch(): pl.pallas_call(functools.partial(fetch_kernel, cuts), out_shape=out_shape...]
    all_to_all x2 -> x0, waiting for transfers between devices: 12.2 us -> none  [the longest x1 7.19 us: on_device(): lax.all_to_all(expert_out.reshape(ep_count, CAP, -1), 'ep', split_axis=0,...]
    reduce_sum x4 -> x0, other arithmetic: 11.5 us -> none  [the longest x1 11.2 us: on_device(): jnp.sum(picked * gate_scores[:, :, None], axis=1).astype(jnp.bfloat16)]
    dot_general x6 -> x0, matrix products: 10.7 us -> none  [the longest x1 6.41 us: on_device(): partial_out = jnp.dot(hidden, w_down, preferred_element_type=jnp.float32)]
  transfers between devices with their start and end apart: 3 -> 16, of which waited for: 3 -> 7; matrix products, arithmetic and copies ran while one was open for 3% -> 0% of each run, Pallas kernels for 0% -> 20%
where the time goes in v2:
time: 43.1 us; the launch traced here: 43 us
  starting transfers between devices  15.1 us (35%)
  waiting for transfers between devices  13.8 us (32%)
  Pallas kernels  13.2 us (31%)
  between operations  0.77 us (2%)
    ppermute x16, starting transfers between devices, swap(): return lax.ppermute(value, axis, [(i, i ^ mask) for i in range(count)])  15.1 us
    ppermute x16, waiting for transfers between devices, swap(): return lax.ppermute(value, axis, [(i, i ^ mask) for i in range(count)])  13.8 us
    pallas_call x2, Pallas kernels, fetch(): pl.pallas_call(functools.partial(fetch_kernel, cuts), out_shape=out_shape...  5.21 us
    pallas_call x1, Pallas kernels, on_device(): pl.pallas_call(functools.partial(attend_kernel, ep_count, pd_count, width...  2.25 us
    pallas_call x1, Pallas kernels, route(): pl.pallas_call(functools.partial(route_kernel, ep_count), out_shape=out_s...  1.64 us
    pallas_call x1, Pallas kernels, on_device(): pl.pallas_call(combine_kernel, out_shape=mixed, in_specs=[VMEM] * (1 + ep...  1.59 us
    pallas_call x1, Pallas kernels, on_device(): pl.pallas_call(functools.partial(second_kernel, late, others, width), out...  1.18 us
  transfers between devices with their start and end apart: 16, of which 7 were waited for; matrix products, arithmetic and copies ran while one was open for 0% of the time, Pallas kernels for 20%

profile of v2, /device:TPU:0, one launch (start us, length us, event | category | flops | bytes accessed | tf_op | source)
XLA Modules:
  0.0 43.0 jit_solution(3381781841375640185)
XLA Ops:
  0.6 1.6 %route.1 = (bf16[16,2176]{1,0:T(8,128)(2,1)S(1)}, bf16[16,2176]{1,0:T(8,128)(2,1)S(1)}, bf16[16,2176]{1,0:T(8,128)(2,1)S(1)}, bf16[16,2176]{1,0:T(8,128)(2,1)S(1)}, f32[64,256]{1,0:T(8,128)S(1)}) custom-call(s32[8,256]{1,0:T(8,128)} %bitcast.12, f32[8,256]{1,0:T(8,128)} %bitcast.13, bf16[256,1792]{1,0:T(8,128)(2,1)} %tokens_ref.1, ...), custom_call_target="tpu_custom_call" | custom-call | flops 117440512 | bytes 917504 | tf_op jit(solution)/shard_map/route/pallas_call | solution.py:84
  2.3 3.0 %collective-permute-start.3 = (bf16[16,2176]{1,0:T(8,128)(2,1)S(1)}, bf16[16,2176]{1,0:T(8,128)(2,1)S(1)}, u32[]{:S(2)}, u32[]{:S(2)}) collective-permute-start(bf16[16,2176]{1,0:T(8,128)(2,1)S(1)} %get-tuple-element.33.refs_0_), channel_id=1, source_target_pairs={{0,2},{1,3},{2,0},{3,1},{4,6},{5,7},{6,4},{7,5},{8,10},{9,11},{10,... | collective-permute-start | bytes 208904 | tf_op jit(solution)/shard_map/ppermute | solution.py:24
  5.3 1.6 %collective-permute-start = (bf16[16,2176]{1,0:T(8,128)(2,1)S(1)}, bf16[16,2176]{1,0:T(8,128)(2,1)S(1)}, u32[]{:S(2)}, u32[]{:S(2)}) collective-permute-start(bf16[16,2176]{1,0:T(8,128)(2,1)S(1)} %get-tuple-element.29), channel_id=1, source_target_pairs={{0,4},{4,0},{8,12},{12,8},{1,5},{5,1},{9,13},{13,9},{2,6},{6,2},{1... | collective-permute-start | bytes 208904 | tf_op jit(solution)/shard_map/ppermute | solution.py:24
  6.9 2.6 %collective-permute-start.1 = (bf16[16,2176]{1,0:T(8,128)(2,1)S(1)}, bf16[16,2176]{1,0:T(8,128)(2,1)S(1)}, u32[]{:S(2)}, u32[]{:S(2)}) collective-permute-start(bf16[16,2176]{1,0:T(8,128)(2,1)S(1)} %get-tuple-element.30), channel_id=1, source_target_pairs={{0,8},{4,12},{8,0},{12,4},{1,9},{5,13},{9,1},{13,5},{2,10},{6,14},... | collective-permute-start | bytes 208904 | tf_op jit(solution)/shard_map/ppermute | solution.py:24
  9.4 0.2 collective-permute-start.2
  9.7 2.0 %fetch.2 = (bf16[7168,256]{1,0:T(8,128)(2,1)S(1)}, f32[8,128]{1,0:T(8,128)S(1)}) custom-call(f32[64,256]{1,0:T(8,128)S(1)} %get-tuple-element.27.after_ref.combine_ref, bf16[7168,256]{1,0:T(8,128)(2,1)} %bitcast.8), custom_call_target="tpu_custom_call" | custom-call | tf_op jit(solution)/shard_map/fetch/pallas_call | solution.py:117
  11.7 0.0 collective-permute-done.3.refs_4_.refs_0_
  11.7 0.0 collective-permute-done.refs_0_
  11.7 2.4 %collective-permute-done.1.refs_1_ = bf16[16,2176]{1,0:T(8,128)(2,1)S(1)} collective-permute-done((bf16[16,2176]{1,0:T(8,128)(2,1)S(1)}, bf16[16,2176]{1,0:T(8,128)(2,1)S(1)}, u32[]{:S(2)}, u32[]{:S(2)}) %collective-permute-start.1) | collective-permute-done | bytes 69664 | tf_op jit(solution)/shard_map/ppermute | solution.py:24
  14.1 1.5 %collective-permute-done.2.refs_2_ = bf16[16,2176]{1,0:T(8,128)(2,1)S(1)} collective-permute-done((bf16[16,2176]{1,0:T(8,128)(2,1)S(1)}, bf16[16,2176]{1,0:T(8,128)(2,1)S(1)}, u32[]{:S(2)}, u32[]{:S(2)}) %collective-permute-start.2) | collective-permute-done | bytes 69664 | tf_op jit(solution)/shard_map/ppermute | solution.py:24
  15.6 0.1 collective-permute-start.5
  15.7 0.6 %collective-permute-start.6 = (bf16[48,2176]{1,0:T(8,128)(2,1)S(1)}, bf16[48,2176]{1,0:T(8,128)(2,1)S(1)}, u32[]{:S(2)}, u32[]{:S(2)}) collective-permute-start(bf16[48,2176]{1,0:T(8,128)(2,1)S(1)} %join.1.after_ref.refs_1_), channel_id=1, source_target_pairs={{0,2},{1,3},{2,0},{3,1},{4,6},{5,7},{6,4},{7,5},{8,10},{9,11},{10,... | collective-permute-start | bytes 626696 | tf_op jit(solution)/shard_map/ppermute | solution.py:24
  16.3 0.2 collective-permute-start.4
  16.5 3.2 %fetch.3 = (bf16[7168,256]{1,0:T(8,128)(2,1)S(1)}, bf16[256,7168]{1,0:T(8,128)(2,1)S(1)}, f32[8,128]{1,0:T(8,128)S(1)}) custom-call(bf16[48,2176]{1,0:T(8,128)(2,1)S(1)} %join.1.after_ref.refs_1_, bf16[7168,256]{1,0:T(8,128)(2,1)} %bitcast.9, bf16[256,7168]{1,0:T(8,128)(2,1)} %bitcast.10), custom_call_target="tpu_custom_call" | custom-call | tf_op jit(solution)/shard_map/fetch/pallas_call | solution.py:117
  19.6 0.0 collective-permute-done.4.refs_2_
  19.6 0.0 collective-permute-done.5.refs_3_
  19.7 0.8 %gate_up_first.1 = (f32[64,256]{1,0:T(8,128)S(1)}, f32[64,256]{1,0:T(8,128)S(1)}) custom-call(bf16[7168,256]{1,0:T(8,128)(2,1)S(1)} %get-tuple-element.28.gate_ref, bf16[7168,256]{1,0:T(8,128)(2,1)S(1)} %get-tuple-element.34.up_ref, bf16[16,2176]{1,0:T(8,128)(2,1)S(1)} %get-tuple-element.33.refs_0_, bf16[48,2176]{1,0:T(8,128)(2,1)S(1)} %join.1.after_ref.refs_1_, ...), custom_call_target="tpu_custom_call" | custom-call | flops 939524096 | bytes 3670016 | tf_op jit(solution)/shard_map/gate_up_first/pallas_call | solution.py:332
  20.4 2.8 %collective-permute-done.6.refs_0_ = bf16[48,2176]{1,0:T(8,128)(2,1)S(1)} collective-permute-done((bf16[48,2176]{1,0:T(8,128)(2,1)S(1)}, bf16[48,2176]{1,0:T(8,128)(2,1)S(1)}, u32[]{:S(2)}, u32[]{:S(2)}) %collective-permute-start.6) | collective-permute-done | bytes 208928 | tf_op jit(solution)/shard_map/ppermute | solution.py:24
  23.3 0.0 collective-permute-start.8
  23.3 0.5 %collective-permute-start.7 = (bf16[16,2176]{1,0:T(8,128)(2,1)S(1)}, bf16[16,2176]{1,0:T(8,128)(2,1)S(1)}, u32[]{:S(2)}, u32[]{:S(2)}) collective-permute-start(bf16[16,2176]{1,0:T(8,128)(2,1)S(1)} %collective-permute-done.3.refs_4_.refs_0_), channel_id=1, source_target_pairs={{0,1},{1,0},{2,3},{3,2},{4,5},{5,4},{6,7},{7,6},{8,9},{9,8},{10,11... | collective-permute-start | bytes 208904 | tf_op jit(solution)/shard_map/ppermute | solution.py:24
  23.8 1.0 %collective-permute-done.7.refs_2_.refs_6_ = bf16[16,2176]{1,0:T(8,128)(2,1)S(1)} collective-permute-done((bf16[16,2176]{1,0:T(8,128)(2,1)S(1)}, bf16[16,2176]{1,0:T(8,128)(2,1)S(1)}, u32[]{:S(2)}, u32[]{:S(2)}) %collective-permute-start.7) | collective-permute-done | bytes 69664 | tf_op jit(solution)/shard_map/ppermute | solution.py:24
  24.8 0.0 collective-permute-done.8.refs_3_.refs_7_
  24.8 1.2 %gate_up_down.1 = (bf16[64,1792]{1,0:T(8,128)(2,1)S(1)}, bf16[64,1792]{1,0:T(8,128)(2,1)S(1)}, bf16[64,256]{1,0:T(8,128)(2,1)S(1)}) custom-call(bf16[7168,256]{1,0:T(8,128)(2,1)S(1)} %get-tuple-element.28.gate_ref, bf16[7168,256]{1,0:T(8,128)(2,1)S(1)} %get-tuple-element.34.up_ref, bf16[256,7168]{1,0:T(8,128)(2,1)S(1)} %get-tuple-element.35.down_ref, ...), custom_call_target="tpu_custom_call" | custom-call | flops 1409286144 | bytes 3670016 | tf_op jit(solution)/shard_map/gate_up_down/pallas_call | solution.py:348
  26.0 0.0 copy-start
  26.0 0.0 copy-start.1
  26.0 0.0 copy-start.2
  26.1 0.3 collective-permute-start.10
  26.3 0.3 collective-permute-start.9
  26.6 0.5 %down_rest.1 = (f32[64,1792]{1,0:T(8,128)S(1)}, f32[64,1792]{1,0:T(8,128)S(1)}) custom-call(bf16[64,256]{1,0:T(8,128)(2,1)S(1)} %get-tuple-element.39.hidden_ref, bf16[256,7168]{1,0:T(8,128)(2,1)S(1)} %get-tuple-element.35.down_ref), custom_call_target="tpu_custom_call" | custom-call | flops 234881024 | bytes 1835008 | tf_op jit(solution)/shard_map/down_rest/pallas_call | solution.py:359
  27.1 0.5 %collective-permute-done.10.arrived_ref = bf16[64,1792]{1,0:T(8,128)(2,1)S(1)} collective-permute-done((bf16[64,1792]{1,0:T(8,128)(2,1)S(1)}, bf16[64,1792]{1,0:T(8,128)(2,1)S(1)}, u32[]{:S(2)}, u32[]{:S(2)}) %collective-permute-start.10) | collective-permute-done | bytes 229408 | tf_op jit(solution)/shard_map/ppermute | solution.py:24
  27.7 0.6 %collective-permute-start.13 = (bf16[32,1792]{1,0:T(8,128)(2,1)S(1)}, bf16[32,1792]{1,0:T(8,128)(2,1)S(1)}, u32[]{:S(2)}, u32[]{:S(2)}) collective-permute-start(bf16[32,1792]{1,0:T(8,128)(2,1)S(1)} %convert_element_type.7), channel_id=1, source_target_pairs={{0,2},{1,3},{2,0},{3,1},{4,6},{5,7},{6,4},{7,5},{8,10},{9,11},{10,... | collective-permute-start | bytes 344072 | tf_op jit(solution)/shard_map/ppermute | solution.py:24
  28.3 1.6 %collective-permute-start.11 = (bf16[32,1792]{1,0:T(8,128)(2,1)S(1)}, bf16[32,1792]{1,0:T(8,128)(2,1)S(1)}, u32[]{:S(2)}, u32[]{:S(2)}) collective-permute-start(bf16[32,1792]{1,0:T(8,128)(2,1)S(1)} %convert_element_type.6), channel_id=1, source_target_pairs={{0,2},{1,3},{2,0},{3,1},{4,6},{5,7},{6,4},{7,5},{8,10},{9,11},{10,... | collective-permute-start | bytes 344072 | tf_op jit(solution)/shard_map/ppermute | solution.py:24
  29.8 0.0 collective-permute-done.9.arrived_ref
  29.9 3.8 %collective-permute-done.13.arrived_ref = bf16[32,1792]{1,0:T(8,128)(2,1)S(1)} collective-permute-done((bf16[32,1792]{1,0:T(8,128)(2,1)S(1)}, bf16[32,1792]{1,0:T(8,128)(2,1)S(1)}, u32[]{:S(2)}, u32[]{:S(2)}) %collective-permute-start.13) | collective-permute-done | bytes 114720 | tf_op jit(solution)/shard_map/ppermute | solution.py:24
  33.8 1.6 %collective-permute-start.14 = (bf16[16,1792]{1,0:T(8,128)(2,1)S(1)}, bf16[16,1792]{1,0:T(8,128)(2,1)S(1)}, u32[]{:S(2)}, u32[]{:S(2)}) collective-permute-start(bf16[16,1792]{1,0:T(8,128)(2,1)S(1)} %get-tuple-element.50), channel_id=1, source_target_pairs={{0,8},{4,12},{8,0},{12,4},{1,9},{5,13},{9,1},{13,5},{2,10},{6,14},... | collective-permute-start | bytes 172040 | tf_op jit(solution)/shard_map/ppermute | solution.py:24
  35.4 0.6 %collective-permute-start.15 = (bf16[16,1792]{1,0:T(8,128)(2,1)S(1)}, bf16[16,1792]{1,0:T(8,128)(2,1)S(1)}, u32[]{:S(2)}, u32[]{:S(2)}) collective-permute-start(bf16[16,1792]{1,0:T(8,128)(2,1)S(1)} %get-tuple-element.51), channel_id=1, source_target_pairs={{0,12},{4,8},{8,4},{12,0},{1,13},{5,9},{9,5},{13,1},{2,14},{6,10},... | collective-permute-start | bytes 172040 | tf_op jit(solution)/shard_map/ppermute | solution.py:24
  36.0 0.0 collective-permute-done.11.arrived_ref
  36.0 1.4 %collective-permute-start.12 = (bf16[16,1792]{1,0:T(8,128)(2,1)S(1)}, bf16[16,1792]{1,0:T(8,128)(2,1)S(1)}, u32[]{:S(2)}, u32[]{:S(2)}) collective-permute-start(bf16[16,1792]{1,0:T(8,128)(2,1)S(1)} %get-tuple-element.47), channel_id=1, source_target_pairs={{0,4},{4,0},{8,12},{12,8},{1,5},{5,1},{9,13},{13,9},{2,6},{6,2},{1... | collective-permute-start | bytes 172040 | tf_op jit(solution)/shard_map/ppermute | solution.py:24
  37.4 0.0 copy-done
  37.4 0.0 copy-done.1
  37.4 0.0 copy-done.2
  37.4 2.3 %attend.1 = bf16[4,16,512]{2,1,0:T(8,128)(2,1)} custom-call(s32[4,4]{1,0:T(4,128)S(1)} %copy-done.1, s32[16]{0:T(128)S(1)} %copy-done.2, bf16[4,16,576]{2,1,0:T(8,128)(2,1)S(1)} %bitcast.7, bf16[16,2176]{1,0:T(8,128)(2,1)S(1)} %get-tuple-element.33.refs_0_, bf16[48,2176]{1,0:T(8,128)(2,1)S(1)} %join.1.after_ref.refs_1_, ...), custom_call_target="tpu_custom_call" | custom-call | flops 234881024 | bytes 3670016 | tf_op jit(solution)/shard_map/attend/pallas_call | solution.py:399
  39.7 0.0 collective-permute-done.14.refs_2_
  39.7 1.7 %collective-permute-done.15.refs_3_ = bf16[16,1792]{1,0:T(8,128)(2,1)S(1)} collective-permute-done((bf16[16,1792]{1,0:T(8,128)(2,1)S(1)}, bf16[16,1792]{1,0:T(8,128)(2,1)S(1)}, u32[]{:S(2)}, u32[]{:S(2)}) %collective-permute-start.15) | collective-permute-done | bytes 57376 | tf_op jit(solution)/shard_map/ppermute | solution.py:24
  41.4 0.0 collective-permute-done.12.refs_1_
  41.4 1.6 %combine.1 = bf16[256,1792]{1,0:T(8,128)(2,1)} custom-call(f32[64,256]{1,0:T(8,128)S(1)} %get-tuple-element.27.after_ref.combine_ref, bf16[16,1792]{1,0:T(8,128)(2,1)S(1)} %get-tuple-element.46.refs_0_, bf16[16,1792]{1,0:T(8,128)(2,1)S(1)} %collective-permute-done.12.refs_1_, bf16[16,1792]{1,0:T(8,128)(2,1)S(1)} %collective-permute-done.14.refs_2_, ...), custom_call_target="tpu_custom_call" | custom-call | flops 117440512 | bytes 917504 | tf_op jit(solution)/shard_map/combine/pallas_call | solution.py:387
  (8 shorter events, 0.2 us)
Async XLA Ops:
  2.3 9.4 %collective-permute-start.3 = (bf16[16,2176]{1,0:T(8,128)(2,1)S(1)}, bf16[16,2176]{1,0:T(8,128)(2,1)S(1)}, u32[]{:S(2)}, u32[]{:S(2)}) collective-permute-start(bf16[16,2176]{1,0:T(8,128)(2,1)S(1)} %get-tuple-element.33.refs_0_), channel_id=1, source_target_pairs={{0,2},{1,3},{2,0},{3,1},{4,6},{5,7},{6,4},{7,5},{8,10},{9,11},{10,... | collective-permute-start | bytes 208904 | tf_op jit(solution)/shard_map/ppermute | solution.py:24
  5.3 6.5 %collective-permute-start = (bf16[16,2176]{1,0:T(8,128)(2,1)S(1)}, bf16[16,2176]{1,0:T(8,128)(2,1)S(1)}, u32[]{:S(2)}, u32[]{:S(2)}) collective-permute-start(bf16[16,2176]{1,0:T(8,128)(2,1)S(1)} %get-tuple-element.29), channel_id=1, source_target_pairs={{0,4},{4,0},{8,12},{12,8},{1,5},{5,1},{9,13},{13,9},{2,6},{6,2},{1... | collective-permute-start | bytes 208904 | tf_op jit(solution)/shard_map/ppermute | solution.py:24
  6.9 7.2 %collective-permute-start.1 = (bf16[16,2176]{1,0:T(8,128)(2,1)S(1)}, bf16[16,2176]{1,0:T(8,128)(2,1)S(1)}, u32[]{:S(2)}, u32[]{:S(2)}) collective-permute-start(bf16[16,2176]{1,0:T(8,128)(2,1)S(1)} %get-tuple-element.30), channel_id=1, source_target_pairs={{0,8},{4,12},{8,0},{12,4},{1,9},{5,13},{9,1},{13,5},{2,10},{6,14},... | collective-permute-start | bytes 208904 | tf_op jit(solution)/shard_map/ppermute | solution.py:24
  9.4 6.1 %collective-permute-start.2 = (bf16[16,2176]{1,0:T(8,128)(2,1)S(1)}, bf16[16,2176]{1,0:T(8,128)(2,1)S(1)}, u32[]{:S(2)}, u32[]{:S(2)}) collective-permute-start(bf16[16,2176]{1,0:T(8,128)(2,1)S(1)} %get-tuple-element.31), channel_id=1, source_target_pairs={{0,12},{4,8},{8,4},{12,0},{1,13},{5,9},{9,5},{13,1},{2,14},{6,10},... | collective-permute-start | bytes 208904 | tf_op jit(solution)/shard_map/ppermute | solution.py:24
  15.6 4.0 %collective-permute-start.5 = (bf16[48,2176]{1,0:T(8,128)(2,1)S(1)}, bf16[48,2176]{1,0:T(8,128)(2,1)S(1)}, u32[]{:S(2)}, u32[]{:S(2)}) collective-permute-start(bf16[48,2176]{1,0:T(8,128)(2,1)S(1)} %join.1.after_ref.refs_1_), channel_id=1, source_target_pairs={{0,1},{1,0},{2,3},{3,2},{4,5},{5,4},{6,7},{7,6},{8,9},{9,8},{10,11... | collective-permute-start | bytes 626696 | tf_op jit(solution)/shard_map/ppermute | solution.py:24
  15.7 7.6 %collective-permute-start.6 = (bf16[48,2176]{1,0:T(8,128)(2,1)S(1)}, bf16[48,2176]{1,0:T(8,128)(2,1)S(1)}, u32[]{:S(2)}, u32[]{:S(2)}) collective-permute-start(bf16[48,2176]{1,0:T(8,128)(2,1)S(1)} %join.1.after_ref.refs_1_), channel_id=1, source_target_pairs={{0,2},{1,3},{2,0},{3,1},{4,6},{5,7},{6,4},{7,5},{8,10},{9,11},{10,... | collective-permute-start | bytes 626696 | tf_op jit(solution)/shard_map/ppermute | solution.py:24
  16.3 3.3 %collective-permute-start.4 = (bf16[16,2176]{1,0:T(8,128)(2,1)S(1)}, bf16[16,2176]{1,0:T(8,128)(2,1)S(1)}, u32[]{:S(2)}, u32[]{:S(2)}) collective-permute-start(bf16[16,2176]{1,0:T(8,128)(2,1)S(1)} %get-tuple-element.33.refs_0_), channel_id=1, source_target_pairs={{0,1},{1,0},{2,3},{3,2},{4,5},{5,4},{6,7},{7,6},{8,9},{9,8},{10,11... | collective-permute-start | bytes 208904 | tf_op jit(solution)/shard_map/ppermute | solution.py:24
  23.3 1.6 %collective-permute-start.8 = (bf16[48,2176]{1,0:T(8,128)(2,1)S(1)}, bf16[48,2176]{1,0:T(8,128)(2,1)S(1)}, u32[]{:S(2)}, u32[]{:S(2)}) collective-permute-start(bf16[48,2176]{1,0:T(8,128)(2,1)S(1)} %tie.1.refs_1_.refs_5_), channel_id=1, source_target_pairs={{0,1},{1,0},{2,3},{3,2},{4,5},{5,4},{6,7},{7,6},{8,9},{9,8},{10,11... | collective-permute-start | bytes 626696 | tf_op jit(solution)/shard_map/ppermute | solution.py:24
  23.3 1.6 %collective-permute-start.7 = (bf16[16,2176]{1,0:T(8,128)(2,1)S(1)}, bf16[16,2176]{1,0:T(8,128)(2,1)S(1)}, u32[]{:S(2)}, u32[]{:S(2)}) collective-permute-start(bf16[16,2176]{1,0:T(8,128)(2,1)S(1)} %collective-permute-done.3.refs_4_.refs_0_), channel_id=1, source_target_pairs={{0,1},{1,0},{2,3},{3,2},{4,5},{5,4},{6,7},{7,6},{8,9},{9,8},{10,11... | collective-permute-start | bytes 208904 | tf_op jit(solution)/shard_map/ppermute | solution.py:24
  26.0 11.4 %copy-start = (bf16[1,4,16,576]{3,2,1,0:T(8,128)(2,1)S(1)}, bf16[1,4,16,576]{3,2,1,0:T(8,128)(2,1)}, u32[]{:S(2)}) copy-start(bf16[1,4,16,576]{3,2,1,0:T(8,128)(2,1)} %param.19) | copy-start | bytes 221188
  26.0 11.4 %copy-start.1 = (s32[4,4]{1,0:T(4,128)S(1)}, s32[4,4]{1,0:T(4,128)}, u32[]{:S(2)}) copy-start(s32[4,4]{1,0:T(4,128)} %dest_ref.3) | copy-start | bytes 196
  26.0 11.4 %copy-start.2 = (s32[16]{0:T(128)S(1)}, s32[16]{0:T(128)}, u32[]{:S(2)}) copy-start(s32[16]{0:T(128)} %len_ref.1) | copy-start | bytes 196
  26.1 1.6 %collective-permute-start.10 = (bf16[64,1792]{1,0:T(8,128)(2,1)S(1)}, bf16[64,1792]{1,0:T(8,128)(2,1)S(1)}, u32[]{:S(2)}, u32[]{:S(2)}) collective-permute-start(bf16[64,1792]{1,0:T(8,128)(2,1)S(1)} %get-tuple-element.44), channel_id=1, source_target_pairs={{0,1},{1,0},{2,3},{3,2},{4,5},{5,4},{6,7},{7,6},{8,9},{9,8},{10,11... | collective-permute-start | bytes 688136 | tf_op jit(solution)/shard_map/ppermute | solution.py:24
  26.3 3.5 %collective-permute-start.9 = (bf16[64,1792]{1,0:T(8,128)(2,1)S(1)}, bf16[64,1792]{1,0:T(8,128)(2,1)S(1)}, u32[]{:S(2)}, u32[]{:S(2)}) collective-permute-start(bf16[64,1792]{1,0:T(8,128)(2,1)S(1)} %get-tuple-element.41), channel_id=1, source_target_pairs={{0,1},{1,0},{2,3},{3,2},{4,5},{5,4},{6,7},{7,6},{8,9},{9,8},{10,11... | collective-permute-start | bytes 688136 | tf_op jit(solution)/shard_map/ppermute | solution.py:24
  27.7 6.1 %collective-permute-start.13 = (bf16[32,1792]{1,0:T(8,128)(2,1)S(1)}, bf16[32,1792]{1,0:T(8,128)(2,1)S(1)}, u32[]{:S(2)}, u32[]{:S(2)}) collective-permute-start(bf16[32,1792]{1,0:T(8,128)(2,1)S(1)} %convert_element_type.7), channel_id=1, source_target_pairs={{0,2},{1,3},{2,0},{3,1},{4,6},{5,7},{6,4},{7,5},{8,10},{9,11},{10,... | collective-permute-start | bytes 344072 | tf_op jit(solution)/shard_map/ppermute | solution.py:24
  28.3 7.7 %collective-permute-start.11 = (bf16[32,1792]{1,0:T(8,128)(2,1)S(1)}, bf16[32,1792]{1,0:T(8,128)(2,1)S(1)}, u32[]{:S(2)}, u32[]{:S(2)}) collective-permute-start(bf16[32,1792]{1,0:T(8,128)(2,1)S(1)} %convert_element_type.6), channel_id=1, source_target_pairs={{0,2},{1,3},{2,0},{3,1},{4,6},{5,7},{6,4},{7,5},{8,10},{9,11},{10,... | collective-permute-start | bytes 344072 | tf_op jit(solution)/shard_map/ppermute | solution.py:24
  33.8 5.9 %collective-permute-start.14 = (bf16[16,1792]{1,0:T(8,128)(2,1)S(1)}, bf16[16,1792]{1,0:T(8,128)(2,1)S(1)}, u32[]{:S(2)}, u32[]{:S(2)}) collective-permute-start(bf16[16,1792]{1,0:T(8,128)(2,1)S(1)} %get-tuple-element.50), channel_id=1, source_target_pairs={{0,8},{4,12},{8,0},{12,4},{1,9},{5,13},{9,1},{13,5},{2,10},{6,14},... | collective-permute-start | bytes 172040 | tf_op jit(solution)/shard_map/ppermute | solution.py:24
  35.4 6.0 %collective-permute-start.15 = (bf16[16,1792]{1,0:T(8,128)(2,1)S(1)}, bf16[16,1792]{1,0:T(8,128)(2,1)S(1)}, u32[]{:S(2)}, u32[]{:S(2)}) collective-permute-start(bf16[16,1792]{1,0:T(8,128)(2,1)S(1)} %get-tuple-element.51), channel_id=1, source_target_pairs={{0,12},{4,8},{8,4},{12,0},{1,13},{5,9},{9,5},{13,1},{2,14},{6,10},... | collective-permute-start | bytes 172040 | tf_op jit(solution)/shard_map/ppermute | solution.py:24
  36.0 5.3 %collective-permute-start.12 = (bf16[16,1792]{1,0:T(8,128)(2,1)S(1)}, bf16[16,1792]{1,0:T(8,128)(2,1)S(1)}, u32[]{:S(2)}, u32[]{:S(2)}) collective-permute-start(bf16[16,1792]{1,0:T(8,128)(2,1)S(1)} %get-tuple-element.47), channel_id=1, source_target_pairs={{0,4},{4,0},{8,12},{12,8},{1,5},{5,1},{9,13},{13,9},{2,6},{6,2},{1... | collective-permute-start | bytes 172040 | tf_op jit(solution)/shard_map/ppermute | solution.py:24

commit v3 on v2

v3 whole, which is shorter than its diff:
```python
import functools

import jax
import jax.numpy as jnp
from jax import lax
from jax.experimental import pallas as pl
from jax.experimental.pallas import tpu as pltpu
from jax.sharding import PartitionSpec as P

LATC = 512
CAP = 16

score_scale = 192.0 ** (-0.5)

bf16, f32, i32 = jnp.bfloat16, jnp.float32, jnp.int32
VMEM = pl.BlockSpec(memory_space=pltpu.VMEM)
SMEM = pl.BlockSpec(memory_space=pltpu.SMEM)
HBM = pl.BlockSpec(memory_space=pltpu.HBM)
ANY = pl.BlockSpec(memory_space=pl.ANY)


def swap(value, axis, mask):
    count = lax.axis_size(axis)
    return lax.ppermute(value, axis, [(i, i ^ mask) for i in range(count)])


def in_hbm(value):
    return pltpu.with_memory_space_constraint(value, pltpu.HBM)


def params(arrays, extra=6 << 20):
    held = sum(a.size * a.dtype.itemsize for a in arrays)
    return pltpu.CompilerParams(vmem_limit_bytes=min(held + extra, 60 << 20))


def cost(flops, moved=0):
    return pl.CostEstimate(flops=flops, bytes_accessed=moved, transcendentals=0)


def fold_widths(latr):
    first = latr // 2 // 128 * 128
    return first, latr - first, -(-(latr - first) // 128) * 128


def slots_of(ids, own, ep_count):
    token_count = ids.shape[1]
    served = []
    for d in range(ep_count):
        named = jnp.where(ids == (own ^ d), 1.0, 0.0)
        served.append(jnp.sum(named, axis=0, keepdims=True))
    shape = (token_count, token_count)
    earlier = lax.broadcasted_iota(i32, shape, 0) < lax.broadcasted_iota(i32, shape, 1)
    marks = jnp.concatenate(served, axis=0)
    rank = jnp.dot(
        marks.astype(bf16), jnp.where(earlier, 1.0, 0.0).astype(bf16), preferred_element_type=f32
    )
    rank = jnp.where(marks > 0.5, rank, -1.0)
    slots = lax.broadcasted_iota(i32, (CAP, token_count), 0).astype(f32)
    return [slots == rank[d : d + 1] for d in range(ep_count)]


def route_kernel(ep_count, *refs):
    sources, blocks = refs[:4], refs[4 : 4 + ep_count]
    held, sems = refs[4 + ep_count : -1], refs[-1]
    copies = [pltpu.make_async_copy(sources[i], held[i], sems.at[i]) for i in range(4)]
    for copy in copies:
        copy.start()
    ids_ref, dest_ref, cache_ref, tokens_ref = held
    own = lax.axis_index("ep")
    width = tokens_ref.shape[1]
    first, second, wide = fold_widths(cache_ref.shape[2])
    part = cache_ref.shape[1]
    copies[0].wait()
    chosen = slots_of(ids_ref[...], own, ep_count)
    dispatch = jnp.concatenate([jnp.where(c, 1.0, 0.0) for c in chosen], axis=0).astype(bf16)
    copies[1].wait()
    copies[2].wait()
    for d in range(ep_count):
        pick = i32(0)
        for k in range(ep_count):
            pick = jnp.where(dest_ref[own, k] == (own ^ d), k, pick)
        kept = cache_ref[pick].astype(f32)
        above = jnp.concatenate([kept[:, :first], jnp.zeros((part, wide - first), f32)], axis=1)
        below = jnp.concatenate([kept[:, first:], jnp.zeros((part, wide - second), f32)], axis=1)
        blocks[d][:, width:] = jnp.concatenate([above, below], axis=0).astype(bf16)
    copies[3].wait()
    rows = jnp.dot(dispatch, tokens_ref[...], preferred_element_type=f32)
    for d in range(ep_count):
        blocks[d][:, :width] = rows[d * CAP : (d + 1) * CAP].astype(bf16)


def route(ids, tokens, cache_rows, destination, ep_count):
    width = tokens.shape[1]
    wide = fold_widths(cache_rows.shape[2])[2]
    sources = [ids, destination, cache_rows, tokens]
    out_shape = [jax.ShapeDtypeStruct((CAP, width + wide), bf16)] * ep_count
    places = [pltpu.VMEM, pltpu.SMEM, pltpu.VMEM, pltpu.VMEM]
    return pl.pallas_call(
        functools.partial(route_kernel, ep_count),
        out_shape=out_shape,
        in_specs=[HBM] * 4,
        out_specs=[VMEM] * ep_count,
        scratch_shapes=[p(a.shape, a.dtype) for p, a in zip(places, sources)]
        + [pltpu.SemaphoreType.DMA((4,))],
        compiler_params=params(sources * 2 + out_shape * 2),
        cost_estimate=cost(4 * ep_count * CAP * tokens.size, 2 * tokens.size),
        name="route",
    )(*map(in_hbm, sources))


def gates_kernel(ep_count, cuts, ids_ref, gates_ref, *refs):
    mark_ref = refs[-2]
    copies = start_copies(cuts, refs)
    ids, gates, own = ids_ref[...], gates_ref[...], lax.axis_index("ep")
    chosen = slots_of(ids, own, ep_count)
    table = []
    for d in range(ep_count):
        named = ids == (own ^ d)
        gate = jnp.sum(jnp.where(named, gates, 0.0), axis=0, keepdims=True)
        table.append(jnp.where(chosen[d], gate, 0.0))
    table = jnp.concatenate(table, axis=0)
    high = table.astype(bf16).astype(f32)
    mark_ref[...] = jnp.concatenate([high, table - high], axis=0).T.astype(bf16)
    for copy in copies:
        copy.wait()


def start_copies(cuts, refs):
    count, sems = (len(refs) - 2) // 2, refs[-1]
    copies = []
    for i in range(count):
        rows = refs[i].shape[0] // cuts
        for c in range(cuts):
            at = pl.ds(c * rows, rows)
            copies.append(
                pltpu.make_async_copy(refs[i].at[at], refs[count + i].at[at], sems.at[i, c])
            )
    for copy in copies:
        copy.start()
    return copies


def fetch(arrays, ids, gates, ep_count):
    cuts = 4
    mark = jax.ShapeDtypeStruct((ids.shape[1], 2 * ep_count * CAP), bf16)
    outs = pl.pallas_call(
        functools.partial(gates_kernel, ep_count, cuts),
        out_shape=[pltpu.VMEM(a.shape, a.dtype) for a in arrays] + [mark],
        in_specs=[VMEM] * 2 + [HBM] * len(arrays),
        out_specs=[VMEM] * (len(arrays) + 1),
        scratch_shapes=[pltpu.SemaphoreType.DMA((len(arrays), cuts))],
        compiler_params=params([mark] * 4),
        cost_estimate=cost(0, 0),
        name="fetch",
    )(*map(in_hbm, [ids, gates, *arrays]))
    return outs[:-1], outs[-1]


def fetch_part_kernel(part, parts, source_ref, *refs):
    out_ref, sems = refs[-2:]
    rows = source_ref.shape[0] // parts // 2
    copies = []
    for c in range(2):
        at = pl.ds(part * 2 * rows + c * rows, rows)
        copies.append(pltpu.make_async_copy(source_ref.at[at], out_ref.at[at], sems.at[c]))
    for copy in copies:
        copy.start()
    for copy in copies:
        copy.wait()


def fetch_part(array, part, parts, after, held=None):
    extra = () if held is None else (held,)
    return pl.pallas_call(
        functools.partial(fetch_part_kernel, part, parts),
        out_shape=pltpu.VMEM(array.shape, array.dtype),
        in_specs=[HBM] + [VMEM] * len(extra) + [ANY] * len(after),
        out_specs=VMEM,
        input_output_aliases={1: 0} if extra else {},
        scratch_shapes=[pltpu.SemaphoreType.DMA((2,))],
        compiler_params=pltpu.CompilerParams(vmem_limit_bytes=1 << 20),
        cost_estimate=cost(0, 0),
        name="fetch_part",
    )(in_hbm(array), *extra, *after)


def join_kernel(count, *refs):
    out_ref, at = refs[-1], 0
    for ref in refs[:count]:
        out_ref[at : at + ref.shape[0], :] = ref[...]
        at += ref.shape[0]


def join(blocks, after=(), weight=0):
    rows = sum(b.shape[0] for b in blocks)
    out_shape = jax.ShapeDtypeStruct((rows, blocks[0].shape[1]), blocks[0].dtype)
    return pl.pallas_call(
        functools.partial(join_kernel, len(blocks)),
        out_shape=out_shape,
        in_specs=[VMEM] * len(blocks) + [ANY] * len(after),
        out_specs=VMEM,
        compiler_params=params([out_shape] * 3, 1 << 20),
        cost_estimate=cost(0, weight),
        name="join",
    )(*blocks, *after)


def tie_kernel(*refs):
    pass


def tie(value, after):
    return pl.pallas_call(
        tie_kernel,
        out_shape=jax.ShapeDtypeStruct(value.shape, value.dtype),
        in_specs=[ANY] * (1 + len(after)),
        out_specs=ANY,
        input_output_aliases={0: 0},
        compiler_params=pltpu.CompilerParams(vmem_limit_bytes=1 << 20),
        cost_estimate=cost(0, 0),
        name="tie",
    )(value, *after)


def total_kernel(kept_ref, arrived_ref, *outs):
    at = 0
    for out in outs:
        rows = pl.ds(at, out.shape[0])
        out[...] = (kept_ref[rows, :] + arrived_ref[rows, :].astype(f32)).astype(out.dtype)
        at += out.shape[0]


def total(kept, arrived, count, dtype=bf16):
    rows, columns = kept.shape
    out_shape = [jax.ShapeDtypeStruct((rows // count, columns), dtype)] * count
    return pl.pallas_call(
        total_kernel,
        out_shape=out_shape,
        in_specs=[VMEM, VMEM],
        out_specs=[VMEM] * count,
        compiler_params=params([kept] * 4, 1 << 20),
        cost_estimate=cost(kept.size, 8 * kept.size),
        name="total",
    )(kept, arrived)


def piece_sums(piece_refs, masks, me, width, gate_ref, up_ref):
    gate_sums = up_sums = None
    for refs, m in zip(piece_refs, masks):
        rows = jnp.concatenate([r[:, :width] for r in refs], axis=0)
        at = pl.ds(pl.multiple_of((me ^ m) * width, width), width)
        g = jnp.dot(rows, gate_ref[at, :], preferred_element_type=f32)
        u = jnp.dot(rows, up_ref[at, :], preferred_element_type=f32)
        gate_sums = g if gate_sums is None else gate_sums + g
        up_sums = u if up_sums is None else up_sums + u
    return gate_sums, up_sums


def gate_up_kernel(masks, width, has_sums, gate_ref, up_ref, *refs):
    before, refs = (refs[:2], refs[2:]) if has_sums else ((), refs)
    pieces, outs = refs[:-2], refs[-2:]
    per = len(pieces) // len(masks)
    groups = [pieces[i * per : (i + 1) * per] for i in range(len(masks))]
    sums = piece_sums(groups, masks, lax.axis_index("pd"), width, gate_ref, up_ref)
    for i in range(2):
        outs[i][...] = sums[i] + before[i][...] if has_sums else sums[i]


def gate_up(masks, width, w_gate, w_up, pieces, before=()):
    operands = [g for m in masks for g in pieces[m]]
    rows = sum(g.shape[0] for g in pieces[masks[0]])
    sums = jax.ShapeDtypeStruct((rows, w_gate.shape[1]), f32)
    return pl.pallas_call(
        functools.partial(gate_up_kernel, masks, width, bool(before)),
        out_shape=[sums, sums],
        in_specs=[VMEM] * (2 + len(before) + len(operands)),
        out_specs=[VMEM, VMEM],
        compiler_params=params(operands * 2),
        cost_estimate=cost(4 * rows * w_gate.size, 4 * w_gate.size),
        name="gate_up",
    )(w_gate, w_up, *before, *operands)


def hidden_kernel(masks, target, width, gate_ref, up_ref, down_ref, *refs):
    (gsum_ref, usum_ref), pieces, (hidden_ref, out_ref) = refs[:2], refs[2:-2], refs[-2:]
    per = len(pieces) // len(masks)
    groups = [pieces[i * per : (i + 1) * per] for i in range(len(masks))]
    me = lax.axis_index("pd")
    gate_sums, up_sums = piece_sums(groups, masks, me, width, gate_ref, up_ref)
    gate_sums, up_sums = gate_sums + gsum_ref[...], up_sums + usum_ref[...]
    hidden = (gate_sums / (1.0 + jnp.exp(-gate_sums)) * up_sums).astype(bf16)
    hidden_ref[...] = hidden
    at = pl.ds(pl.multiple_of((me ^ target) * width, width), width)
    out_ref[...] = jnp.dot(hidden, down_ref[:, at], preferred_element_type=f32).astype(bf16)


def hidden_units_of(masks, target, width, w_gate, w_up, w_down, sums, pieces):
    operands = [g for m in masks for g in pieces[m]]
    rows, units = sums[0].shape
    out_shape = [jax.ShapeDtypeStruct((rows, n), bf16) for n in (units, width)]
    return pl.pallas_call(
        functools.partial(hidden_kernel, masks, target, width),
        out_shape=out_shape,
        in_specs=[VMEM] * (5 + len(operands)),
        out_specs=[VMEM] * 2,
        compiler_params=params(operands * 2 + out_shape * 2),
        cost_estimate=cost(6 * rows * w_gate.size, 4 * w_gate.size),
        name="hidden",
    )(w_gate, w_up, w_down, *sums, *operands)


def down_kernel(targets, width, hidden_ref, down_ref, *outs):
    me = lax.axis_index("pd")
    for out, m in zip(outs, targets):
        at = pl.ds(pl.multiple_of((me ^ m) * width, width), width)
        product = jnp.dot(hidden_ref[...], down_ref[:, at], preferred_element_type=f32)
        out[...] = product.astype(out.dtype)


def down(targets, width, hidden, w_down, dtype):
    out_shape = [jax.ShapeDtypeStruct((hidden.shape[0], width), dtype)] * len(targets)
    return pl.pallas_call(
        functools.partial(down_kernel, targets, width),
        out_shape=out_shape,
        in_specs=[VMEM, VMEM],
        out_specs=[VMEM] * len(out_shape),
        compiler_params=params(out_shape * 2),
        cost_estimate=cost(2 * hidden.shape[0] * w_down.size, 2 * w_down.size),
        name="down",
    )(hidden, w_down)


def attend_kernel(ep_count, pd_count, width, dest_ref, len_ref, query_ref, *refs):
    pieces, out_ref = refs[:-1], refs[-1]
    per = len(pieces) // pd_count
    own, me = lax.axis_index("ep"), lax.axis_index("pd")
    rows, latr = query_ref.shape
    first, second, wide = fold_widths(latr)
    part, heads = CAP // 2, rows // ep_count
    keys = []
    for ref in pieces:
        count = ref.shape[0] // CAP
        folded = ref[:, width:].astype(f32).reshape(count, CAP, wide)
        whole = jnp.concatenate([folded[:, :part, :first], folded[:, part:, :second]], axis=2)
        keys.append(whole.reshape(count * part, latr))
    keys = jnp.concatenate(keys, axis=0).astype(bf16)
    shape = (1, keys.shape[0])
    column = lax.broadcasted_iota(i32, shape, 1)
    block = column // part % ep_count
    position = (me ^ (column // (part * ep_count))) * part + column % part
    length = jnp.zeros(shape, i32)
    for d in range(ep_count):
        j = own ^ d
        here = i32(0)
        for k in range(ep_count):
            here = jnp.where(dest_ref[j, k] == own, len_ref[j * ep_count + k], here)
        length = jnp.where(block == d, here, length)
    slot = jnp.where(position < length, own ^ block, -1)
    usable = lax.broadcasted_iota(i32, (rows, 1), 0) // heads == slot
    scores = lax.dot_general(
        query_ref[...], keys, (((1,), (1,)), ((), ())), preferred_element_type=f32
    )
    scores = scores * score_scale
    top = jnp.max(jnp.where(usable, scores, -1e30), axis=1, keepdims=True)
    weights = jnp.where(usable, jnp.exp(scores - top), 0.0)
    total = jnp.sum(weights, axis=1, keepdims=True)
    summed = jnp.dot(weights.astype(bf16), keys[:, :LATC], preferred_element_type=f32)
    out_ref[...] = (summed / total).astype(bf16)


def combine_kernel(cuts, table_ref, *refs):
    blocks, (out_ref, held_ref, sems) = refs[:-3], refs[-3:]
    rows = jnp.concatenate([b[...] for b in blocks] * 2, axis=0)
    table, width = table_ref[...], held_ref.shape[1] // cuts
    copies = []
    for c in range(cuts):
        at = pl.ds(c * width, width)
        mixed = jnp.dot(
            table, rows[:, c * width : (c + 1) * width], preferred_element_type=f32
        )
        held_ref[:, at] = mixed.astype(bf16)
        copies.append(pltpu.make_async_copy(held_ref.at[:, at], out_ref.at[:, at], sems.at[c]))
        copies[-1].start()
    for copy in copies:
        copy.wait()


def mix(table, blocks):
    mixed = jax.ShapeDtypeStruct((table.shape[0], blocks[0].shape[1]), bf16)
    cuts = 2 if mixed.shape[1] % 256 == 0 else 1
    return pl.pallas_call(
        functools.partial(combine_kernel, cuts),
        out_shape=mixed,
        in_specs=[VMEM] * (1 + len(blocks)),
        out_specs=HBM,
        scratch_shapes=[pltpu.VMEM(mixed.shape, bf16), pltpu.SemaphoreType.DMA((cuts,))],
        compiler_params=params([mixed] * 4 + blocks * 2),
        cost_estimate=cost(4 * CAP * len(blocks) * mixed.size, 2 * mixed.size),
        name="combine",
    )(table, *blocks)


def spread(pieces, m, bit):
    have = [m]
    while bit:
        for k in list(have):
            pieces[k ^ bit] = [swap(g, "pd", bit) for g in pieces[k]]
            have.append(k ^ bit)
        bit //= 2


def on_device(
    tokens,
    expert_ids,
    gate_scores,
    gate_weight,
    up_weight,
    down_weight,
    cache_rows,
    lengths,
    destination,
    decode_query,
):
    ep_count = lax.axis_size("ep")
    pd_count = lax.axis_size("pd")
    width = tokens.shape[1]
    half = ep_count // 2
    ids = expert_ids.T

    blocks = route(ids, tokens, cache_rows, destination, ep_count)
    arrived = [blocks[0]] + [swap(blocks[d], "ep", d) for d in range(1, ep_count)]
    bit = pd_count // 2
    over = swap(blocks[0], "pd", bit)
    (w_gate, w_up), table = fetch([gate_weight[0], up_weight[0]], ids, gate_scores.T, ep_count)
    rest = join(arrived[1:], [table, over])
    pieces = {0: [blocks[0], rest]}
    pieces[bit] = [over, swap(rest, "pd", bit)]
    pieces[0][1] = join(arrived[1:], [rest])
    w_down = fetch_part(down_weight[0], 0, 1, pieces[0])
    spread(pieces, 0, bit // 2)
    sums = gate_up([0], width, w_gate, w_up, pieces)
    pieces[bit][1] = tie(pieces[bit][1], [sums[0], w_down])
    spread(pieces, bit, bit // 2)
    sums = gate_up(list(range(1, bit + 1)), width, w_gate, w_up, pieces, before=sums)
    late = list(range(bit + 1, pd_count))
    others = sorted([m for m in range(pd_count) if m & 1], reverse=True)
    stay = sorted([m for m in range(pd_count) if not m & 1], reverse=True)
    hidden, part = hidden_units_of(
        late, others[0], width, w_gate, w_up, w_down, sums, pieces
    )
    parts = {others[0]: part}
    parts.update(zip(others[1:], down(others[1:], width, hidden, w_down, bf16)))
    kept = dict(zip(stay, down(stay, width, hidden, w_down, f32)))
    cut = half * CAP
    for m in stay:
        sent = bf16 if m & 2 else f32
        kept[m] = dict(zip((0, cut), total(kept[m], swap(parts[m ^ 1], "pd", 1), 2, sent)))

    operands = [g for m in range(pd_count) for g in pieces[m]]
    queries = decode_query.reshape(-1, decode_query.shape[3])
    attended = jax.ShapeDtypeStruct((queries.shape[0], LATC), bf16)
    attended = pl.pallas_call(
        functools.partial(attend_kernel, ep_count, pd_count, width),
        out_shape=attended,
        in_specs=[SMEM, SMEM, VMEM] + [VMEM] * len(operands),
        out_specs=VMEM,
        compiler_params=params(operands + [queries, attended] * 4, 12 << 20),
        cost_estimate=cost(8 * CAP * ep_count * tokens.size, 8 * tokens.size),
        name="attend",
    )(*map(in_hbm, [destination, lengths, queries]), *operands)

    returned = [None] * ep_count
    for low in (cut, 0):
        rows = {m: kept[m][low] for m in stay}
        bit = 2
        while bit < pd_count:
            last = bit * 2 == pd_count
            for m in sorted(rows, reverse=True):
                if m & bit:
                    sent = rows.pop(m).astype(bf16)
                    over = swap(sent, "pd", bit)
                    rows[m ^ bit] = total(rows[m ^ bit], over, half if last else 1, bf16 if last else f32)
                    rows[m ^ bit] = rows[m ^ bit] if last else rows[m ^ bit][0]
            bit *= 2
        for i, block in enumerate(rows[0]):
            d = low // CAP + i
            returned[d] = swap(block, "ep", d) if d else block
    mixed = mix(table, returned)
    return (mixed, attended.reshape(decode_query.shape[:3] + (LATC,)))


def solution(mesh):
    in_specs = (
        P(("group", "ep"), "pd"),
        P(("group", "ep"), None),
        P(("group", "ep"), None),
        P("ep", None, "pd"),
        P("ep", None, "pd"),
        P("ep", "pd", None),
        P(("group", "ep"), "pd", None),
        P("group"),
        P("group", None),
        P(("group", "ep"), None, "pd", None),
    )
    out_specs = (P(("group", "ep"), "pd"), P(("group", "ep"), None, "pd", None))
    return jax.shard_map(
        on_device, mesh=mesh, in_specs=in_specs, out_specs=out_specs, check_vma=False
    )
```

time: 43.1 us -> 41.3 us (0.958)
  waiting for transfers between devices: 13.8 us -> 11.8 us
    ppermute x16, waiting for transfers between devices: 13.8 us -> 11.8 us  [swap(): return lax.ppermute(value, axis, [(i, i ^ mask) for i in range(count)])]
    pallas_call x6 -> x8, Pallas kernels: 9.2 us -> 9.86 us  [the longest x1 3.88 us: fetch(): pl.pallas_call(functools.partial(gates_kernel, ep_count, cuts), out_shape...]
  transfers between devices with their start and end apart: 16 -> 16, of which waited for: 7 -> 8; matrix products, arithmetic and copies ran while one was open for 0% -> 0% of each run, Pallas kernels for 20% -> 24%
where the time goes in v3:
time: 41.3 us; the launch traced here: 41 us
  starting transfers between devices  14.9 us (36%)
  Pallas kernels  13.5 us (33%)
  waiting for transfers between devices  11.8 us (29%)
  between operations  0.74 us (2%)
    ppermute x16, starting transfers between devices, swap(): return lax.ppermute(value, axis, [(i, i ^ mask) for i in range(count)])  14.9 us
    ppermute x16, waiting for transfers between devices, swap(): return lax.ppermute(value, axis, [(i, i ^ mask) for i in range(count)])  11.8 us
    pallas_call x1, Pallas kernels, fetch(): pl.pallas_call(functools.partial(gates_kernel, ep_count, cuts), out_shape...  3.88 us
    pallas_call x1, Pallas kernels, fetch_part(): pl.pallas_call(functools.partial(fetch_part_kernel, part, parts), out_sha...  2.07 us
    pallas_call x1, Pallas kernels, on_device(): pl.pallas_call(functools.partial(attend_kernel, ep_count, pd_count, width...  1.96 us
    pallas_call x1, Pallas kernels, route(): pl.pallas_call(functools.partial(route_kernel, ep_count), out_shape=out_s...  1.56 us
    pallas_call x1, Pallas kernels, mix(): pl.pallas_call(functools.partial(combine_kernel, cuts), out_shape=mixed,...  1.22 us
    pallas_call x2, Pallas kernels, gate_up(): pl.pallas_call(functools.partial(gate_up_kernel, masks, width, bool(befor...  1.21 us
  transfers between devices with their start and end apart: 16, of which 8 were waited for; matrix products, arithmetic and copies ran while one was open for 0% of the time, Pallas kernels for 24%

profile of v3, /device:TPU:0, one launch (start us, length us, event | category | flops | bytes accessed | tf_op | source)
XLA Modules:
  0.0 41.0 jit_solution(2698439655531738103)
XLA Ops:
  0.6 1.6 %route.1 = (bf16[16,2176]{1,0:T(8,128)(2,1)S(1)}, bf16[16,2176]{1,0:T(8,128)(2,1)S(1)}, bf16[16,2176]{1,0:T(8,128)(2,1)S(1)}, bf16[16,2176]{1,0:T(8,128)(2,1)S(1)}) custom-call(s32[8,256]{1,0:T(8,128)} %bitcast.12, s32[4,4]{1,0:T(4,128)} %dest_ref.1, bf16[4,8,576]{2,1,0:T(8,128)(2,1)} %refs_2_.1, bf16[256,1792]{1,0:T(8,128)(2,1)} %refs_3_.1), custom_call_target="tpu_custom_call" | custom-call | flops 117440512 | bytes 917504 | tf_op jit(solution)/shard_map/route/pallas_call | solution.py:98
  2.2 3.0 %collective-permute-start.3 = (bf16[16,2176]{1,0:T(8,128)(2,1)S(1)}, bf16[16,2176]{1,0:T(8,128)(2,1)S(1)}, u32[]{:S(2)}, u32[]{:S(2)}) collective-permute-start(bf16[16,2176]{1,0:T(8,128)(2,1)S(1)} %get-tuple-element.28.refs_0_), channel_id=1, source_target_pairs={{0,2},{1,3},{2,0},{3,1},{4,6},{5,7},{6,4},{7,5},{8,10},{9,11},{10,... | collective-permute-start | bytes 208904 | tf_op jit(solution)/shard_map/ppermute | solution.py:24
  5.2 1.6 %collective-permute-start = (bf16[16,2176]{1,0:T(8,128)(2,1)S(1)}, bf16[16,2176]{1,0:T(8,128)(2,1)S(1)}, u32[]{:S(2)}, u32[]{:S(2)}) collective-permute-start(bf16[16,2176]{1,0:T(8,128)(2,1)S(1)} %get-tuple-element.29), channel_id=1, source_target_pairs={{0,4},{4,0},{8,12},{12,8},{1,5},{5,1},{9,13},{13,9},{2,6},{6,2},{1... | collective-permute-start | bytes 208904 | tf_op jit(solution)/shard_map/ppermute | solution.py:24
  6.8 2.6 %collective-permute-start.1 = (bf16[16,2176]{1,0:T(8,128)(2,1)S(1)}, bf16[16,2176]{1,0:T(8,128)(2,1)S(1)}, u32[]{:S(2)}, u32[]{:S(2)}) collective-permute-start(bf16[16,2176]{1,0:T(8,128)(2,1)S(1)} %get-tuple-element.30), channel_id=1, source_target_pairs={{0,8},{4,12},{8,0},{12,4},{1,9},{5,13},{9,1},{13,5},{2,10},{6,14},... | collective-permute-start | bytes 208904 | tf_op jit(solution)/shard_map/ppermute | solution.py:24
  9.4 0.2 collective-permute-start.2
  9.6 3.9 %fetch.1 = (bf16[7168,256]{1,0:T(8,128)(2,1)S(1)}, bf16[7168,256]{1,0:T(8,128)(2,1)S(1)}, bf16[256,128]{1,0:T(8,128)(2,1)S(1)}) custom-call(s32[8,256]{1,0:T(8,128)} %bitcast.13, f32[8,256]{1,0:T(8,128)} %bitcast.14, bf16[7168,256]{1,0:T(8,128)(2,1)} %bitcast.7, bf16[7168,256]{1,0:T(8,128)(2,1)} %bitcast.8), custom_call_target="tpu_custom_call" | custom-call | tf_op jit(solution)/shard_map/fetch/pallas_call | solution.py:146
  13.5 0.0 collective-permute-done.3.refs_4_
  13.5 0.0 collective-permute-done.refs_0_
  13.5 0.5 %collective-permute-done.1.refs_1_ = bf16[16,2176]{1,0:T(8,128)(2,1)S(1)} collective-permute-done((bf16[16,2176]{1,0:T(8,128)(2,1)S(1)}, bf16[16,2176]{1,0:T(8,128)(2,1)S(1)}, u32[]{:S(2)}, u32[]{:S(2)}) %collective-permute-start.1) | collective-permute-done | bytes 69664 | tf_op jit(solution)/shard_map/ppermute | solution.py:24
  14.0 1.5 %collective-permute-done.2.refs_2_ = bf16[16,2176]{1,0:T(8,128)(2,1)S(1)} collective-permute-done((bf16[16,2176]{1,0:T(8,128)(2,1)S(1)}, bf16[16,2176]{1,0:T(8,128)(2,1)S(1)}, u32[]{:S(2)}, u32[]{:S(2)}) %collective-permute-start.2) | collective-permute-done | bytes 69664 | tf_op jit(solution)/shard_map/ppermute | solution.py:24
  15.5 0.6 %collective-permute-start.6 = (bf16[48,2176]{1,0:T(8,128)(2,1)S(1)}, bf16[48,2176]{1,0:T(8,128)(2,1)S(1)}, u32[]{:S(2)}, u32[]{:S(2)}) collective-permute-start(bf16[48,2176]{1,0:T(8,128)(2,1)S(1)} %join.2.refs_3_), channel_id=1, source_target_pairs={{0,2},{1,3},{2,0},{3,1},{4,6},{5,7},{6,4},{7,5},{8,10},{9,11},{10,... | collective-permute-start | bytes 626696 | tf_op jit(solution)/shard_map/ppermute | solution.py:24
  16.1 0.1 collective-permute-start.5
  16.2 2.1 %fetch_part.1.refs_2_.down_ref = bf16[256,7168]{1,0:T(8,128)(2,1)S(1)} custom-call(bf16[256,7168]{1,0:T(8,128)(2,1)} %bitcast.9, bf16[16,2176]{1,0:T(8,128)(2,1)S(1)} %get-tuple-element.28.refs_0_, bf16[48,2176]{1,0:T(8,128)(2,1)S(1)} %join.3.refs_1_), custom_call_target="tpu_custom_call" | custom-call | tf_op jit(solution)/shard_map/fetch_part/pallas_call | solution.py:174
  18.3 0.4 %gate_up.2 = (f32[64,256]{1,0:T(8,128)S(1)}, f32[64,256]{1,0:T(8,128)S(1)}) custom-call(bf16[7168,256]{1,0:T(8,128)(2,1)S(1)} %get-tuple-element.26.gate_ref, bf16[7168,256]{1,0:T(8,128)(2,1)S(1)} %get-tuple-element.27.up_ref, bf16[16,2176]{1,0:T(8,128)(2,1)S(1)} %get-tuple-element.28.refs_0_, bf16[48,2176]{1,0:T(8,128)(2,1)S(1)} %join.3.refs_1_), custom_call_target="tpu_custom_call" | custom-call | flops 469762048 | bytes 7340032 | tf_op jit(solution)/shard_map/gate_up/pallas_call | solution.py:273
  18.8 2.6 %collective-permute-done.6.refs_0_ = bf16[48,2176]{1,0:T(8,128)(2,1)S(1)} collective-permute-done((bf16[48,2176]{1,0:T(8,128)(2,1)S(1)}, bf16[48,2176]{1,0:T(8,128)(2,1)S(1)}, u32[]{:S(2)}, u32[]{:S(2)}) %collective-permute-start.6) | collective-permute-done | bytes 208928 | tf_op jit(solution)/shard_map/ppermute | solution.py:24
  21.4 0.0 collective-permute-start.8
  21.4 0.5 %collective-permute-start.4 = (bf16[16,2176]{1,0:T(8,128)(2,1)S(1)}, bf16[16,2176]{1,0:T(8,128)(2,1)S(1)}, u32[]{:S(2)}, u32[]{:S(2)}) collective-permute-start(bf16[16,2176]{1,0:T(8,128)(2,1)S(1)} %get-tuple-element.28.refs_0_), channel_id=1, source_target_pairs={{0,1},{1,0},{2,3},{3,2},{4,5},{5,4},{6,7},{7,6},{8,9},{9,8},{10,11... | collective-permute-start | bytes 208904 | tf_op jit(solution)/shard_map/ppermute | solution.py:24
  21.9 0.0 collective-permute-start.7
  21.9 1.0 %collective-permute-done.4.refs_2_ = bf16[16,2176]{1,0:T(8,128)(2,1)S(1)} collective-permute-done((bf16[16,2176]{1,0:T(8,128)(2,1)S(1)}, bf16[16,2176]{1,0:T(8,128)(2,1)S(1)}, u32[]{:S(2)}, u32[]{:S(2)}) %collective-permute-start.4) | collective-permute-done | bytes 69664 | tf_op jit(solution)/shard_map/ppermute | solution.py:24
  23.0 0.0 collective-permute-done.5.refs_3_
  23.0 0.8 %gate_up.3 = (f32[64,256]{1,0:T(8,128)S(1)}, f32[64,256]{1,0:T(8,128)S(1)}) custom-call(bf16[7168,256]{1,0:T(8,128)(2,1)S(1)} %get-tuple-element.26.gate_ref, bf16[7168,256]{1,0:T(8,128)(2,1)S(1)} %get-tuple-element.27.up_ref, f32[64,256]{1,0:T(8,128)S(1)} %get-tuple-element.32.refs_1_.refs_0_, f32[64,256]{1,0:T(8,128)S(1)} %get-tuple-element.33.refs_1_, ...), custom_call_target="tpu_custom_call" | custom-call | flops 469762048 | bytes 7340032 | tf_op jit(solution)/shard_map/gate_up/pallas_call | solution.py:273
  23.7 0.0 collective-permute-done.7.refs_2_.refs_6_
  23.7 0.0 collective-permute-done.8.refs_3_.refs_7_
  23.8 0.7 %hidden.1 = (bf16[64,256]{1,0:T(8,128)(2,1)S(1)}, bf16[64,1792]{1,0:T(8,128)(2,1)S(1)}) custom-call(bf16[7168,256]{1,0:T(8,128)(2,1)S(1)} %get-tuple-element.26.gate_ref, bf16[7168,256]{1,0:T(8,128)(2,1)S(1)} %get-tuple-element.27.up_ref, bf16[256,7168]{1,0:T(8,128)(2,1)S(1)} %fetch_part.1.refs_2_.down_ref, f32[64,256]{1,0:T(8,128)S(1)} %get-tuple-element.34.refs_0_, ...), custom_call_target="tpu_custom_call" | custom-call | flops 704643072 | bytes 7340032 | tf_op jit(solution)/shard_map/hidden/pallas_call | solution.py:301
  24.5 0.3 collective-permute-start.10
  24.7 0.3 down.3
  25.0 0.4 collective-permute-start.9
  25.4 0.5 %down.2 = (f32[64,1792]{1,0:T(8,128)S(1)}, f32[64,1792]{1,0:T(8,128)S(1)}) custom-call(bf16[64,256]{1,0:T(8,128)(2,1)S(1)} %get-tuple-element.36.hidden_ref, bf16[256,7168]{1,0:T(8,128)(2,1)S(1)} %fetch_part.1.refs_2_.down_ref), custom_call_target="tpu_custom_call" | custom-call | flops 234881024 | bytes 3670016 | tf_op jit(solution)/shard_map/down/pallas_call | solution.py:322
  25.8 0.2 collective-permute-done.10.arrived_ref
  26.0 0.1 total.5
  26.1 0.6 %collective-permute-start.13 = (bf16[32,1792]{1,0:T(8,128)(2,1)S(1)}, bf16[32,1792]{1,0:T(8,128)(2,1)S(1)}, u32[]{:S(2)}, u32[]{:S(2)}) collective-permute-start(bf16[32,1792]{1,0:T(8,128)(2,1)S(1)} %get-tuple-element.45), channel_id=1, source_target_pairs={{0,2},{1,3},{2,0},{3,1},{4,6},{5,7},{6,4},{7,5},{8,10},{9,11},{10,... | collective-permute-start | bytes 344072 | tf_op jit(solution)/shard_map/ppermute | solution.py:24
  26.7 1.5 %collective-permute-start.11 = (bf16[32,1792]{1,0:T(8,128)(2,1)S(1)}, bf16[32,1792]{1,0:T(8,128)(2,1)S(1)}, u32[]{:S(2)}, u32[]{:S(2)}) collective-permute-start(bf16[32,1792]{1,0:T(8,128)(2,1)S(1)} %get-tuple-element.41), channel_id=1, source_target_pairs={{0,2},{1,3},{2,0},{3,1},{4,6},{5,7},{6,4},{7,5},{8,10},{9,11},{10,... | collective-permute-start | bytes 344072 | tf_op jit(solution)/shard_map/ppermute | solution.py:24
  28.2 0.0 collective-permute-done.9.arrived_ref
  28.2 3.9 %collective-permute-done.13.arrived_ref = bf16[32,1792]{1,0:T(8,128)(2,1)S(1)} collective-permute-done((bf16[32,1792]{1,0:T(8,128)(2,1)S(1)}, bf16[32,1792]{1,0:T(8,128)(2,1)S(1)}, u32[]{:S(2)}, u32[]{:S(2)}) %collective-permute-start.13) | collective-permute-done | bytes 114720 | tf_op jit(solution)/shard_map/ppermute | solution.py:24
  32.2 1.6 %collective-permute-start.14 = (bf16[16,1792]{1,0:T(8,128)(2,1)S(1)}, bf16[16,1792]{1,0:T(8,128)(2,1)S(1)}, u32[]{:S(2)}, u32[]{:S(2)}) collective-permute-start(bf16[16,1792]{1,0:T(8,128)(2,1)S(1)} %get-tuple-element.46), channel_id=1, source_target_pairs={{0,8},{4,12},{8,0},{12,4},{1,9},{5,13},{9,1},{13,5},{2,10},{6,14},... | collective-permute-start | bytes 172040 | tf_op jit(solution)/shard_map/ppermute | solution.py:24
  33.8 0.7 %collective-permute-start.15 = (bf16[16,1792]{1,0:T(8,128)(2,1)S(1)}, bf16[16,1792]{1,0:T(8,128)(2,1)S(1)}, u32[]{:S(2)}, u32[]{:S(2)}) collective-permute-start(bf16[16,1792]{1,0:T(8,128)(2,1)S(1)} %get-tuple-element.47), channel_id=1, source_target_pairs={{0,12},{4,8},{8,4},{12,0},{1,13},{5,9},{9,5},{13,1},{2,14},{6,10},... | collective-permute-start | bytes 172040 | tf_op jit(solution)/shard_map/ppermute | solution.py:24
  34.5 0.0 collective-permute-done.11.arrived_ref
  34.5 1.3 %collective-permute-start.12 = (bf16[16,1792]{1,0:T(8,128)(2,1)S(1)}, bf16[16,1792]{1,0:T(8,128)(2,1)S(1)}, u32[]{:S(2)}, u32[]{:S(2)}) collective-permute-start(bf16[16,1792]{1,0:T(8,128)(2,1)S(1)} %get-tuple-element.43), channel_id=1, source_target_pairs={{0,4},{4,0},{8,12},{12,8},{1,5},{5,1},{9,13},{13,9},{2,6},{6,2},{1... | collective-permute-start | bytes 172040 | tf_op jit(solution)/shard_map/ppermute | solution.py:24
  35.8 2.0 %attend.1 = bf16[64,512]{1,0:T(8,128)(2,1)} custom-call(s32[4,4]{1,0:T(4,128)} %dest_ref.1, s32[16]{0:T(128)} %len_ref.1, bf16[64,576]{1,0:T(8,128)(2,1)} %bitcast.10, bf16[16,2176]{1,0:T(8,128)(2,1)S(1)} %get-tuple-element.28.refs_0_, bf16[48,2176]{1,0:T(8,128)(2,1)S(1)} %join.3.refs_1_, bf16[16,2176]{1,0:T(8,128)(2,1)S(1)} %collective-permute-done.4.refs_2_, ...), custom_call_target="tpu_custom_call" | custom-call | flops 234881024 | bytes 3670016 | tf_op jit(solution)/shard_map/attend/pallas_call | solution.py:462
  37.8 0.1 collective-permute-done.14.refs_2_
  37.9 1.9 %collective-permute-done.15.refs_3_ = bf16[16,1792]{1,0:T(8,128)(2,1)S(1)} collective-permute-done((bf16[16,1792]{1,0:T(8,128)(2,1)S(1)}, bf16[16,1792]{1,0:T(8,128)(2,1)S(1)}, u32[]{:S(2)}, u32[]{:S(2)}) %collective-permute-start.15) | collective-permute-done | bytes 57376 | tf_op jit(solution)/shard_map/ppermute | solution.py:24
  39.8 0.0 collective-permute-done.12.refs_1_
  39.8 1.2 %combine.1 = bf16[256,1792]{1,0:T(8,128)(2,1)} custom-call(bf16[256,128]{1,0:T(8,128)(2,1)S(1)} %get-tuple-element.25.refs_3_.table_ref, bf16[16,1792]{1,0:T(8,128)(2,1)S(1)} %get-tuple-element.42.refs_0_, bf16[16,1792]{1,0:T(8,128)(2,1)S(1)} %collective-permute-done.12.refs_1_, bf16[16,1792]{1,0:T(8,128)(2,1)S(1)} %collective-permute-done.14.refs_2_, ...), custom_call_target="tpu_custom_call" | custom-call | flops 117440512 | bytes 917504 | tf_op jit(solution)/shard_map/combine/pallas_call | solution.py:391
  (6 shorter events, 0.1 us)
Async XLA Ops:
  2.2 11.3 %collective-permute-start.3 = (bf16[16,2176]{1,0:T(8,128)(2,1)S(1)}, bf16[16,2176]{1,0:T(8,128)(2,1)S(1)}, u32[]{:S(2)}, u32[]{:S(2)}) collective-permute-start(bf16[16,2176]{1,0:T(8,128)(2,1)S(1)} %get-tuple-element.28.refs_0_), channel_id=1, source_target_pairs={{0,2},{1,3},{2,0},{3,1},{4,6},{5,7},{6,4},{7,5},{8,10},{9,11},{10,... | collective-permute-start | bytes 208904 | tf_op jit(solution)/shard_map/ppermute | solution.py:24
  5.2 8.3 %collective-permute-start = (bf16[16,2176]{1,0:T(8,128)(2,1)S(1)}, bf16[16,2176]{1,0:T(8,128)(2,1)S(1)}, u32[]{:S(2)}, u32[]{:S(2)}) collective-permute-start(bf16[16,2176]{1,0:T(8,128)(2,1)S(1)} %get-tuple-element.29), channel_id=1, source_target_pairs={{0,4},{4,0},{8,12},{12,8},{1,5},{5,1},{9,13},{13,9},{2,6},{6,2},{1... | collective-permute-start | bytes 208904 | tf_op jit(solution)/shard_map/ppermute | solution.py:24
  6.8 7.2 %collective-permute-start.1 = (bf16[16,2176]{1,0:T(8,128)(2,1)S(1)}, bf16[16,2176]{1,0:T(8,128)(2,1)S(1)}, u32[]{:S(2)}, u32[]{:S(2)}) collective-permute-start(bf16[16,2176]{1,0:T(8,128)(2,1)S(1)} %get-tuple-element.30), channel_id=1, source_target_pairs={{0,8},{4,12},{8,0},{12,4},{1,9},{5,13},{9,1},{13,5},{2,10},{6,14},... | collective-permute-start | bytes 208904 | tf_op jit(solution)/shard_map/ppermute | solution.py:24
  9.4 6.1 %collective-permute-start.2 = (bf16[16,2176]{1,0:T(8,128)(2,1)S(1)}, bf16[16,2176]{1,0:T(8,128)(2,1)S(1)}, u32[]{:S(2)}, u32[]{:S(2)}) collective-permute-start(bf16[16,2176]{1,0:T(8,128)(2,1)S(1)} %get-tuple-element.31), channel_id=1, source_target_pairs={{0,12},{4,8},{8,4},{12,0},{1,13},{5,9},{9,5},{13,1},{2,14},{6,10},... | collective-permute-start | bytes 208904 | tf_op jit(solution)/shard_map/ppermute | solution.py:24
  15.5 5.9 %collective-permute-start.6 = (bf16[48,2176]{1,0:T(8,128)(2,1)S(1)}, bf16[48,2176]{1,0:T(8,128)(2,1)S(1)}, u32[]{:S(2)}, u32[]{:S(2)}) collective-permute-start(bf16[48,2176]{1,0:T(8,128)(2,1)S(1)} %join.2.refs_3_), channel_id=1, source_target_pairs={{0,2},{1,3},{2,0},{3,1},{4,6},{5,7},{6,4},{7,5},{8,10},{9,11},{10,... | collective-permute-start | bytes 626696 | tf_op jit(solution)/shard_map/ppermute | solution.py:24
  16.1 6.8 %collective-permute-start.5 = (bf16[48,2176]{1,0:T(8,128)(2,1)S(1)}, bf16[48,2176]{1,0:T(8,128)(2,1)S(1)}, u32[]{:S(2)}, u32[]{:S(2)}) collective-permute-start(bf16[48,2176]{1,0:T(8,128)(2,1)S(1)} %join.3.refs_1_), channel_id=1, source_target_pairs={{0,1},{1,0},{2,3},{3,2},{4,5},{5,4},{6,7},{7,6},{8,9},{9,8},{10,11... | collective-permute-start | bytes 626696 | tf_op jit(solution)/shard_map/ppermute | solution.py:24
  21.4 2.4 %collective-permute-start.8 = (bf16[48,2176]{1,0:T(8,128)(2,1)S(1)}, bf16[48,2176]{1,0:T(8,128)(2,1)S(1)}, u32[]{:S(2)}, u32[]{:S(2)}) collective-permute-start(bf16[48,2176]{1,0:T(8,128)(2,1)S(1)} %tie.1.refs_5_), channel_id=1, source_target_pairs={{0,1},{1,0},{2,3},{3,2},{4,5},{5,4},{6,7},{7,6},{8,9},{9,8},{10,11... | collective-permute-start | bytes 626696 | tf_op jit(solution)/shard_map/ppermute | solution.py:24
  21.4 1.6 %collective-permute-start.4 = (bf16[16,2176]{1,0:T(8,128)(2,1)S(1)}, bf16[16,2176]{1,0:T(8,128)(2,1)S(1)}, u32[]{:S(2)}, u32[]{:S(2)}) collective-permute-start(bf16[16,2176]{1,0:T(8,128)(2,1)S(1)} %get-tuple-element.28.refs_0_), channel_id=1, source_target_pairs={{0,1},{1,0},{2,3},{3,2},{4,5},{5,4},{6,7},{7,6},{8,9},{9,8},{10,11... | collective-permute-start | bytes 208904 | tf_op jit(solution)/shard_map/ppermute | solution.py:24
  21.9 1.8 %collective-permute-start.7 = (bf16[16,2176]{1,0:T(8,128)(2,1)S(1)}, bf16[16,2176]{1,0:T(8,128)(2,1)S(1)}, u32[]{:S(2)}, u32[]{:S(2)}) collective-permute-start(bf16[16,2176]{1,0:T(8,128)(2,1)S(1)} %collective-permute-done.3.refs_4_), channel_id=1, source_target_pairs={{0,1},{1,0},{2,3},{3,2},{4,5},{5,4},{6,7},{7,6},{8,9},{9,8},{10,11... | collective-permute-start | bytes 208904 | tf_op jit(solution)/shard_map/ppermute | solution.py:24
  24.5 1.5 %collective-permute-start.10 = (bf16[64,1792]{1,0:T(8,128)(2,1)S(1)}, bf16[64,1792]{1,0:T(8,128)(2,1)S(1)}, u32[]{:S(2)}, u32[]{:S(2)}) collective-permute-start(bf16[64,1792]{1,0:T(8,128)(2,1)S(1)} %get-tuple-element.40), channel_id=1, source_target_pairs={{0,1},{1,0},{2,3},{3,2},{4,5},{5,4},{6,7},{7,6},{8,9},{9,8},{10,11... | collective-permute-start | bytes 688136 | tf_op jit(solution)/shard_map/ppermute | solution.py:24
  25.0 3.1 %collective-permute-start.9 = (bf16[64,1792]{1,0:T(8,128)(2,1)S(1)}, bf16[64,1792]{1,0:T(8,128)(2,1)S(1)}, u32[]{:S(2)}, u32[]{:S(2)}) collective-permute-start(bf16[64,1792]{1,0:T(8,128)(2,1)S(1)} %down.3), channel_id=1, source_target_pairs={{0,1},{1,0},{2,3},{3,2},{4,5},{5,4},{6,7},{7,6},{8,9},{9,8},{10,11... | collective-permute-start | bytes 688136 | tf_op jit(solution)/shard_map/ppermute | solution.py:24
  26.1 6.1 %collective-permute-start.13 = (bf16[32,1792]{1,0:T(8,128)(2,1)S(1)}, bf16[32,1792]{1,0:T(8,128)(2,1)S(1)}, u32[]{:S(2)}, u32[]{:S(2)}) collective-permute-start(bf16[32,1792]{1,0:T(8,128)(2,1)S(1)} %get-tuple-element.45), channel_id=1, source_target_pairs={{0,2},{1,3},{2,0},{3,1},{4,6},{5,7},{6,4},{7,5},{8,10},{9,11},{10,... | collective-permute-start | bytes 344072 | tf_op jit(solution)/shard_map/ppermute | solution.py:24
  26.7 7.8 %collective-permute-start.11 = (bf16[32,1792]{1,0:T(8,128)(2,1)S(1)}, bf16[32,1792]{1,0:T(8,128)(2,1)S(1)}, u32[]{:S(2)}, u32[]{:S(2)}) collective-permute-start(bf16[32,1792]{1,0:T(8,128)(2,1)S(1)} %get-tuple-element.41), channel_id=1, source_target_pairs={{0,2},{1,3},{2,0},{3,1},{4,6},{5,7},{6,4},{7,5},{8,10},{9,11},{10,... | collective-permute-start | bytes 344072 | tf_op jit(solution)/shard_map/ppermute | solution.py:24
  32.2 5.7 %collective-permute-start.14 = (bf16[16,1792]{1,0:T(8,128)(2,1)S(1)}, bf16[16,1792]{1,0:T(8,128)(2,1)S(1)}, u32[]{:S(2)}, u32[]{:S(2)}) collective-permute-start(bf16[16,1792]{1,0:T(8,128)(2,1)S(1)} %get-tuple-element.46), channel_id=1, source_target_pairs={{0,8},{4,12},{8,0},{12,4},{1,9},{5,13},{9,1},{13,5},{2,10},{6,14},... | collective-permute-start | bytes 172040 | tf_op jit(solution)/shard_map/ppermute | solution.py:24
  33.8 6.0 %collective-permute-start.15 = (bf16[16,1792]{1,0:T(8,128)(2,1)S(1)}, bf16[16,1792]{1,0:T(8,128)(2,1)S(1)}, u32[]{:S(2)}, u32[]{:S(2)}) collective-permute-start(bf16[16,1792]{1,0:T(8,128)(2,1)S(1)} %get-tuple-element.47), channel_id=1, source_target_pairs={{0,12},{4,8},{8,4},{12,0},{1,13},{5,9},{9,5},{13,1},{2,14},{6,10},... | collective-permute-start | bytes 172040 | tf_op jit(solution)/shard_map/ppermute | solution.py:24
  34.5 5.3 %collective-permute-start.12 = (bf16[16,1792]{1,0:T(8,128)(2,1)S(1)}, bf16[16,1792]{1,0:T(8,128)(2,1)S(1)}, u32[]{:S(2)}, u32[]{:S(2)}) collective-permute-start(bf16[16,1792]{1,0:T(8,128)(2,1)S(1)} %get-tuple-element.43), channel_id=1, source_target_pairs={{0,4},{4,0},{8,12},{12,8},{1,5},{5,1},{9,13},{13,9},{2,6},{6,2},{1... | collective-permute-start | bytes 172040 | tf_op jit(solution)/shard_map/ppermute | solution.py:24

commit v4 on v3

--- a/solution.py
+++ b/solution.py
@@ -22,6 +22,16 @@
 def swap(value, axis, mask):
     count = lax.axis_size(axis)
     return lax.ppermute(value, axis, [(i, i ^ mask) for i in range(count)])
+
+
+def swap_both(value, ep_mask, pd_mask):
+    ep_count, pd_count = lax.axis_size("ep"), lax.axis_size("pd")
+    pairs = [
+        (i * pd_count + j, (i ^ ep_mask) * pd_count + (j ^ pd_mask))
+        for i in range(ep_count)
+        for j in range(pd_count)
+    ]
+    return lax.ppermute(value, ("ep", "pd"), pairs)
 
 
 def in_hbm(value):
@@ -108,10 +118,8 @@
     )(*map(in_hbm, sources))
 
 
-def gates_kernel(ep_count, cuts, ids_ref, gates_ref, *refs):
-    mark_ref = refs[-2]
-    copies = start_copies(cuts, refs)
-    ids, gates, own = ids_ref[...], gates_ref[...], lax.axis_index("ep")
+def gate_table(ids, gates, ep_count):
+    own = lax.axis_index("ep")
     chosen = slots_of(ids, own, ep_count)
     table = []
     for d in range(ep_count):
@@ -120,68 +128,44 @@
         table.append(jnp.where(chosen[d], gate, 0.0))
     table = jnp.concatenate(table, axis=0)
     high = table.astype(bf16).astype(f32)
-    mark_ref[...] = jnp.concatenate([high, table - high], axis=0).T.astype(bf16)
-    for copy in copies:
-        copy.wait()
-
-
-def start_copies(cuts, refs):
-    count, sems = (len(refs) - 2) // 2, refs[-1]
-    copies = []
+    return jnp.concatenate([high, table - high], axis=0).T.astype(bf16)
+
+
+def fetch_kernel(ep_count, count, skip, *refs):
+    sources, outs, sems = refs[:count], refs[skip:-1], refs[-1]
+    cuts, copies = sems.shape[1], []
     for i in range(count):
-        rows = refs[i].shape[0] // cuts
+        rows = sources[i].shape[0] // cuts
         for c in range(cuts):
             at = pl.ds(c * rows, rows)
             copies.append(
-                pltpu.make_async_copy(refs[i].at[at], refs[count + i].at[at], sems.at[i, c])
+                pltpu.make_async_copy(sources[i].at[at], outs[i].at[at], sems.at[i, c])
             )
     for copy in copies:
         copy.start()
-    return copies
-
-
-def fetch(arrays, ids, gates, ep_count):
-    cuts = 4
-    mark = jax.ShapeDtypeStruct((ids.shape[1], 2 * ep_count * CAP), bf16)
-    outs = pl.pallas_call(
-        functools.partial(gates_kernel, ep_count, cuts),
-        out_shape=[pltpu.VMEM(a.shape, a.dtype) for a in arrays] + [mark],
-        in_specs=[VMEM] * 2 + [HBM] * len(arrays),
-        out_specs=[VMEM] * (len(arrays) + 1),
-        scratch_shapes=[pltpu.SemaphoreType.DMA((len(arrays), cuts))],
-        compiler_params=params([mark] * 4),
+    if len(outs) > count:
+        ids_ref, gates_ref = refs[count : count + 2]
+        outs[-1][...] = gate_table(ids_ref[...], gates_ref[...], ep_count)
+    for copy in copies:
+        copy.wait()
+
+
+def fetch(arrays, after=(), routing=(), ep_count=0):
+    operands = [in_hbm(a) for a in [*arrays, *routing]]
+    out_shape = [pltpu.VMEM(a.shape, a.dtype) for a in arrays]
+    table = []
+    if routing:
+        table = [jax.ShapeDtypeStruct((routing[0].shape[1], 2 * ep_count * CAP), bf16)]
+    return pl.pallas_call(
+        functools.partial(fetch_kernel, ep_count, len(arrays), len(operands) + len(after)),
+        out_shape=out_shape + table,
+        in_specs=[HBM] * len(arrays) + [VMEM] * len(routing) + [ANY] * len(after),
+        out_specs=[VMEM] * len(out_shape + table),
+        scratch_shapes=[pltpu.SemaphoreType.DMA((len(arrays), 4))],
+        compiler_params=params(table * 4, 1 << 20),
         cost_estimate=cost(0, 0),
         name="fetch",
-    )(*map(in_hbm, [ids, gates, *arrays]))
-    return outs[:-1], outs[-1]
-
-
-def fetch_part_kernel(part, parts, source_ref, *refs):
-    out_ref, sems = refs[-2:]
-    rows = source_ref.shape[0] // parts // 2
-    copies = []
-    for c in range(2):
-        at = pl.ds(part * 2 * rows + c * rows, rows)
-        copies.append(pltpu.make_async_copy(source_ref.at[at], out_ref.at[at], sems.at[c]))
-    for copy in copies:
-        copy.start()
-    for copy in copies:
-        copy.wait()
-
-
-def fetch_part(array, part, parts, after, held=None):
-    extra = () if held is None else (held,)
-    return pl.pallas_call(
-        functools.partial(fetch_part_kernel, part, parts),
-        out_shape=pltpu.VMEM(array.shape, array.dtype),
-        in_specs=[HBM] + [VMEM] * len(extra) + [ANY] * len(after),
-        out_specs=VMEM,
-        input_output_aliases={1: 0} if extra else {},
-        scratch_shapes=[pltpu.SemaphoreType.DMA((2,))],
-        compiler_params=pltpu.CompilerParams(vmem_limit_bytes=1 << 20),
-        cost_estimate=cost(0, 0),
-        name="fetch_part",
-    )(in_hbm(array), *extra, *after)
+    )(*operands, *after)
 
 
 def join_kernel(count, *refs):
@@ -222,24 +206,21 @@
     )(value, *after)
 
 
-def total_kernel(kept_ref, arrived_ref, *outs):
-    at = 0
-    for out in outs:
+def total_kernel(cuts, kept_ref, arrived_ref, *outs):
+    for out, at in zip(outs, cuts):
         rows = pl.ds(at, out.shape[0])
-        out[...] = (kept_ref[rows, :] + arrived_ref[rows, :].astype(f32)).astype(out.dtype)
-        at += out.shape[0]
-
-
-def total(kept, arrived, count, dtype=bf16):
-    rows, columns = kept.shape
-    out_shape = [jax.ShapeDtypeStruct((rows // count, columns), dtype)] * count
-    return pl.pallas_call(
-        total_kernel,
+        out[...] = (kept_ref[rows, :].astype(f32) + arrived_ref[rows, :].astype(f32)).astype(out.dtype)
+
+
+def total(kept, arrived, pieces):
+    out_shape = [jax.ShapeDtypeStruct((rows, kept.shape[1]), dtype) for _, rows, dtype in pieces]
+    return pl.pallas_call(
+        functools.partial(total_kernel, [at for at, _, _ in pieces]),
         out_shape=out_shape,
         in_specs=[VMEM, VMEM],
-        out_specs=[VMEM] * count,
+        out_specs=[VMEM] * len(out_shape),
         compiler_params=params([kept] * 4, 1 << 20),
-        cost_estimate=cost(kept.size, 8 * kept.size),
+        cost_estimate=cost(0, 0),
         name="total",
     )(kept, arrived)
 
@@ -276,7 +257,7 @@
         in_specs=[VMEM] * (2 + len(before) + len(operands)),
         out_specs=[VMEM, VMEM],
         compiler_params=params(operands * 2),
-        cost_estimate=cost(4 * rows * w_gate.size, 4 * w_gate.size),
+        cost_estimate=cost(0, 0),
         name="gate_up",
     )(w_gate, w_up, *before, *operands)
 
@@ -304,7 +285,7 @@
         in_specs=[VMEM] * (5 + len(operands)),
         out_specs=[VMEM] * 2,
         compiler_params=params(operands * 2 + out_shape * 2),
-        cost_estimate=cost(6 * rows * w_gate.size, 4 * w_gate.size),
+        cost_estimate=cost(0, 0),
         name="hidden",
     )(w_gate, w_up, w_down, *sums, *operands)
 
@@ -368,9 +349,16 @@
     out_ref[...] = (summed / total).astype(bf16)
 
 
-def combine_kernel(cuts, table_ref, *refs):
+def combine_kernel(cuts, counts, table_ref, *refs):
     blocks, (out_ref, held_ref, sems) = refs[:-3], refs[-3:]
-    rows = jnp.concatenate([b[...] for b in blocks] * 2, axis=0)
+    rows, at = [], 0
+    for count in counts:
+        block = blocks[at][...]
+        if count == 2:
+            block = (block.astype(f32) + blocks[at + 1][...].astype(f32)).astype(bf16)
+        rows.append(block)
+        at += count
+    rows = jnp.concatenate(rows * 2, axis=0)
     table, width = table_ref[...], held_ref.shape[1] // cuts
     copies = []
     for c in range(cuts):
@@ -386,18 +374,19 @@
 
 
 def mix(table, blocks):
-    mixed = jax.ShapeDtypeStruct((table.shape[0], blocks[0].shape[1]), bf16)
+    operands = [part for block in blocks for part in block]
+    mixed = jax.ShapeDtypeStruct((table.shape[0], operands[0].shape[1]), bf16)
     cuts = 2 if mixed.shape[1] % 256 == 0 else 1
     return pl.pallas_call(
-        functools.partial(combine_kernel, cuts),
+        functools.partial(combine_kernel, cuts, [len(block) for block in blocks]),
         out_shape=mixed,
-        in_specs=[VMEM] * (1 + len(blocks)),
+        in_specs=[VMEM] * (1 + len(operands)),
         out_specs=HBM,
         scratch_shapes=[pltpu.VMEM(mixed.shape, bf16), pltpu.SemaphoreType.DMA((cuts,))],
-        compiler_params=params([mixed] * 4 + blocks * 2),
+        compiler_params=params([mixed] * 4 + operands * 2),
         cost_estimate=cost(4 * CAP * len(blocks) * mixed.size, 2 * mixed.size),
         name="combine",
-    )(table, *blocks)
+    )(table, *operands)
 
 
 def spread(pieces, m, bit):
@@ -424,22 +413,24 @@
     ep_count = lax.axis_size("ep")
     pd_count = lax.axis_size("pd")
     width = tokens.shape[1]
-    half = ep_count // 2
     ids = expert_ids.T
 
     blocks = route(ids, tokens, cache_rows, destination, ep_count)
+    bit = pd_count // 2
+    cut_in = cut_out = min(2, ep_count)
     arrived = [blocks[0]] + [swap(blocks[d], "ep", d) for d in range(1, ep_count)]
-    bit = pd_count // 2
-    over = swap(blocks[0], "pd", bit)
-    (w_gate, w_up), table = fetch([gate_weight[0], up_weight[0]], ids, gate_scores.T, ep_count)
-    rest = join(arrived[1:], [table, over])
-    pieces = {0: [blocks[0], rest]}
-    pieces[bit] = [over, swap(rest, "pd", bit)]
-    pieces[0][1] = join(arrived[1:], [rest])
-    w_down = fetch_part(down_weight[0], 0, 1, pieces[0])
+    over = [swap(blocks[0], "pd", bit)]
+    over += [swap_both(blocks[d], d, bit) for d in range(1, cut_in)]
+    w_gate, w_up, table = fetch([gate_weight[0], up_weight[0]], [], (ids, gate_scores.T), ep_count)
+    rest = join(arrived[cut_in:], [table])
+
+    pieces = {0: [join(arrived[:cut_in], [rest])], bit: [join(over, [rest])]}
+    pieces[bit] += [swap(tie(rest, pieces[0] + pieces[bit]), "pd", bit)]
+    pieces[0] += [join(arrived[cut_in:], pieces[0])]
+    (w_down,) = fetch([down_weight[0]], pieces[0])
     spread(pieces, 0, bit // 2)
     sums = gate_up([0], width, w_gate, w_up, pieces)
-    pieces[bit][1] = tie(pieces[bit][1], [sums[0], w_down])
+    pieces[bit][-1] = tie(pieces[bit][-1], [sums[0], w_down])
     spread(pieces, bit, bit // 2)
     sums = gate_up(list(range(1, bit + 1)), width, w_gate, w_up, pieces, before=sums)
     late = list(range(bit + 1, pd_count))
@@ -451,11 +442,19 @@
     parts = {others[0]: part}
     parts.update(zip(others[1:], down(others[1:], width, hidden, w_down, bf16)))
     kept = dict(zip(stay, down(stay, width, hidden, w_down, f32)))
-    cut = half * CAP
+    direct = range(1, cut_out)
+    shares = [(0, CAP)] + [(d * CAP, CAP) for d in direct]
+    if cut_out < ep_count:
+        shares += [(cut_out * CAP, (ep_count - cut_out) * CAP)]
     for m in stay:
-        sent = bf16 if m & 2 else f32
-        kept[m] = dict(zip((0, cut), total(kept[m], swap(parts[m ^ 1], "pd", 1), 2, sent)))
-
+        kinds = [bf16] * len(shares)
+        if not m & bit:
+            kinds[0] = kinds[-1] = f32
+        kept[m] = total(
+            kept[m],
+            swap(parts[m ^ 1], "pd", 1),
+            [(at, rows, kind) for (at, rows), kind in zip(shares, kinds)],
+        )
     operands = [g for m in range(pd_count) for g in pieces[m]]
     queries = decode_query.reshape(-1, decode_query.shape[3])
     attended = jax.ShapeDtypeStruct((queries.shape[0], LATC), bf16)
@@ -469,22 +468,17 @@
         name="attend",
     )(*map(in_hbm, [destination, lengths, queries]), *operands)
 
-    returned = [None] * ep_count
-    for low in (cut, 0):
-        rows = {m: kept[m][low] for m in stay}
-        bit = 2
-        while bit < pd_count:
-            last = bit * 2 == pd_count
-            for m in sorted(rows, reverse=True):
-                if m & bit:
-                    sent = rows.pop(m).astype(bf16)
-                    over = swap(sent, "pd", bit)
-                    rows[m ^ bit] = total(rows[m ^ bit], over, half if last else 1, bf16 if last else f32)
-                    rows[m ^ bit] = rows[m ^ bit] if last else rows[m ^ bit][0]
-            bit *= 2
-        for i, block in enumerate(rows[0]):
-            d = low // CAP + i
-            returned[d] = swap(block, "ep", d) if d else block
+    staged = []
+    if cut_out < ep_count:
+        staged = total(
+            kept[0][-1],
+            swap(kept[bit][-1], "pd", bit),
+            [(d * CAP, CAP, bf16) for d in range(ep_count - cut_out)],
+        )
+    returned = [[total(kept[0][0], swap(kept[bit][0], "pd", bit), [(0, CAP, bf16)])[0]]]
+    for d in direct:
+        returned += [[swap(kept[0][d], "ep", d), swap_both(kept[bit][d], d, bit)]]
+    returned += [[swap(block, "ep", cut_out + i)] for i, block in enumerate(staged)]
     mixed = mix(table, returned)
     return (mixed, attended.reshape(decode_query.shape[:3] + (LATC,)))
 

time: 41.3 us -> 40.3 us (0.976)
  waiting for transfers between devices: 11.8 us -> 5.71 us
  starting transfers between devices: 14.9 us -> 20 us
    ppermute x16, waiting for transfers between devices: 11.8 us -> 5.53 us  [swap(): return lax.ppermute(value, axis, [(i, i ^ mask) for i in range(count)])]
    ppermute x0 -> x2, starting transfers between devices: none -> 2.82 us  [swap_both(): return lax.ppermute(value, ('ep', 'pd'), pairs)]
    ppermute x16, starting transfers between devices: 14.9 us -> 17.2 us  [swap(): return lax.ppermute(value, axis, [(i, i ^ mask) for i in range(count)])]
  transfers between devices with their start and end apart: 16 -> 18, of which waited for: 8 -> 7; matrix products, arithmetic and copies ran while one was open for 0% -> 0% of each run, Pallas kernels for 24% -> 25%
where the time goes in v4:
time: 40.3 us; the launch traced here: 40 us
  starting transfers between devices  20 us (50%)
  Pallas kernels  13.5 us (33%)
  waiting for transfers between devices  5.71 us (14%)
  between operations  0.79 us (2%)
    ppermute x16, starting transfers between devices, swap(): return lax.ppermute(value, axis, [(i, i ^ mask) for i in range(count)])  17.2 us
    pallas_call x2, Pallas kernels, fetch(): pl.pallas_call(functools.partial(fetch_kernel, ep_count, len(arrays), len...  5.93 us
    ppermute x16, waiting for transfers between devices, swap(): return lax.ppermute(value, axis, [(i, i ^ mask) for i in range(count)])  5.53 us
    ppermute x2, starting transfers between devices, swap_both(): return lax.ppermute(value, ('ep', 'pd'), pairs)  2.82 us
    pallas_call x1, Pallas kernels, on_device(): pl.pallas_call(functools.partial(attend_kernel, ep_count, pd_count, width...  1.96 us
    pallas_call x1, Pallas kernels, route(): pl.pallas_call(functools.partial(route_kernel, ep_count), out_shape=out_s...  1.56 us
    pallas_call x1, Pallas kernels, mix(): pl.pallas_call(functools.partial(combine_kernel, cuts, [len(block) for bl...  1.23 us
    pallas_call x2, Pallas kernels, gate_up(): pl.pallas_call(functools.partial(gate_up_kernel, masks, width, bool(befor...  1.21 us
  transfers between devices with their start and end apart: 18, of which 7 were waited for; matrix products, arithmetic and copies ran while one was open for 0% of the time, Pallas kernels for 25%

profile of v4, /device:TPU:0, one launch (start us, length us, event | category | flops | bytes accessed | tf_op | source)
XLA Modules:
  0.0 40.0 jit_solution(10899792064489120169)
XLA Ops:
  0.6 1.6 %route.1 = (bf16[16,2176]{1,0:T(8,128)(2,1)S(1)}, bf16[16,2176]{1,0:T(8,128)(2,1)S(1)}, bf16[16,2176]{1,0:T(8,128)(2,1)S(1)}, bf16[16,2176]{1,0:T(8,128)(2,1)S(1)}) custom-call(s32[8,256]{1,0:T(8,128)} %bitcast.12, s32[4,4]{1,0:T(4,128)} %dest_ref.1, bf16[4,8,576]{2,1,0:T(8,128)(2,1)} %refs_2_.1, bf16[256,1792]{1,0:T(8,128)(2,1)} %refs_3_.1), custom_call_target="tpu_custom_call" | custom-call | flops 117440512 | bytes 917504 | tf_op jit(solution)/shard_map/route/pallas_call | solution.py:108
  2.2 4.1 %collective-permute-start.1 = (bf16[16,2176]{1,0:T(8,128)(2,1)S(1)}, bf16[16,2176]{1,0:T(8,128)(2,1)S(1)}, u32[]{:S(2)}, u32[]{:S(2)}) collective-permute-start(bf16[16,2176]{1,0:T(8,128)(2,1)S(1)} %get-tuple-element.30), channel_id=1, source_target_pairs={{0,8},{4,12},{8,0},{12,4},{1,9},{5,13},{9,1},{13,5},{2,10},{6,14},... | collective-permute-start | bytes 208904 | tf_op jit(solution)/shard_map/ppermute | solution.py:24
  6.3 1.3 %collective-permute-start.2 = (bf16[16,2176]{1,0:T(8,128)(2,1)S(1)}, bf16[16,2176]{1,0:T(8,128)(2,1)S(1)}, u32[]{:S(2)}, u32[]{:S(2)}) collective-permute-start(bf16[16,2176]{1,0:T(8,128)(2,1)S(1)} %get-tuple-element.31), channel_id=1, source_target_pairs={{0,12},{4,8},{8,4},{12,0},{1,13},{5,9},{9,5},{13,1},{2,14},{6,10},... | collective-permute-start | bytes 208904 | tf_op jit(solution)/shard_map/ppermute | solution.py:24
  7.6 0.2 collective-permute-start
  7.9 1.5 %collective-permute-start.5 = (bf16[16,2176]{1,0:T(8,128)(2,1)S(1)}, bf16[16,2176]{1,0:T(8,128)(2,1)S(1)}, u32[]{:S(2)}, u32[]{:S(2)}) collective-permute-start(bf16[16,2176]{1,0:T(8,128)(2,1)S(1)} %get-tuple-element.28.refs_0_), channel_id=1, source_target_pairs={{0,2},{1,3},{2,0},{3,1},{4,6},{5,7},{6,4},{7,5},{8,10},{9,11},{10,... | collective-permute-start | bytes 208904 | tf_op jit(solution)/shard_map/ppermute | solution.py:24
  9.4 1.8 %collective-permute-start.6 = (bf16[16,2176]{1,0:T(8,128)(2,1)S(1)}, bf16[16,2176]{1,0:T(8,128)(2,1)S(1)}, u32[]{:S(2)}, u32[]{:S(2)}) collective-permute-start(bf16[16,2176]{1,0:T(8,128)(2,1)S(1)} %get-tuple-element.29), channel_id=1, source_target_pairs={{0,6},{1,7},{2,4},{3,5},{4,2},{5,3},{6,0},{7,1},{8,14},{9,15},{10,... | collective-permute-start | bytes 208904 | tf_op jit(solution)/shard_map/ppermute | solution.py:34
  11.1 3.9 %fetch.2 = (bf16[7168,256]{1,0:T(8,128)(2,1)S(1)}, bf16[7168,256]{1,0:T(8,128)(2,1)S(1)}, bf16[256,128]{1,0:T(8,128)(2,1)S(1)}) custom-call(bf16[7168,256]{1,0:T(8,128)(2,1)} %bitcast.7, bf16[7168,256]{1,0:T(8,128)(2,1)} %bitcast.8, s32[8,256]{1,0:T(8,128)} %bitcast.13, f32[8,256]{1,0:T(8,128)} %bitcast.14), custom_call_target="tpu_custom_call" | custom-call | tf_op jit(solution)/shard_map/fetch/pallas_call | solution.py:159
  15.0 0.0 collective-permute-done.1.refs_0_
  15.0 0.0 collective-permute-done.2.refs_1_
  15.1 0.0 collective-permute-done.refs_1_
  15.1 0.0 collective-permute-done.5.refs_0_
  15.1 0.2 collective-permute-done.6.refs_1_
  15.3 1.4 %collective-permute-start.7 = (bf16[32,2176]{1,0:T(8,128)(2,1)S(1)}, bf16[32,2176]{1,0:T(8,128)(2,1)S(1)}, u32[]{:S(2)}, u32[]{:S(2)}) collective-permute-start(bf16[32,2176]{1,0:T(8,128)(2,1)S(1)} %tie.2), channel_id=1, source_target_pairs={{0,2},{1,3},{2,0},{3,1},{4,6},{5,7},{6,4},{7,5},{8,10},{9,11},{10,... | collective-permute-start | bytes 417800 | tf_op jit(solution)/shard_map/ppermute | solution.py:24
  16.7 0.0 collective-permute-start.3
  16.7 0.5 %collective-permute-start.8 = (bf16[32,2176]{1,0:T(8,128)(2,1)S(1)}, bf16[32,2176]{1,0:T(8,128)(2,1)S(1)}, u32[]{:S(2)}, u32[]{:S(2)}) collective-permute-start(bf16[32,2176]{1,0:T(8,128)(2,1)S(1)} %join.7.refs_2_.refs_4_), channel_id=1, source_target_pairs={{0,1},{1,0},{2,3},{3,2},{4,5},{5,4},{6,7},{7,6},{8,9},{9,8},{10,11... | collective-permute-start | bytes 417800 | tf_op jit(solution)/shard_map/ppermute | solution.py:24
  17.2 0.1 collective-permute-start.4
  17.3 2.0 %fetch.3.refs_2_.down_ref = bf16[256,7168]{1,0:T(8,128)(2,1)S(1)} custom-call(bf16[256,7168]{1,0:T(8,128)(2,1)} %bitcast.9, bf16[32,2176]{1,0:T(8,128)(2,1)S(1)} %join.5.refs_2_.refs_1_.refs_0_, bf16[32,2176]{1,0:T(8,128)(2,1)S(1)} %join.6.refs_2_.refs_1_), custom_call_target="tpu_custom_call" | custom-call | tf_op jit(solution)/shard_map/fetch/pallas_call | solution.py:159
  19.4 0.4 %gate_up.2 = (f32[64,256]{1,0:T(8,128)S(1)}, f32[64,256]{1,0:T(8,128)S(1)}) custom-call(bf16[7168,256]{1,0:T(8,128)(2,1)S(1)} %get-tuple-element.26.gate_ref, bf16[7168,256]{1,0:T(8,128)(2,1)S(1)} %get-tuple-element.27.up_ref, bf16[32,2176]{1,0:T(8,128)(2,1)S(1)} %join.5.refs_2_.refs_1_.refs_0_, bf16[32,2176]{1,0:T(8,128)(2,1)S(1)} %join.6.refs_2_.refs_1_), custom_call_target="tpu_custom_call" | custom-call | tf_op jit(solution)/shard_map/gate_up/pallas_call | solution.py:254
  19.8 0.6 %collective-permute-done.7.refs_0_ = bf16[32,2176]{1,0:T(8,128)(2,1)S(1)} collective-permute-done((bf16[32,2176]{1,0:T(8,128)(2,1)S(1)}, bf16[32,2176]{1,0:T(8,128)(2,1)S(1)}, u32[]{:S(2)}, u32[]{:S(2)}) %collective-permute-start.7) | collective-permute-done | bytes 139296 | tf_op jit(solution)/shard_map/ppermute | solution.py:24
  20.4 0.0 collective-permute-start.9
  20.4 0.0 collective-permute-done.4.refs_3_
  20.4 0.0 collective-permute-done.3.refs_2_
  20.4 0.8 %gate_up.3 = (f32[64,256]{1,0:T(8,128)S(1)}, f32[64,256]{1,0:T(8,128)S(1)}) custom-call(bf16[7168,256]{1,0:T(8,128)(2,1)S(1)} %get-tuple-element.26.gate_ref, bf16[7168,256]{1,0:T(8,128)(2,1)S(1)} %get-tuple-element.27.up_ref, f32[64,256]{1,0:T(8,128)S(1)} %get-tuple-element.32.refs_1_.refs_0_, f32[64,256]{1,0:T(8,128)S(1)} %get-tuple-element.33.refs_1_, ...), custom_call_target="tpu_custom_call" | custom-call | tf_op jit(solution)/shard_map/gate_up/pallas_call | solution.py:254
  21.2 0.0 collective-permute-done.8.refs_2_.refs_6_
  21.2 0.6 %collective-permute-done.9.refs_3_.refs_7_ = bf16[32,2176]{1,0:T(8,128)(2,1)S(1)} collective-permute-done((bf16[32,2176]{1,0:T(8,128)(2,1)S(1)}, bf16[32,2176]{1,0:T(8,128)(2,1)S(1)}, u32[]{:S(2)}, u32[]{:S(2)}) %collective-permute-start.9) | collective-permute-done | bytes 139296 | tf_op jit(solution)/shard_map/ppermute | solution.py:24
  21.8 0.7 %hidden.1 = (bf16[64,256]{1,0:T(8,128)(2,1)S(1)}, bf16[64,1792]{1,0:T(8,128)(2,1)S(1)}) custom-call(bf16[7168,256]{1,0:T(8,128)(2,1)S(1)} %get-tuple-element.26.gate_ref, bf16[7168,256]{1,0:T(8,128)(2,1)S(1)} %get-tuple-element.27.up_ref, bf16[256,7168]{1,0:T(8,128)(2,1)S(1)} %fetch.3.refs_2_.down_ref, f32[64,256]{1,0:T(8,128)S(1)} %get-tuple-element.34.refs_0_, ...), custom_call_target="tpu_custom_call" | custom-call | tf_op jit(solution)/shard_map/hidden/pallas_call | solution.py:282
  22.5 0.2 collective-permute-start.11
  22.7 0.3 down.3
  23.0 0.4 %collective-permute-start.10 = (bf16[64,1792]{1,0:T(8,128)(2,1)S(1)}, bf16[64,1792]{1,0:T(8,128)(2,1)S(1)}, u32[]{:S(2)}, u32[]{:S(2)}) collective-permute-start(bf16[64,1792]{1,0:T(8,128)(2,1)S(1)} %down.3), channel_id=1, source_target_pairs={{0,1},{1,0},{2,3},{3,2},{4,5},{5,4},{6,7},{7,6},{8,9},{9,8},{10,11... | collective-permute-start | bytes 688136 | tf_op jit(solution)/shard_map/ppermute | solution.py:24
  23.4 0.5 %down.2 = (f32[64,1792]{1,0:T(8,128)S(1)}, f32[64,1792]{1,0:T(8,128)S(1)}) custom-call(bf16[64,256]{1,0:T(8,128)(2,1)S(1)} %get-tuple-element.36.hidden_ref, bf16[256,7168]{1,0:T(8,128)(2,1)S(1)} %fetch.3.refs_2_.down_ref), custom_call_target="tpu_custom_call" | custom-call | flops 234881024 | bytes 3670016 | tf_op jit(solution)/shard_map/down/pallas_call | solution.py:303
  23.9 0.2 collective-permute-done.11.arrived_ref
  24.1 1.4 %collective-permute-start.15 = (bf16[32,1792]{1,0:T(8,128)(2,1)S(1)}, bf16[32,1792]{1,0:T(8,128)(2,1)S(1)}, u32[]{:S(2)}, u32[]{:S(2)}) collective-permute-start(bf16[32,1792]{1,0:T(8,128)(2,1)S(1)} %get-tuple-element.45), channel_id=1, source_target_pairs={{0,2},{1,3},{2,0},{3,1},{4,6},{5,7},{6,4},{7,5},{8,10},{9,11},{10,... | collective-permute-start | bytes 344072 | tf_op jit(solution)/shard_map/ppermute | solution.py:24
  25.5 0.7 %collective-permute-start.12 = (bf16[16,1792]{1,0:T(8,128)(2,1)S(1)}, bf16[16,1792]{1,0:T(8,128)(2,1)S(1)}, u32[]{:S(2)}, u32[]{:S(2)}) collective-permute-start(bf16[16,1792]{1,0:T(8,128)(2,1)S(1)} %get-tuple-element.41), channel_id=1, source_target_pairs={{0,2},{1,3},{2,0},{3,1},{4,6},{5,7},{6,4},{7,5},{8,10},{9,11},{10,... | collective-permute-start | bytes 172040 | tf_op jit(solution)/shard_map/ppermute | solution.py:24
  26.2 1.1 %collective-permute-start.14 = (bf16[16,1792]{1,0:T(8,128)(2,1)S(1)}, bf16[16,1792]{1,0:T(8,128)(2,1)S(1)}, u32[]{:S(2)}, u32[]{:S(2)}) collective-permute-start(bf16[16,1792]{1,0:T(8,128)(2,1)S(1)} %get-tuple-element.43), channel_id=1, source_target_pairs={{0,6},{1,7},{2,4},{3,5},{4,2},{5,3},{6,0},{7,1},{8,14},{9,15},{10,... | collective-permute-start | bytes 172040 | tf_op jit(solution)/shard_map/ppermute | solution.py:34
  27.2 0.0 collective-permute-done.10.arrived_ref
  27.3 1.8 %collective-permute-start.13 = (bf16[16,1792]{1,0:T(8,128)(2,1)S(1)}, bf16[16,1792]{1,0:T(8,128)(2,1)S(1)}, u32[]{:S(2)}, u32[]{:S(2)}) collective-permute-start(bf16[16,1792]{1,0:T(8,128)(2,1)S(1)} %get-tuple-element.42), channel_id=1, source_target_pairs={{0,4},{4,0},{8,12},{12,8},{1,5},{5,1},{9,13},{13,9},{2,6},{6,2},{1... | collective-permute-start | bytes 172040 | tf_op jit(solution)/shard_map/ppermute | solution.py:24
  29.1 1.5 %collective-permute-done.15.arrived_ref = bf16[32,1792]{1,0:T(8,128)(2,1)S(1)} collective-permute-done((bf16[32,1792]{1,0:T(8,128)(2,1)S(1)}, bf16[32,1792]{1,0:T(8,128)(2,1)S(1)}, u32[]{:S(2)}, u32[]{:S(2)}) %collective-permute-start.15) | collective-permute-done | bytes 114720 | tf_op jit(solution)/shard_map/ppermute | solution.py:24
  30.6 2.2 %collective-permute-start.16 = (bf16[16,1792]{1,0:T(8,128)(2,1)S(1)}, bf16[16,1792]{1,0:T(8,128)(2,1)S(1)}, u32[]{:S(2)}, u32[]{:S(2)}) collective-permute-start(bf16[16,1792]{1,0:T(8,128)(2,1)S(1)} %get-tuple-element.46), channel_id=1, source_target_pairs={{0,8},{4,12},{8,0},{12,4},{1,9},{5,13},{9,1},{13,5},{2,10},{6,14},... | collective-permute-start | bytes 172040 | tf_op jit(solution)/shard_map/ppermute | solution.py:24
  32.8 1.3 %collective-permute-start.17 = (bf16[16,1792]{1,0:T(8,128)(2,1)S(1)}, bf16[16,1792]{1,0:T(8,128)(2,1)S(1)}, u32[]{:S(2)}, u32[]{:S(2)}) collective-permute-start(bf16[16,1792]{1,0:T(8,128)(2,1)S(1)} %get-tuple-element.47), channel_id=1, source_target_pairs={{0,12},{4,8},{8,4},{12,0},{1,13},{5,9},{9,5},{13,1},{2,14},{6,10},... | collective-permute-start | bytes 172040 | tf_op jit(solution)/shard_map/ppermute | solution.py:24
  34.1 2.0 %attend.1 = bf16[64,512]{1,0:T(8,128)(2,1)} custom-call(s32[4,4]{1,0:T(4,128)} %dest_ref.1, s32[16]{0:T(128)} %len_ref.1, bf16[64,576]{1,0:T(8,128)(2,1)} %bitcast.10, bf16[32,2176]{1,0:T(8,128)(2,1)S(1)} %join.5.refs_2_.refs_1_.refs_0_, bf16[32,2176]{1,0:T(8,128)(2,1)S(1)} %join.6.refs_2_.refs_1_, bf16[32,2176]{1,0:T(8,128)(2,1)S(1)} %collective-permute-done.3.refs_2_, ...), custom_call_target="tpu_custom_call" | custom-call | flops 234881024 | bytes 3670016 | tf_op jit(solution)/shard_map/attend/pallas_call | solution.py:461
  36.1 0.0 collective-permute-done.12.arrived_ref
  36.1 0.0 collective-permute-done.14.refs_2_
  36.1 0.0 collective-permute-done.13.refs_1_
  36.1 0.7 %collective-permute-done.16.refs_3_ = bf16[16,1792]{1,0:T(8,128)(2,1)S(1)} collective-permute-done((bf16[16,1792]{1,0:T(8,128)(2,1)S(1)}, bf16[16,1792]{1,0:T(8,128)(2,1)S(1)}, u32[]{:S(2)}, u32[]{:S(2)}) %collective-permute-start.16) | collective-permute-done | bytes 57376 | tf_op jit(solution)/shard_map/ppermute | solution.py:24
  36.8 1.9 %collective-permute-done.17.refs_4_ = bf16[16,1792]{1,0:T(8,128)(2,1)S(1)} collective-permute-done((bf16[16,1792]{1,0:T(8,128)(2,1)S(1)}, bf16[16,1792]{1,0:T(8,128)(2,1)S(1)}, u32[]{:S(2)}, u32[]{:S(2)}) %collective-permute-start.17) | collective-permute-done | bytes 57376 | tf_op jit(solution)/shard_map/ppermute | solution.py:24
  38.7 1.2 %combine.1 = bf16[256,1792]{1,0:T(8,128)(2,1)} custom-call(bf16[256,128]{1,0:T(8,128)(2,1)S(1)} %get-tuple-element.25.refs_2_.table_ref, bf16[16,1792]{1,0:T(8,128)(2,1)S(1)} %total.6.refs_0_, bf16[16,1792]{1,0:T(8,128)(2,1)S(1)} %collective-permute-done.13.refs_1_, bf16[16,1792]{1,0:T(8,128)(2,1)S(1)} %collective-permute-done.14.refs_2_, ...), custom_call_target="tpu_custom_call" | custom-call | flops 117440512 | bytes 917504 | tf_op jit(solution)/shard_map/combine/pallas_call | solution.py:380
  (10 shorter events, 0.2 us)
Async XLA Ops:
  2.2 12.8 %collective-permute-start.1 = (bf16[16,2176]{1,0:T(8,128)(2,1)S(1)}, bf16[16,2176]{1,0:T(8,128)(2,1)S(1)}, u32[]{:S(2)}, u32[]{:S(2)}) collective-permute-start(bf16[16,2176]{1,0:T(8,128)(2,1)S(1)} %get-tuple-element.30), channel_id=1, source_target_pairs={{0,8},{4,12},{8,0},{12,4},{1,9},{5,13},{9,1},{13,5},{2,10},{6,14},... | collective-permute-start | bytes 208904 | tf_op jit(solution)/shard_map/ppermute | solution.py:24
  6.3 8.7 %collective-permute-start.2 = (bf16[16,2176]{1,0:T(8,128)(2,1)S(1)}, bf16[16,2176]{1,0:T(8,128)(2,1)S(1)}, u32[]{:S(2)}, u32[]{:S(2)}) collective-permute-start(bf16[16,2176]{1,0:T(8,128)(2,1)S(1)} %get-tuple-element.31), channel_id=1, source_target_pairs={{0,12},{4,8},{8,4},{12,0},{1,13},{5,9},{9,5},{13,1},{2,14},{6,10},... | collective-permute-start | bytes 208904 | tf_op jit(solution)/shard_map/ppermute | solution.py:24
  7.6 7.4 %collective-permute-start = (bf16[16,2176]{1,0:T(8,128)(2,1)S(1)}, bf16[16,2176]{1,0:T(8,128)(2,1)S(1)}, u32[]{:S(2)}, u32[]{:S(2)}) collective-permute-start(bf16[16,2176]{1,0:T(8,128)(2,1)S(1)} %get-tuple-element.29), channel_id=1, source_target_pairs={{0,4},{4,0},{8,12},{12,8},{1,5},{5,1},{9,13},{13,9},{2,6},{6,2},{1... | collective-permute-start | bytes 208904 | tf_op jit(solution)/shard_map/ppermute | solution.py:24
  7.9 7.2 %collective-permute-start.5 = (bf16[16,2176]{1,0:T(8,128)(2,1)S(1)}, bf16[16,2176]{1,0:T(8,128)(2,1)S(1)}, u32[]{:S(2)}, u32[]{:S(2)}) collective-permute-start(bf16[16,2176]{1,0:T(8,128)(2,1)S(1)} %get-tuple-element.28.refs_0_), channel_id=1, source_target_pairs={{0,2},{1,3},{2,0},{3,1},{4,6},{5,7},{6,4},{7,5},{8,10},{9,11},{10,... | collective-permute-start | bytes 208904 | tf_op jit(solution)/shard_map/ppermute | solution.py:24
  9.4 5.9 %collective-permute-start.6 = (bf16[16,2176]{1,0:T(8,128)(2,1)S(1)}, bf16[16,2176]{1,0:T(8,128)(2,1)S(1)}, u32[]{:S(2)}, u32[]{:S(2)}) collective-permute-start(bf16[16,2176]{1,0:T(8,128)(2,1)S(1)} %get-tuple-element.29), channel_id=1, source_target_pairs={{0,6},{1,7},{2,4},{3,5},{4,2},{5,3},{6,0},{7,1},{8,14},{9,15},{10,... | collective-permute-start | bytes 208904 | tf_op jit(solution)/shard_map/ppermute | solution.py:34
  15.3 5.1 %collective-permute-start.7 = (bf16[32,2176]{1,0:T(8,128)(2,1)S(1)}, bf16[32,2176]{1,0:T(8,128)(2,1)S(1)}, u32[]{:S(2)}, u32[]{:S(2)}) collective-permute-start(bf16[32,2176]{1,0:T(8,128)(2,1)S(1)} %tie.2), channel_id=1, source_target_pairs={{0,2},{1,3},{2,0},{3,1},{4,6},{5,7},{6,4},{7,5},{8,10},{9,11},{10,... | collective-permute-start | bytes 417800 | tf_op jit(solution)/shard_map/ppermute | solution.py:24
  16.7 3.7 %collective-permute-start.3 = (bf16[32,2176]{1,0:T(8,128)(2,1)S(1)}, bf16[32,2176]{1,0:T(8,128)(2,1)S(1)}, u32[]{:S(2)}, u32[]{:S(2)}) collective-permute-start(bf16[32,2176]{1,0:T(8,128)(2,1)S(1)} %join.5.refs_2_.refs_1_.refs_0_), channel_id=1, source_target_pairs={{0,1},{1,0},{2,3},{3,2},{4,5},{5,4},{6,7},{7,6},{8,9},{9,8},{10,11... | collective-permute-start | bytes 417800 | tf_op jit(solution)/shard_map/ppermute | solution.py:24
  16.7 4.5 %collective-permute-start.8 = (bf16[32,2176]{1,0:T(8,128)(2,1)S(1)}, bf16[32,2176]{1,0:T(8,128)(2,1)S(1)}, u32[]{:S(2)}, u32[]{:S(2)}) collective-permute-start(bf16[32,2176]{1,0:T(8,128)(2,1)S(1)} %join.7.refs_2_.refs_4_), channel_id=1, source_target_pairs={{0,1},{1,0},{2,3},{3,2},{4,5},{5,4},{6,7},{7,6},{8,9},{9,8},{10,11... | collective-permute-start | bytes 417800 | tf_op jit(solution)/shard_map/ppermute | solution.py:24
  17.2 3.2 %collective-permute-start.4 = (bf16[32,2176]{1,0:T(8,128)(2,1)S(1)}, bf16[32,2176]{1,0:T(8,128)(2,1)S(1)}, u32[]{:S(2)}, u32[]{:S(2)}) collective-permute-start(bf16[32,2176]{1,0:T(8,128)(2,1)S(1)} %join.6.refs_2_.refs_1_), channel_id=1, source_target_pairs={{0,1},{1,0},{2,3},{3,2},{4,5},{5,4},{6,7},{7,6},{8,9},{9,8},{10,11... | collective-permute-start | bytes 417800 | tf_op jit(solution)/shard_map/ppermute | solution.py:24
  20.4 1.4 %collective-permute-start.9 = (bf16[32,2176]{1,0:T(8,128)(2,1)S(1)}, bf16[32,2176]{1,0:T(8,128)(2,1)S(1)}, u32[]{:S(2)}, u32[]{:S(2)}) collective-permute-start(bf16[32,2176]{1,0:T(8,128)(2,1)S(1)} %tie.3.refs_5_), channel_id=1, source_target_pairs={{0,1},{1,0},{2,3},{3,2},{4,5},{5,4},{6,7},{7,6},{8,9},{9,8},{10,11... | collective-permute-start | bytes 417800 | tf_op jit(solution)/shard_map/ppermute | solution.py:24
  22.5 1.5 %collective-permute-start.11 = (bf16[64,1792]{1,0:T(8,128)(2,1)S(1)}, bf16[64,1792]{1,0:T(8,128)(2,1)S(1)}, u32[]{:S(2)}, u32[]{:S(2)}) collective-permute-start(bf16[64,1792]{1,0:T(8,128)(2,1)S(1)} %get-tuple-element.40), channel_id=1, source_target_pairs={{0,1},{1,0},{2,3},{3,2},{4,5},{5,4},{6,7},{7,6},{8,9},{9,8},{10,11... | collective-permute-start | bytes 688136 | tf_op jit(solution)/shard_map/ppermute | solution.py:24
  23.0 4.2 %collective-permute-start.10 = (bf16[64,1792]{1,0:T(8,128)(2,1)S(1)}, bf16[64,1792]{1,0:T(8,128)(2,1)S(1)}, u32[]{:S(2)}, u32[]{:S(2)}) collective-permute-start(bf16[64,1792]{1,0:T(8,128)(2,1)S(1)} %down.3), channel_id=1, source_target_pairs={{0,1},{1,0},{2,3},{3,2},{4,5},{5,4},{6,7},{7,6},{8,9},{9,8},{10,11... | collective-permute-start | bytes 688136 | tf_op jit(solution)/shard_map/ppermute | solution.py:24
  24.1 6.5 %collective-permute-start.15 = (bf16[32,1792]{1,0:T(8,128)(2,1)S(1)}, bf16[32,1792]{1,0:T(8,128)(2,1)S(1)}, u32[]{:S(2)}, u32[]{:S(2)}) collective-permute-start(bf16[32,1792]{1,0:T(8,128)(2,1)S(1)} %get-tuple-element.45), channel_id=1, source_target_pairs={{0,2},{1,3},{2,0},{3,1},{4,6},{5,7},{6,4},{7,5},{8,10},{9,11},{10,... | collective-permute-start | bytes 344072 | tf_op jit(solution)/shard_map/ppermute | solution.py:24
  25.5 10.6 %collective-permute-start.12 = (bf16[16,1792]{1,0:T(8,128)(2,1)S(1)}, bf16[16,1792]{1,0:T(8,128)(2,1)S(1)}, u32[]{:S(2)}, u32[]{:S(2)}) collective-permute-start(bf16[16,1792]{1,0:T(8,128)(2,1)S(1)} %get-tuple-element.41), channel_id=1, source_target_pairs={{0,2},{1,3},{2,0},{3,1},{4,6},{5,7},{6,4},{7,5},{8,10},{9,11},{10,... | collective-permute-start | bytes 172040 | tf_op jit(solution)/shard_map/ppermute | solution.py:24
  26.2 9.9 %collective-permute-start.14 = (bf16[16,1792]{1,0:T(8,128)(2,1)S(1)}, bf16[16,1792]{1,0:T(8,128)(2,1)S(1)}, u32[]{:S(2)}, u32[]{:S(2)}) collective-permute-start(bf16[16,1792]{1,0:T(8,128)(2,1)S(1)} %get-tuple-element.43), channel_id=1, source_target_pairs={{0,6},{1,7},{2,4},{3,5},{4,2},{5,3},{6,0},{7,1},{8,14},{9,15},{10,... | collective-permute-start | bytes 172040 | tf_op jit(solution)/shard_map/ppermute | solution.py:34
  27.3 8.8 %collective-permute-start.13 = (bf16[16,1792]{1,0:T(8,128)(2,1)S(1)}, bf16[16,1792]{1,0:T(8,128)(2,1)S(1)}, u32[]{:S(2)}, u32[]{:S(2)}) collective-permute-start(bf16[16,1792]{1,0:T(8,128)(2,1)S(1)} %get-tuple-element.42), channel_id=1, source_target_pairs={{0,4},{4,0},{8,12},{12,8},{1,5},{5,1},{9,13},{13,9},{2,6},{6,2},{1... | collective-permute-start | bytes 172040 | tf_op jit(solution)/shard_map/ppermute | solution.py:24
  30.6 6.2 %collective-permute-start.16 = (bf16[16,1792]{1,0:T(8,128)(2,1)S(1)}, bf16[16,1792]{1,0:T(8,128)(2,1)S(1)}, u32[]{:S(2)}, u32[]{:S(2)}) collective-permute-start(bf16[16,1792]{1,0:T(8,128)(2,1)S(1)} %get-tuple-element.46), channel_id=1, source_target_pairs={{0,8},{4,12},{8,0},{12,4},{1,9},{5,13},{9,1},{13,5},{2,10},{6,14},... | collective-permute-start | bytes 172040 | tf_op jit(solution)/shard_map/ppermute | solution.py:24
  32.8 6.0 %collective-permute-start.17 = (bf16[16,1792]{1,0:T(8,128)(2,1)S(1)}, bf16[16,1792]{1,0:T(8,128)(2,1)S(1)}, u32[]{:S(2)}, u32[]{:S(2)}) collective-permute-start(bf16[16,1792]{1,0:T(8,128)(2,1)S(1)} %get-tuple-element.47), channel_id=1, source_target_pairs={{0,12},{4,8},{8,4},{12,0},{1,13},{5,9},{9,5},{13,1},{2,14},{6,10},... | collective-permute-start | bytes 172040 | tf_op jit(solution)/shard_map/ppermute | solution.py:24

commit v5 on v4

--- a/solution.py
+++ b/solution.py
@@ -311,9 +311,9 @@
     )(hidden, w_down)
 
 
-def attend_kernel(ep_count, pd_count, width, dest_ref, len_ref, query_ref, *refs):
+def attend_kernel(order, pd_count, width, dest_ref, len_ref, query_ref, *refs):
     pieces, out_ref = refs[:-1], refs[-1]
-    per = len(pieces) // pd_count
+    ep_count = len(order)
     own, me = lax.axis_index("ep"), lax.axis_index("pd")
     rows, latr = query_ref.shape
     first, second, wide = fold_widths(latr)
@@ -327,16 +327,17 @@
     keys = jnp.concatenate(keys, axis=0).astype(bf16)
     shape = (1, keys.shape[0])
     column = lax.broadcasted_iota(i32, shape, 1)
-    block = column // part % ep_count
+    place = column // part % ep_count
     position = (me ^ (column // (part * ep_count))) * part + column % part
-    length = jnp.zeros(shape, i32)
-    for d in range(ep_count):
+    length, slot = jnp.zeros(shape, i32), jnp.zeros(shape, i32)
+    for i, d in enumerate(order):
         j = own ^ d
         here = i32(0)
         for k in range(ep_count):
             here = jnp.where(dest_ref[j, k] == own, len_ref[j * ep_count + k], here)
-        length = jnp.where(block == d, here, length)
-    slot = jnp.where(position < length, own ^ block, -1)
+        length = jnp.where(place == i, here, length)
+        slot = jnp.where(place == i, j, slot)
+    slot = jnp.where(position < length, slot, -1)
     usable = lax.broadcasted_iota(i32, (rows, 1), 0) // heads == slot
     scores = lax.dot_general(
         query_ref[...], keys, (((1,), (1,)), ((), ())), preferred_element_type=f32
@@ -417,16 +418,19 @@
 
     blocks = route(ids, tokens, cache_rows, destination, ep_count)
     bit = pd_count // 2
-    cut_in = cut_out = min(2, ep_count)
+    direct = [1]
+    staged = [d for d in range(1, ep_count) if d not in direct]
+    order = [0, *direct, *staged]
     arrived = [blocks[0]] + [swap(blocks[d], "ep", d) for d in range(1, ep_count)]
-    over = [swap(blocks[0], "pd", bit)]
-    over += [swap_both(blocks[d], d, bit) for d in range(1, cut_in)]
-    w_gate, w_up, table = fetch([gate_weight[0], up_weight[0]], [], (ids, gate_scores.T), ep_count)
-    rest = join(arrived[cut_in:], [table])
-
-    pieces = {0: [join(arrived[:cut_in], [rest])], bit: [join(over, [rest])]}
+    over = [swap(blocks[0], "pd", bit)] + [swap_both(blocks[d], d, bit) for d in direct]
+    w_gate, w_up, table = fetch(
+        [gate_weight[0], up_weight[0]], [], (ids, gate_scores.T), ep_count
+    )
+    rest = join([arrived[d] for d in staged], [table])
+
+    pieces = {0: [join([arrived[d] for d in [0, *direct]], [rest])], bit: [join(over, [rest])]}
     pieces[bit] += [swap(tie(rest, pieces[0] + pieces[bit]), "pd", bit)]
-    pieces[0] += [join(arrived[cut_in:], pieces[0])]
+    pieces[0] += [join([arrived[d] for d in staged], pieces[0])]
     (w_down,) = fetch([down_weight[0]], pieces[0])
     spread(pieces, 0, bit // 2)
     sums = gate_up([0], width, w_gate, w_up, pieces)
@@ -442,14 +446,12 @@
     parts = {others[0]: part}
     parts.update(zip(others[1:], down(others[1:], width, hidden, w_down, bf16)))
     kept = dict(zip(stay, down(stay, width, hidden, w_down, f32)))
-    direct = range(1, cut_out)
-    shares = [(0, CAP)] + [(d * CAP, CAP) for d in direct]
-    if cut_out < ep_count:
-        shares += [(cut_out * CAP, (ep_count - cut_out) * CAP)]
+    direct = [ep_count - 1]
+    summed = [d for d in order if d and d not in direct]
+    groups = [[d] for d in direct] + [[0], summed]
+    shares = [(order.index(group[0]) * CAP, len(group) * CAP) for group in groups]
     for m in stay:
-        kinds = [bf16] * len(shares)
-        if not m & bit:
-            kinds[0] = kinds[-1] = f32
+        kinds = [bf16 if m & bit or i < len(direct) else f32 for i in range(len(groups))]
         kept[m] = total(
             kept[m],
             swap(parts[m ^ 1], "pd", 1),
@@ -459,7 +461,7 @@
     queries = decode_query.reshape(-1, decode_query.shape[3])
     attended = jax.ShapeDtypeStruct((queries.shape[0], LATC), bf16)
     attended = pl.pallas_call(
-        functools.partial(attend_kernel, ep_count, pd_count, width),
+        functools.partial(attend_kernel, order, pd_count, width),
         out_shape=attended,
         in_specs=[SMEM, SMEM, VMEM] + [VMEM] * len(operands),
         out_specs=VMEM,
@@ -468,17 +470,16 @@
         name="attend",
     )(*map(in_hbm, [destination, lengths, queries]), *operands)
 
-    staged = []
-    if cut_out < ep_count:
-        staged = total(
-            kept[0][-1],
-            swap(kept[bit][-1], "pd", bit),
-            [(d * CAP, CAP, bf16) for d in range(ep_count - cut_out)],
-        )
-    returned = [[total(kept[0][0], swap(kept[bit][0], "pd", bit), [(0, CAP, bf16)])[0]]]
-    for d in direct:
-        returned += [[swap(kept[0][d], "ep", d), swap_both(kept[bit][d], d, bit)]]
-    returned += [[swap(block, "ep", cut_out + i)] for i, block in enumerate(staged)]
+    staged = total(
+        kept[0][-1],
+        swap(kept[bit][-1], "pd", bit),
+        [(i * CAP, CAP, bf16) for i in range(len(summed))],
+    )
+    returned = {d: [swap(block, "ep", d)] for d, block in zip(summed, staged)}
+    for i, d in enumerate(direct):
+        returned[d] = [swap(kept[0][i], "ep", d), swap_both(kept[bit][i], d, bit)]
+    returned[0] = total(kept[0][-2], swap(kept[bit][-2], "pd", bit), [(0, CAP, bf16)])
+    returned = [returned[d] for d in range(ep_count)]
     mixed = mix(table, returned)
     return (mixed, attended.reshape(decode_query.shape[:3] + (LATC,)))
 

time: 40.3 us -> 38.4 us (0.953)
  waiting for transfers between devices: 5.71 us -> 2.41 us
  starting transfers between devices: 20 us -> 21.4 us
    ppermute x16, waiting for transfers between devices: 5.53 us -> 2.22 us  [swap(): return lax.ppermute(value, axis, [(i, i ^ mask) for i in range(count)])]
    ppermute x2, starting transfers between devices: 2.82 us -> 5 us  [swap_both(): return lax.ppermute(value, ('ep', 'pd'), pairs)]
    ppermute x16, starting transfers between devices: 17.2 us -> 16.4 us  [swap(): return lax.ppermute(value, axis, [(i, i ^ mask) for i in range(count)])]
  transfers between devices with their start and end apart: 18 -> 18, of which waited for: 7 -> 5; matrix products, arithmetic and copies ran while one was open for 0% -> 0% of each run, Pallas kernels for 25% -> 26%
where the time goes in v5:
time: 38.4 us; the launch traced here: 38.1 us
  starting transfers between devices  21.4 us (56%)
  Pallas kernels  13.5 us (35%)
  waiting for transfers between devices  2.41 us (6%)
  between operations  0.8 us (2%)
    ppermute x16, starting transfers between devices, swap(): return lax.ppermute(value, axis, [(i, i ^ mask) for i in range(count)])  16.4 us
    pallas_call x2, Pallas kernels, fetch(): pl.pallas_call(functools.partial(fetch_kernel, ep_count, len(arrays), len...  5.93 us
    ppermute x2, starting transfers between devices, swap_both(): return lax.ppermute(value, ('ep', 'pd'), pairs)  5 us
    ppermute x16, waiting for transfers between devices, swap(): return lax.ppermute(value, axis, [(i, i ^ mask) for i in range(count)])  2.22 us
    pallas_call x1, Pallas kernels, on_device(): pl.pallas_call(functools.partial(attend_kernel, order, pd_count, width),...  1.96 us
    pallas_call x1, Pallas kernels, route(): pl.pallas_call(functools.partial(route_kernel, ep_count), out_shape=out_s...  1.56 us
    pallas_call x1, Pallas kernels, mix(): pl.pallas_call(functools.partial(combine_kernel, cuts, [len(block) for bl...  1.22 us
    pallas_call x2, Pallas kernels, gate_up(): pl.pallas_call(functools.partial(gate_up_kernel, masks, width, bool(befor...  1.21 us
  transfers between devices with their start and end apart: 18, of which 5 were waited for; matrix products, arithmetic and copies ran while one was open for 0% of the time, Pallas kernels for 26%

profile of v5, /device:TPU:0, one launch (start us, length us, event | category | flops | bytes accessed | tf_op | source)
XLA Modules:
  0.0 38.1 jit_solution(11770984220211608796)
XLA Ops:
  0.6 1.6 %route.1 = (bf16[16,2176]{1,0:T(8,128)(2,1)S(1)}, bf16[16,2176]{1,0:T(8,128)(2,1)S(1)}, bf16[16,2176]{1,0:T(8,128)(2,1)S(1)}, bf16[16,2176]{1,0:T(8,128)(2,1)S(1)}) custom-call(s32[8,256]{1,0:T(8,128)} %bitcast.12, s32[4,4]{1,0:T(4,128)} %dest_ref.1, bf16[4,8,576]{2,1,0:T(8,128)(2,1)} %refs_2_.1, bf16[256,1792]{1,0:T(8,128)(2,1)} %refs_3_.1), custom_call_target="tpu_custom_call" | custom-call | flops 117440512 | bytes 917504 | tf_op jit(solution)/shard_map/route/pallas_call | solution.py:108
  2.2 4.1 %collective-permute-start.1 = (bf16[16,2176]{1,0:T(8,128)(2,1)S(1)}, bf16[16,2176]{1,0:T(8,128)(2,1)S(1)}, u32[]{:S(2)}, u32[]{:S(2)}) collective-permute-start(bf16[16,2176]{1,0:T(8,128)(2,1)S(1)} %get-tuple-element.30), channel_id=1, source_target_pairs={{0,8},{4,12},{8,0},{12,4},{1,9},{5,13},{9,1},{13,5},{2,10},{6,14},... | collective-permute-start | bytes 208904 | tf_op jit(solution)/shard_map/ppermute | solution.py:24
  6.3 1.3 %collective-permute-start.2 = (bf16[16,2176]{1,0:T(8,128)(2,1)S(1)}, bf16[16,2176]{1,0:T(8,128)(2,1)S(1)}, u32[]{:S(2)}, u32[]{:S(2)}) collective-permute-start(bf16[16,2176]{1,0:T(8,128)(2,1)S(1)} %get-tuple-element.31), channel_id=1, source_target_pairs={{0,12},{4,8},{8,4},{12,0},{1,13},{5,9},{9,5},{13,1},{2,14},{6,10},... | collective-permute-start | bytes 208904 | tf_op jit(solution)/shard_map/ppermute | solution.py:24
  7.6 0.2 collective-permute-start
  7.9 1.5 %collective-permute-start.5 = (bf16[16,2176]{1,0:T(8,128)(2,1)S(1)}, bf16[16,2176]{1,0:T(8,128)(2,1)S(1)}, u32[]{:S(2)}, u32[]{:S(2)}) collective-permute-start(bf16[16,2176]{1,0:T(8,128)(2,1)S(1)} %get-tuple-element.28.refs_0_), channel_id=1, source_target_pairs={{0,2},{1,3},{2,0},{3,1},{4,6},{5,7},{6,4},{7,5},{8,10},{9,11},{10,... | collective-permute-start | bytes 208904 | tf_op jit(solution)/shard_map/ppermute | solution.py:24
  9.4 1.8 %collective-permute-start.6 = (bf16[16,2176]{1,0:T(8,128)(2,1)S(1)}, bf16[16,2176]{1,0:T(8,128)(2,1)S(1)}, u32[]{:S(2)}, u32[]{:S(2)}) collective-permute-start(bf16[16,2176]{1,0:T(8,128)(2,1)S(1)} %get-tuple-element.29), channel_id=1, source_target_pairs={{0,6},{1,7},{2,4},{3,5},{4,2},{5,3},{6,0},{7,1},{8,14},{9,15},{10,... | collective-permute-start | bytes 208904 | tf_op jit(solution)/shard_map/ppermute | solution.py:34
  11.1 3.9 %fetch.2 = (bf16[7168,256]{1,0:T(8,128)(2,1)S(1)}, bf16[7168,256]{1,0:T(8,128)(2,1)S(1)}, bf16[256,128]{1,0:T(8,128)(2,1)S(1)}) custom-call(bf16[7168,256]{1,0:T(8,128)(2,1)} %bitcast.7, bf16[7168,256]{1,0:T(8,128)(2,1)} %bitcast.8, s32[8,256]{1,0:T(8,128)} %bitcast.13, f32[8,256]{1,0:T(8,128)} %bitcast.14), custom_call_target="tpu_custom_call" | custom-call | tf_op jit(solution)/shard_map/fetch/pallas_call | solution.py:159
  15.0 0.0 collective-permute-done.1.refs_0_
  15.0 0.0 collective-permute-done.2.refs_1_
  15.1 0.0 collective-permute-done.refs_1_
  15.1 0.0 collective-permute-done.5.refs_0_
  15.1 0.2 collective-permute-done.6.refs_1_
  15.3 1.4 %collective-permute-start.7 = (bf16[32,2176]{1,0:T(8,128)(2,1)S(1)}, bf16[32,2176]{1,0:T(8,128)(2,1)S(1)}, u32[]{:S(2)}, u32[]{:S(2)}) collective-permute-start(bf16[32,2176]{1,0:T(8,128)(2,1)S(1)} %tie.2), channel_id=1, source_target_pairs={{0,2},{1,3},{2,0},{3,1},{4,6},{5,7},{6,4},{7,5},{8,10},{9,11},{10,... | collective-permute-start | bytes 417800 | tf_op jit(solution)/shard_map/ppermute | solution.py:24
  16.7 0.0 collective-permute-start.3
  16.7 0.5 %collective-permute-start.8 = (bf16[32,2176]{1,0:T(8,128)(2,1)S(1)}, bf16[32,2176]{1,0:T(8,128)(2,1)S(1)}, u32[]{:S(2)}, u32[]{:S(2)}) collective-permute-start(bf16[32,2176]{1,0:T(8,128)(2,1)S(1)} %join.7.refs_2_.refs_4_), channel_id=1, source_target_pairs={{0,1},{1,0},{2,3},{3,2},{4,5},{5,4},{6,7},{7,6},{8,9},{9,8},{10,11... | collective-permute-start | bytes 417800 | tf_op jit(solution)/shard_map/ppermute | solution.py:24
  17.2 0.1 collective-permute-start.4
  17.3 2.0 %fetch.3.refs_2_.down_ref = bf16[256,7168]{1,0:T(8,128)(2,1)S(1)} custom-call(bf16[256,7168]{1,0:T(8,128)(2,1)} %bitcast.9, bf16[32,2176]{1,0:T(8,128)(2,1)S(1)} %join.5.refs_2_.refs_1_.refs_0_, bf16[32,2176]{1,0:T(8,128)(2,1)S(1)} %join.6.refs_2_.refs_1_), custom_call_target="tpu_custom_call" | custom-call | tf_op jit(solution)/shard_map/fetch/pallas_call | solution.py:159
  19.4 0.4 %gate_up.2 = (f32[64,256]{1,0:T(8,128)S(1)}, f32[64,256]{1,0:T(8,128)S(1)}) custom-call(bf16[7168,256]{1,0:T(8,128)(2,1)S(1)} %get-tuple-element.26.gate_ref, bf16[7168,256]{1,0:T(8,128)(2,1)S(1)} %get-tuple-element.27.up_ref, bf16[32,2176]{1,0:T(8,128)(2,1)S(1)} %join.5.refs_2_.refs_1_.refs_0_, bf16[32,2176]{1,0:T(8,128)(2,1)S(1)} %join.6.refs_2_.refs_1_), custom_call_target="tpu_custom_call" | custom-call | tf_op jit(solution)/shard_map/gate_up/pallas_call | solution.py:254
  19.8 0.6 %collective-permute-done.7.refs_0_ = bf16[32,2176]{1,0:T(8,128)(2,1)S(1)} collective-permute-done((bf16[32,2176]{1,0:T(8,128)(2,1)S(1)}, bf16[32,2176]{1,0:T(8,128)(2,1)S(1)}, u32[]{:S(2)}, u32[]{:S(2)}) %collective-permute-start.7) | collective-permute-done | bytes 139296 | tf_op jit(solution)/shard_map/ppermute | solution.py:24
  20.4 0.0 collective-permute-start.9
  20.4 0.0 collective-permute-done.4.refs_3_
  20.4 0.0 collective-permute-done.3.refs_2_
  20.4 0.8 %gate_up.3 = (f32[64,256]{1,0:T(8,128)S(1)}, f32[64,256]{1,0:T(8,128)S(1)}) custom-call(bf16[7168,256]{1,0:T(8,128)(2,1)S(1)} %get-tuple-element.26.gate_ref, bf16[7168,256]{1,0:T(8,128)(2,1)S(1)} %get-tuple-element.27.up_ref, f32[64,256]{1,0:T(8,128)S(1)} %get-tuple-element.32.refs_1_.refs_0_, f32[64,256]{1,0:T(8,128)S(1)} %get-tuple-element.33.refs_1_, ...), custom_call_target="tpu_custom_call" | custom-call | tf_op jit(solution)/shard_map/gate_up/pallas_call | solution.py:254
  21.2 0.0 collective-permute-done.8.refs_2_.refs_6_
  21.2 0.6 %collective-permute-done.9.refs_3_.refs_7_ = bf16[32,2176]{1,0:T(8,128)(2,1)S(1)} collective-permute-done((bf16[32,2176]{1,0:T(8,128)(2,1)S(1)}, bf16[32,2176]{1,0:T(8,128)(2,1)S(1)}, u32[]{:S(2)}, u32[]{:S(2)}) %collective-permute-start.9) | collective-permute-done | bytes 139296 | tf_op jit(solution)/shard_map/ppermute | solution.py:24
  21.8 0.7 %hidden.1 = (bf16[64,256]{1,0:T(8,128)(2,1)S(1)}, bf16[64,1792]{1,0:T(8,128)(2,1)S(1)}) custom-call(bf16[7168,256]{1,0:T(8,128)(2,1)S(1)} %get-tuple-element.26.gate_ref, bf16[7168,256]{1,0:T(8,128)(2,1)S(1)} %get-tuple-element.27.up_ref, bf16[256,7168]{1,0:T(8,128)(2,1)S(1)} %fetch.3.refs_2_.down_ref, f32[64,256]{1,0:T(8,128)S(1)} %get-tuple-element.34.refs_0_, ...), custom_call_target="tpu_custom_call" | custom-call | tf_op jit(solution)/shard_map/hidden/pallas_call | solution.py:282
  22.5 0.2 collective-permute-start.11
  22.7 0.3 down.3
  23.0 0.4 %collective-permute-start.10 = (bf16[64,1792]{1,0:T(8,128)(2,1)S(1)}, bf16[64,1792]{1,0:T(8,128)(2,1)S(1)}, u32[]{:S(2)}, u32[]{:S(2)}) collective-permute-start(bf16[64,1792]{1,0:T(8,128)(2,1)S(1)} %down.3), channel_id=1, source_target_pairs={{0,1},{1,0},{2,3},{3,2},{4,5},{5,4},{6,7},{7,6},{8,9},{9,8},{10,11... | collective-permute-start | bytes 688136 | tf_op jit(solution)/shard_map/ppermute | solution.py:24
  23.4 0.5 %down.2 = (f32[64,1792]{1,0:T(8,128)S(1)}, f32[64,1792]{1,0:T(8,128)S(1)}) custom-call(bf16[64,256]{1,0:T(8,128)(2,1)S(1)} %get-tuple-element.36.hidden_ref, bf16[256,7168]{1,0:T(8,128)(2,1)S(1)} %fetch.3.refs_2_.down_ref), custom_call_target="tpu_custom_call" | custom-call | flops 234881024 | bytes 3670016 | tf_op jit(solution)/shard_map/down/pallas_call | solution.py:303
  23.9 0.2 collective-permute-done.11.arrived_ref
  24.1 1.4 %collective-permute-start.13 = (bf16[32,1792]{1,0:T(8,128)(2,1)S(1)}, bf16[32,1792]{1,0:T(8,128)(2,1)S(1)}, u32[]{:S(2)}, u32[]{:S(2)}) collective-permute-start(bf16[32,1792]{1,0:T(8,128)(2,1)S(1)} %get-tuple-element.43), channel_id=1, source_target_pairs={{0,2},{1,3},{2,0},{3,1},{4,6},{5,7},{6,4},{7,5},{8,10},{9,11},{10,... | collective-permute-start | bytes 344072 | tf_op jit(solution)/shard_map/ppermute | solution.py:24
  25.5 0.7 %collective-permute-start.12 = (bf16[16,1792]{1,0:T(8,128)(2,1)S(1)}, bf16[16,1792]{1,0:T(8,128)(2,1)S(1)}, u32[]{:S(2)}, u32[]{:S(2)}) collective-permute-start(bf16[16,1792]{1,0:T(8,128)(2,1)S(1)} %get-tuple-element.41), channel_id=1, source_target_pairs={{0,2},{1,3},{2,0},{3,1},{4,6},{5,7},{6,4},{7,5},{8,10},{9,11},{10,... | collective-permute-start | bytes 172040 | tf_op jit(solution)/shard_map/ppermute | solution.py:24
  26.2 3.2 %collective-permute-start.17 = (bf16[16,1792]{1,0:T(8,128)(2,1)S(1)}, bf16[16,1792]{1,0:T(8,128)(2,1)S(1)}, u32[]{:S(2)}, u32[]{:S(2)}) collective-permute-start(bf16[16,1792]{1,0:T(8,128)(2,1)S(1)} %get-tuple-element.47), channel_id=1, source_target_pairs={{0,14},{1,15},{2,12},{3,13},{4,10},{5,11},{6,8},{7,9},{8,6},{9,7},... | collective-permute-start | bytes 172040 | tf_op jit(solution)/shard_map/ppermute | solution.py:34
  29.4 0.0 collective-permute-done.10.arrived_ref
  29.5 1.4 %collective-permute-start.16 = (bf16[16,1792]{1,0:T(8,128)(2,1)S(1)}, bf16[16,1792]{1,0:T(8,128)(2,1)S(1)}, u32[]{:S(2)}, u32[]{:S(2)}) collective-permute-start(bf16[16,1792]{1,0:T(8,128)(2,1)S(1)} %get-tuple-element.46), channel_id=1, source_target_pairs={{0,12},{4,8},{8,4},{12,0},{1,13},{5,9},{9,5},{13,1},{2,14},{6,10},... | collective-permute-start | bytes 172040 | tf_op jit(solution)/shard_map/ppermute | solution.py:24
  30.9 0.0 collective-permute-done.13.arrived_ref
  30.9 0.8 %collective-permute-start.14 = (bf16[16,1792]{1,0:T(8,128)(2,1)S(1)}, bf16[16,1792]{1,0:T(8,128)(2,1)S(1)}, u32[]{:S(2)}, u32[]{:S(2)}) collective-permute-start(bf16[16,1792]{1,0:T(8,128)(2,1)S(1)} %get-tuple-element.44), channel_id=1, source_target_pairs={{0,4},{4,0},{8,12},{12,8},{1,5},{5,1},{9,13},{13,9},{2,6},{6,2},{1... | collective-permute-start | bytes 172040 | tf_op jit(solution)/shard_map/ppermute | solution.py:24
  31.8 2.3 %collective-permute-start.15 = (bf16[16,1792]{1,0:T(8,128)(2,1)S(1)}, bf16[16,1792]{1,0:T(8,128)(2,1)S(1)}, u32[]{:S(2)}, u32[]{:S(2)}) collective-permute-start(bf16[16,1792]{1,0:T(8,128)(2,1)S(1)} %get-tuple-element.45), channel_id=1, source_target_pairs={{0,8},{4,12},{8,0},{12,4},{1,9},{5,13},{9,1},{13,5},{2,10},{6,14},... | collective-permute-start | bytes 172040 | tf_op jit(solution)/shard_map/ppermute | solution.py:24
  34.0 2.0 %attend.1 = bf16[64,512]{1,0:T(8,128)(2,1)} custom-call(s32[4,4]{1,0:T(4,128)} %dest_ref.1, s32[16]{0:T(128)} %len_ref.1, bf16[64,576]{1,0:T(8,128)(2,1)} %bitcast.10, bf16[32,2176]{1,0:T(8,128)(2,1)S(1)} %join.5.refs_2_.refs_1_.refs_0_, bf16[32,2176]{1,0:T(8,128)(2,1)S(1)} %join.6.refs_2_.refs_1_, bf16[32,2176]{1,0:T(8,128)(2,1)S(1)} %collective-permute-done.3.refs_2_, ...), custom_call_target="tpu_custom_call" | custom-call | flops 234881024 | bytes 3670016 | tf_op jit(solution)/shard_map/attend/pallas_call | solution.py:463
  36.0 0.0 collective-permute-done.12.arrived_ref
  36.0 0.0 collective-permute-done.17.refs_4_
  36.0 0.0 collective-permute-done.16.refs_3_
  36.0 0.0 collective-permute-done.14.refs_1_
  36.0 0.8 %collective-permute-done.15.refs_2_ = bf16[16,1792]{1,0:T(8,128)(2,1)S(1)} collective-permute-done((bf16[16,1792]{1,0:T(8,128)(2,1)S(1)}, bf16[16,1792]{1,0:T(8,128)(2,1)S(1)}, u32[]{:S(2)}, u32[]{:S(2)}) %collective-permute-start.15) | collective-permute-done | bytes 57376 | tf_op jit(solution)/shard_map/ppermute | solution.py:24
  36.8 1.2 %combine.1 = bf16[256,1792]{1,0:T(8,128)(2,1)} custom-call(bf16[256,128]{1,0:T(8,128)(2,1)S(1)} %get-tuple-element.25.refs_2_.table_ref, bf16[16,1792]{1,0:T(8,128)(2,1)S(1)} %total.6.refs_0_, bf16[16,1792]{1,0:T(8,128)(2,1)S(1)} %collective-permute-done.14.refs_1_, bf16[16,1792]{1,0:T(8,128)(2,1)S(1)} %collective-permute-done.15.refs_2_, ...), custom_call_target="tpu_custom_call" | custom-call | flops 117440512 | bytes 917504 | tf_op jit(solution)/shard_map/combine/pallas_call | solution.py:381
  (10 shorter events, 0.2 us)
Async XLA Ops:
  2.2 12.8 %collective-permute-start.1 = (bf16[16,2176]{1,0:T(8,128)(2,1)S(1)}, bf16[16,2176]{1,0:T(8,128)(2,1)S(1)}, u32[]{:S(2)}, u32[]{:S(2)}) collective-permute-start(bf16[16,2176]{1,0:T(8,128)(2,1)S(1)} %get-tuple-element.30), channel_id=1, source_target_pairs={{0,8},{4,12},{8,0},{12,4},{1,9},{5,13},{9,1},{13,5},{2,10},{6,14},... | collective-permute-start | bytes 208904 | tf_op jit(solution)/shard_map/ppermute | solution.py:24
  6.3 8.7 %collective-permute-start.2 = (bf16[16,2176]{1,0:T(8,128)(2,1)S(1)}, bf16[16,2176]{1,0:T(8,128)(2,1)S(1)}, u32[]{:S(2)}, u32[]{:S(2)}) collective-permute-start(bf16[16,2176]{1,0:T(8,128)(2,1)S(1)} %get-tuple-element.31), channel_id=1, source_target_pairs={{0,12},{4,8},{8,4},{12,0},{1,13},{5,9},{9,5},{13,1},{2,14},{6,10},... | collective-permute-start | bytes 208904 | tf_op jit(solution)/shard_map/ppermute | solution.py:24
  7.6 7.4 %collective-permute-start = (bf16[16,2176]{1,0:T(8,128)(2,1)S(1)}, bf16[16,2176]{1,0:T(8,128)(2,1)S(1)}, u32[]{:S(2)}, u32[]{:S(2)}) collective-permute-start(bf16[16,2176]{1,0:T(8,128)(2,1)S(1)} %get-tuple-element.29), channel_id=1, source_target_pairs={{0,4},{4,0},{8,12},{12,8},{1,5},{5,1},{9,13},{13,9},{2,6},{6,2},{1... | collective-permute-start | bytes 208904 | tf_op jit(solution)/shard_map/ppermute | solution.py:24
  7.9 7.2 %collective-permute-start.5 = (bf16[16,2176]{1,0:T(8,128)(2,1)S(1)}, bf16[16,2176]{1,0:T(8,128)(2,1)S(1)}, u32[]{:S(2)}, u32[]{:S(2)}) collective-permute-start(bf16[16,2176]{1,0:T(8,128)(2,1)S(1)} %get-tuple-element.28.refs_0_), channel_id=1, source_target_pairs={{0,2},{1,3},{2,0},{3,1},{4,6},{5,7},{6,4},{7,5},{8,10},{9,11},{10,... | collective-permute-start | bytes 208904 | tf_op jit(solution)/shard_map/ppermute | solution.py:24
  9.4 5.9 %collective-permute-start.6 = (bf16[16,2176]{1,0:T(8,128)(2,1)S(1)}, bf16[16,2176]{1,0:T(8,128)(2,1)S(1)}, u32[]{:S(2)}, u32[]{:S(2)}) collective-permute-start(bf16[16,2176]{1,0:T(8,128)(2,1)S(1)} %get-tuple-element.29), channel_id=1, source_target_pairs={{0,6},{1,7},{2,4},{3,5},{4,2},{5,3},{6,0},{7,1},{8,14},{9,15},{10,... | collective-permute-start | bytes 208904 | tf_op jit(solution)/shard_map/ppermute | solution.py:34
  15.3 5.1 %collective-permute-start.7 = (bf16[32,2176]{1,0:T(8,128)(2,1)S(1)}, bf16[32,2176]{1,0:T(8,128)(2,1)S(1)}, u32[]{:S(2)}, u32[]{:S(2)}) collective-permute-start(bf16[32,2176]{1,0:T(8,128)(2,1)S(1)} %tie.2), channel_id=1, source_target_pairs={{0,2},{1,3},{2,0},{3,1},{4,6},{5,7},{6,4},{7,5},{8,10},{9,11},{10,... | collective-permute-start | bytes 417800 | tf_op jit(solution)/shard_map/ppermute | solution.py:24
  16.7 3.7 %collective-permute-start.3 = (bf16[32,2176]{1,0:T(8,128)(2,1)S(1)}, bf16[32,2176]{1,0:T(8,128)(2,1)S(1)}, u32[]{:S(2)}, u32[]{:S(2)}) collective-permute-start(bf16[32,2176]{1,0:T(8,128)(2,1)S(1)} %join.5.refs_2_.refs_1_.refs_0_), channel_id=1, source_target_pairs={{0,1},{1,0},{2,3},{3,2},{4,5},{5,4},{6,7},{7,6},{8,9},{9,8},{10,11... | collective-permute-start | bytes 417800 | tf_op jit(solution)/shard_map/ppermute | solution.py:24
  16.7 4.5 %collective-permute-start.8 = (bf16[32,2176]{1,0:T(8,128)(2,1)S(1)}, bf16[32,2176]{1,0:T(8,128)(2,1)S(1)}, u32[]{:S(2)}, u32[]{:S(2)}) collective-permute-start(bf16[32,2176]{1,0:T(8,128)(2,1)S(1)} %join.7.refs_2_.refs_4_), channel_id=1, source_target_pairs={{0,1},{1,0},{2,3},{3,2},{4,5},{5,4},{6,7},{7,6},{8,9},{9,8},{10,11... | collective-permute-start | bytes 417800 | tf_op jit(solution)/shard_map/ppermute | solution.py:24
  17.2 3.2 %collective-permute-start.4 = (bf16[32,2176]{1,0:T(8,128)(2,1)S(1)}, bf16[32,2176]{1,0:T(8,128)(2,1)S(1)}, u32[]{:S(2)}, u32[]{:S(2)}) collective-permute-start(bf16[32,2176]{1,0:T(8,128)(2,1)S(1)} %join.6.refs_2_.refs_1_), channel_id=1, source_target_pairs={{0,1},{1,0},{2,3},{3,2},{4,5},{5,4},{6,7},{7,6},{8,9},{9,8},{10,11... | collective-permute-start | bytes 417800 | tf_op jit(solution)/shard_map/ppermute | solution.py:24
  20.4 1.4 %collective-permute-start.9 = (bf16[32,2176]{1,0:T(8,128)(2,1)S(1)}, bf16[32,2176]{1,0:T(8,128)(2,1)S(1)}, u32[]{:S(2)}, u32[]{:S(2)}) collective-permute-start(bf16[32,2176]{1,0:T(8,128)(2,1)S(1)} %tie.3.refs_5_), channel_id=1, source_target_pairs={{0,1},{1,0},{2,3},{3,2},{4,5},{5,4},{6,7},{7,6},{8,9},{9,8},{10,11... | collective-permute-start | bytes 417800 | tf_op jit(solution)/shard_map/ppermute | solution.py:24
  22.5 1.5 %collective-permute-start.11 = (bf16[64,1792]{1,0:T(8,128)(2,1)S(1)}, bf16[64,1792]{1,0:T(8,128)(2,1)S(1)}, u32[]{:S(2)}, u32[]{:S(2)}) collective-permute-start(bf16[64,1792]{1,0:T(8,128)(2,1)S(1)} %get-tuple-element.40), channel_id=1, source_target_pairs={{0,1},{1,0},{2,3},{3,2},{4,5},{5,4},{6,7},{7,6},{8,9},{9,8},{10,11... | collective-permute-start | bytes 688136 | tf_op jit(solution)/shard_map/ppermute | solution.py:24
  23.0 6.4 %collective-permute-start.10 = (bf16[64,1792]{1,0:T(8,128)(2,1)S(1)}, bf16[64,1792]{1,0:T(8,128)(2,1)S(1)}, u32[]{:S(2)}, u32[]{:S(2)}) collective-permute-start(bf16[64,1792]{1,0:T(8,128)(2,1)S(1)} %down.3), channel_id=1, source_target_pairs={{0,1},{1,0},{2,3},{3,2},{4,5},{5,4},{6,7},{7,6},{8,9},{9,8},{10,11... | collective-permute-start | bytes 688136 | tf_op jit(solution)/shard_map/ppermute | solution.py:24
  24.1 6.8 %collective-permute-start.13 = (bf16[32,1792]{1,0:T(8,128)(2,1)S(1)}, bf16[32,1792]{1,0:T(8,128)(2,1)S(1)}, u32[]{:S(2)}, u32[]{:S(2)}) collective-permute-start(bf16[32,1792]{1,0:T(8,128)(2,1)S(1)} %get-tuple-element.43), channel_id=1, source_target_pairs={{0,2},{1,3},{2,0},{3,1},{4,6},{5,7},{6,4},{7,5},{8,10},{9,11},{10,... | collective-permute-start | bytes 344072 | tf_op jit(solution)/shard_map/ppermute | solution.py:24
  25.5 10.5 %collective-permute-start.12 = (bf16[16,1792]{1,0:T(8,128)(2,1)S(1)}, bf16[16,1792]{1,0:T(8,128)(2,1)S(1)}, u32[]{:S(2)}, u32[]{:S(2)}) collective-permute-start(bf16[16,1792]{1,0:T(8,128)(2,1)S(1)} %get-tuple-element.41), channel_id=1, source_target_pairs={{0,2},{1,3},{2,0},{3,1},{4,6},{5,7},{6,4},{7,5},{8,10},{9,11},{10,... | collective-permute-start | bytes 172040 | tf_op jit(solution)/shard_map/ppermute | solution.py:24
  26.2 9.8 %collective-permute-start.17 = (bf16[16,1792]{1,0:T(8,128)(2,1)S(1)}, bf16[16,1792]{1,0:T(8,128)(2,1)S(1)}, u32[]{:S(2)}, u32[]{:S(2)}) collective-permute-start(bf16[16,1792]{1,0:T(8,128)(2,1)S(1)} %get-tuple-element.47), channel_id=1, source_target_pairs={{0,14},{1,15},{2,12},{3,13},{4,10},{5,11},{6,8},{7,9},{8,6},{9,7},... | collective-permute-start | bytes 172040 | tf_op jit(solution)/shard_map/ppermute | solution.py:34
  29.5 6.6 %collective-permute-start.16 = (bf16[16,1792]{1,0:T(8,128)(2,1)S(1)}, bf16[16,1792]{1,0:T(8,128)(2,1)S(1)}, u32[]{:S(2)}, u32[]{:S(2)}) collective-permute-start(bf16[16,1792]{1,0:T(8,128)(2,1)S(1)} %get-tuple-element.46), channel_id=1, source_target_pairs={{0,12},{4,8},{8,4},{12,0},{1,13},{5,9},{9,5},{13,1},{2,14},{6,10},... | collective-permute-start | bytes 172040 | tf_op jit(solution)/shard_map/ppermute | solution.py:24
  30.9 5.1 %collective-permute-start.14 = (bf16[16,1792]{1,0:T(8,128)(2,1)S(1)}, bf16[16,1792]{1,0:T(8,128)(2,1)S(1)}, u32[]{:S(2)}, u32[]{:S(2)}) collective-permute-start(bf16[16,1792]{1,0:T(8,128)(2,1)S(1)} %get-tuple-element.44), channel_id=1, source_target_pairs={{0,4},{4,0},{8,12},{12,8},{1,5},{5,1},{9,13},{13,9},{2,6},{6,2},{1... | collective-permute-start | bytes 172040 | tf_op jit(solution)/shard_map/ppermute | solution.py:24
  31.8 5.1 %collective-permute-start.15 = (bf16[16,1792]{1,0:T(8,128)(2,1)S(1)}, bf16[16,1792]{1,0:T(8,128)(2,1)S(1)}, u32[]{:S(2)}, u32[]{:S(2)}) collective-permute-start(bf16[16,1792]{1,0:T(8,128)(2,1)S(1)} %get-tuple-element.45), channel_id=1, source_target_pairs={{0,8},{4,12},{8,0},{12,4},{1,9},{5,13},{9,1},{13,5},{2,10},{6,14},... | collective-permute-start | bytes 172040 | tf_op jit(solution)/shard_map/ppermute | solution.py:24

commit v6 on v5

--- a/solution.py
+++ b/solution.py
@@ -422,14 +422,15 @@
     staged = [d for d in range(1, ep_count) if d not in direct]
     order = [0, *direct, *staged]
     arrived = [blocks[0]] + [swap(blocks[d], "ep", d) for d in range(1, ep_count)]
-    over = [swap(blocks[0], "pd", bit)] + [swap_both(blocks[d], d, bit) for d in direct]
+    over = [swap(blocks[0], "pd", bit)]
+    over += [join([swap_both(blocks[d], d, bit)]) for d in direct]
     w_gate, w_up, table = fetch(
         [gate_weight[0], up_weight[0]], [], (ids, gate_scores.T), ep_count
     )
     rest = join([arrived[d] for d in staged], [table])
 
     pieces = {0: [join([arrived[d] for d in [0, *direct]], [rest])], bit: [join(over, [rest])]}
-    pieces[bit] += [swap(tie(rest, pieces[0] + pieces[bit]), "pd", bit)]
+    pieces[bit] += [swap(tie(rest, pieces[0] + over[1:]), "pd", bit)]
     pieces[0] += [join([arrived[d] for d in staged], pieces[0])]
     (w_down,) = fetch([down_weight[0]], pieces[0])
     spread(pieces, 0, bit // 2)

time: 38.4 us -> 38 us (0.990)
  starting transfers between devices: 21.4 us -> 19.6 us
  waiting for transfers between devices: 2.41 us -> 3.82 us
    ppermute x16, starting transfers between devices: 16.4 us -> 12.5 us  [swap(): return lax.ppermute(value, axis, [(i, i ^ mask) for i in range(count)])]
    ppermute x2, starting transfers between devices: 5 us -> 7.03 us  [swap_both(): return lax.ppermute(value, ('ep', 'pd'), pairs)]
    ppermute x16, waiting for transfers between devices: 2.22 us -> 3.81 us  [swap(): return lax.ppermute(value, axis, [(i, i ^ mask) for i in range(count)])]
  transfers between devices with their start and end apart: 18 -> 18, of which waited for: 5 -> 5; matrix products, arithmetic and copies ran while one was open for 0% -> 0% of each run, Pallas kernels for 26% -> 27%
where the time goes in v6:
time: 38 us; the launch traced here: 37.7 us
  starting transfers between devices  19.6 us (52%)
  Pallas kernels  13.5 us (36%)
  waiting for transfers between devices  3.82 us (10%)
  between operations  0.81 us (2%)
    ppermute x16, starting transfers between devices, swap(): return lax.ppermute(value, axis, [(i, i ^ mask) for i in range(count)])  12.5 us
    ppermute x2, starting transfers between devices, swap_both(): return lax.ppermute(value, ('ep', 'pd'), pairs)  7.03 us
    pallas_call x2, Pallas kernels, fetch(): pl.pallas_call(functools.partial(fetch_kernel, ep_count, len(arrays), len...  5.93 us
    ppermute x16, waiting for transfers between devices, swap(): return lax.ppermute(value, axis, [(i, i ^ mask) for i in range(count)])  3.81 us
    pallas_call x1, Pallas kernels, on_device(): pl.pallas_call(functools.partial(attend_kernel, order, pd_count, width),...  1.96 us
    pallas_call x1, Pallas kernels, route(): pl.pallas_call(functools.partial(route_kernel, ep_count), out_shape=out_s...  1.56 us
    pallas_call x1, Pallas kernels, mix(): pl.pallas_call(functools.partial(combine_kernel, cuts, [len(block) for bl...  1.22 us
    pallas_call x2, Pallas kernels, gate_up(): pl.pallas_call(functools.partial(gate_up_kernel, masks, width, bool(befor...  1.21 us
  transfers between devices with their start and end apart: 18, of which 5 were waited for; matrix products, arithmetic and copies ran while one was open for 0% of the time, Pallas kernels for 27%

profile of v6, /device:TPU:0, one launch (start us, length us, event | category | flops | bytes accessed | tf_op | source)
XLA Modules:
  0.0 37.7 jit_solution(2332837913174782369)
XLA Ops:
  0.6 1.6 %route.1 = (bf16[16,2176]{1,0:T(8,128)(2,1)S(1)}, bf16[16,2176]{1,0:T(8,128)(2,1)S(1)}, bf16[16,2176]{1,0:T(8,128)(2,1)S(1)}, bf16[16,2176]{1,0:T(8,128)(2,1)S(1)}) custom-call(s32[8,256]{1,0:T(8,128)} %bitcast.12, s32[4,4]{1,0:T(4,128)} %dest_ref.1, bf16[4,8,576]{2,1,0:T(8,128)(2,1)} %refs_2_.1, bf16[256,1792]{1,0:T(8,128)(2,1)} %refs_3_.1), custom_call_target="tpu_custom_call" | custom-call | flops 117440512 | bytes 917504 | tf_op jit(solution)/shard_map/route/pallas_call | solution.py:108
  2.2 4.0 %collective-permute-start.6 = (bf16[16,2176]{1,0:T(8,128)(2,1)S(1)}, bf16[16,2176]{1,0:T(8,128)(2,1)S(1)}, u32[]{:S(2)}, u32[]{:S(2)}) collective-permute-start(bf16[16,2176]{1,0:T(8,128)(2,1)S(1)} %get-tuple-element.29), channel_id=1, source_target_pairs={{0,6},{1,7},{2,4},{3,5},{4,2},{5,3},{6,0},{7,1},{8,14},{9,15},{10,... | collective-permute-start | bytes 208904 | tf_op jit(solution)/shard_map/ppermute | solution.py:34
  6.2 2.6 %collective-permute-start.1 = (bf16[16,2176]{1,0:T(8,128)(2,1)S(1)}, bf16[16,2176]{1,0:T(8,128)(2,1)S(1)}, u32[]{:S(2)}, u32[]{:S(2)}) collective-permute-start(bf16[16,2176]{1,0:T(8,128)(2,1)S(1)} %get-tuple-element.30), channel_id=1, source_target_pairs={{0,8},{4,12},{8,0},{12,4},{1,9},{5,13},{9,1},{13,5},{2,10},{6,14},... | collective-permute-start | bytes 208904 | tf_op jit(solution)/shard_map/ppermute | solution.py:24
  8.8 0.2 collective-permute-start.2
  9.0 0.7 %collective-permute-start = (bf16[16,2176]{1,0:T(8,128)(2,1)S(1)}, bf16[16,2176]{1,0:T(8,128)(2,1)S(1)}, u32[]{:S(2)}, u32[]{:S(2)}) collective-permute-start(bf16[16,2176]{1,0:T(8,128)(2,1)S(1)} %get-tuple-element.29), channel_id=1, source_target_pairs={{0,4},{4,0},{8,12},{12,8},{1,5},{5,1},{9,13},{13,9},{2,6},{6,2},{1... | collective-permute-start | bytes 208904 | tf_op jit(solution)/shard_map/ppermute | solution.py:24
  9.7 0.5 %collective-permute-start.5 = (bf16[16,2176]{1,0:T(8,128)(2,1)S(1)}, bf16[16,2176]{1,0:T(8,128)(2,1)S(1)}, u32[]{:S(2)}, u32[]{:S(2)}) collective-permute-start(bf16[16,2176]{1,0:T(8,128)(2,1)S(1)} %get-tuple-element.28.refs_0_), channel_id=1, source_target_pairs={{0,2},{1,3},{2,0},{3,1},{4,6},{5,7},{6,4},{7,5},{8,10},{9,11},{10,... | collective-permute-start | bytes 208904 | tf_op jit(solution)/shard_map/ppermute | solution.py:24
  10.2 3.9 %fetch.2 = (bf16[7168,256]{1,0:T(8,128)(2,1)S(1)}, bf16[7168,256]{1,0:T(8,128)(2,1)S(1)}, bf16[256,128]{1,0:T(8,128)(2,1)S(1)}) custom-call(bf16[7168,256]{1,0:T(8,128)(2,1)} %bitcast.7, bf16[7168,256]{1,0:T(8,128)(2,1)} %bitcast.8, s32[8,256]{1,0:T(8,128)} %bitcast.13, f32[8,256]{1,0:T(8,128)} %bitcast.14), custom_call_target="tpu_custom_call" | custom-call | tf_op jit(solution)/shard_map/fetch/pallas_call | solution.py:159
  14.1 0.0 collective-permute-done.6.refs_0_
  14.2 0.0 collective-permute-done.1.refs_0_
  14.2 0.9 %collective-permute-done.2.refs_1_ = bf16[16,2176]{1,0:T(8,128)(2,1)S(1)} collective-permute-done((bf16[16,2176]{1,0:T(8,128)(2,1)S(1)}, bf16[16,2176]{1,0:T(8,128)(2,1)S(1)}, u32[]{:S(2)}, u32[]{:S(2)}) %collective-permute-start.2) | collective-permute-done | bytes 69664 | tf_op jit(solution)/shard_map/ppermute | solution.py:24
  15.0 0.0 collective-permute-done.refs_1_
  15.1 0.0 collective-permute-done.5.refs_0_
  15.1 0.7 %collective-permute-start.7 = (bf16[32,2176]{1,0:T(8,128)(2,1)S(1)}, bf16[32,2176]{1,0:T(8,128)(2,1)S(1)}, u32[]{:S(2)}, u32[]{:S(2)}) collective-permute-start(bf16[32,2176]{1,0:T(8,128)(2,1)S(1)} %tie.2), channel_id=1, source_target_pairs={{0,2},{1,3},{2,0},{3,1},{4,6},{5,7},{6,4},{7,5},{8,10},{9,11},{10,... | collective-permute-start | bytes 417800 | tf_op jit(solution)/shard_map/ppermute | solution.py:24
  15.8 0.0 collective-permute-start.3
  15.8 0.5 %collective-permute-start.8 = (bf16[32,2176]{1,0:T(8,128)(2,1)S(1)}, bf16[32,2176]{1,0:T(8,128)(2,1)S(1)}, u32[]{:S(2)}, u32[]{:S(2)}) collective-permute-start(bf16[32,2176]{1,0:T(8,128)(2,1)S(1)} %join.9.refs_4_), channel_id=1, source_target_pairs={{0,1},{1,0},{2,3},{3,2},{4,5},{5,4},{6,7},{7,6},{8,9},{9,8},{10,11... | collective-permute-start | bytes 417800 | tf_op jit(solution)/shard_map/ppermute | solution.py:24
  16.3 0.1 collective-permute-start.4
  16.4 2.0 %fetch.3.refs_2_.down_ref = bf16[256,7168]{1,0:T(8,128)(2,1)S(1)} custom-call(bf16[256,7168]{1,0:T(8,128)(2,1)} %bitcast.9, bf16[32,2176]{1,0:T(8,128)(2,1)S(1)} %join.6.refs_2_.refs_1_.refs_0_, bf16[32,2176]{1,0:T(8,128)(2,1)S(1)} %join.7.refs_2_.refs_1_), custom_call_target="tpu_custom_call" | custom-call | tf_op jit(solution)/shard_map/fetch/pallas_call | solution.py:159
  18.5 0.5 %gate_up.2 = (f32[64,256]{1,0:T(8,128)S(1)}, f32[64,256]{1,0:T(8,128)S(1)}) custom-call(bf16[7168,256]{1,0:T(8,128)(2,1)S(1)} %get-tuple-element.26.gate_ref, bf16[7168,256]{1,0:T(8,128)(2,1)S(1)} %get-tuple-element.27.up_ref, bf16[32,2176]{1,0:T(8,128)(2,1)S(1)} %join.6.refs_2_.refs_1_.refs_0_, bf16[32,2176]{1,0:T(8,128)(2,1)S(1)} %join.7.refs_2_.refs_1_), custom_call_target="tpu_custom_call" | custom-call | tf_op jit(solution)/shard_map/gate_up/pallas_call | solution.py:254
  18.9 1.3 %collective-permute-done.7.refs_0_ = bf16[32,2176]{1,0:T(8,128)(2,1)S(1)} collective-permute-done((bf16[32,2176]{1,0:T(8,128)(2,1)S(1)}, bf16[32,2176]{1,0:T(8,128)(2,1)S(1)}, u32[]{:S(2)}, u32[]{:S(2)}) %collective-permute-start.7) | collective-permute-done | bytes 139296 | tf_op jit(solution)/shard_map/ppermute | solution.py:24
  20.2 0.0 collective-permute-start.9
  20.2 0.0 collective-permute-done.4.refs_3_
  20.2 0.0 collective-permute-done.3.refs_2_
  20.2 0.8 %gate_up.3 = (f32[64,256]{1,0:T(8,128)S(1)}, f32[64,256]{1,0:T(8,128)S(1)}) custom-call(bf16[7168,256]{1,0:T(8,128)(2,1)S(1)} %get-tuple-element.26.gate_ref, bf16[7168,256]{1,0:T(8,128)(2,1)S(1)} %get-tuple-element.27.up_ref, f32[64,256]{1,0:T(8,128)S(1)} %get-tuple-element.32.refs_1_.refs_0_, f32[64,256]{1,0:T(8,128)S(1)} %get-tuple-element.33.refs_1_, ...), custom_call_target="tpu_custom_call" | custom-call | tf_op jit(solution)/shard_map/gate_up/pallas_call | solution.py:254
  21.0 0.0 collective-permute-done.8.refs_2_.refs_6_
  21.0 0.6 %collective-permute-done.9.refs_3_.refs_7_ = bf16[32,2176]{1,0:T(8,128)(2,1)S(1)} collective-permute-done((bf16[32,2176]{1,0:T(8,128)(2,1)S(1)}, bf16[32,2176]{1,0:T(8,128)(2,1)S(1)}, u32[]{:S(2)}, u32[]{:S(2)}) %collective-permute-start.9) | collective-permute-done | bytes 139296 | tf_op jit(solution)/shard_map/ppermute | solution.py:24
  21.6 0.7 %hidden.1 = (bf16[64,256]{1,0:T(8,128)(2,1)S(1)}, bf16[64,1792]{1,0:T(8,128)(2,1)S(1)}) custom-call(bf16[7168,256]{1,0:T(8,128)(2,1)S(1)} %get-tuple-element.26.gate_ref, bf16[7168,256]{1,0:T(8,128)(2,1)S(1)} %get-tuple-element.27.up_ref, bf16[256,7168]{1,0:T(8,128)(2,1)S(1)} %fetch.3.refs_2_.down_ref, f32[64,256]{1,0:T(8,128)S(1)} %get-tuple-element.34.refs_0_, ...), custom_call_target="tpu_custom_call" | custom-call | tf_op jit(solution)/shard_map/hidden/pallas_call | solution.py:282
  22.3 0.2 collective-permute-start.11
  22.5 0.3 down.3
  22.8 0.4 %collective-permute-start.10 = (bf16[64,1792]{1,0:T(8,128)(2,1)S(1)}, bf16[64,1792]{1,0:T(8,128)(2,1)S(1)}, u32[]{:S(2)}, u32[]{:S(2)}) collective-permute-start(bf16[64,1792]{1,0:T(8,128)(2,1)S(1)} %down.3), channel_id=1, source_target_pairs={{0,1},{1,0},{2,3},{3,2},{4,5},{5,4},{6,7},{7,6},{8,9},{9,8},{10,11... | collective-permute-start | bytes 688136 | tf_op jit(solution)/shard_map/ppermute | solution.py:24
  23.2 0.5 %down.2 = (f32[64,1792]{1,0:T(8,128)S(1)}, f32[64,1792]{1,0:T(8,128)S(1)}) custom-call(bf16[64,256]{1,0:T(8,128)(2,1)S(1)} %get-tuple-element.36.hidden_ref, bf16[256,7168]{1,0:T(8,128)(2,1)S(1)} %fetch.3.refs_2_.down_ref), custom_call_target="tpu_custom_call" | custom-call | flops 234881024 | bytes 3670016 | tf_op jit(solution)/shard_map/down/pallas_call | solution.py:303
  23.6 0.2 collective-permute-done.11.arrived_ref
  23.9 0.7 %collective-permute-start.13 = (bf16[32,1792]{1,0:T(8,128)(2,1)S(1)}, bf16[32,1792]{1,0:T(8,128)(2,1)S(1)}, u32[]{:S(2)}, u32[]{:S(2)}) collective-permute-start(bf16[32,1792]{1,0:T(8,128)(2,1)S(1)} %get-tuple-element.43), channel_id=1, source_target_pairs={{0,2},{1,3},{2,0},{3,1},{4,6},{5,7},{6,4},{7,5},{8,10},{9,11},{10,... | collective-permute-start | bytes 344072 | tf_op jit(solution)/shard_map/ppermute | solution.py:24
  24.6 1.4 %collective-permute-start.12 = (bf16[16,1792]{1,0:T(8,128)(2,1)S(1)}, bf16[16,1792]{1,0:T(8,128)(2,1)S(1)}, u32[]{:S(2)}, u32[]{:S(2)}) collective-permute-start(bf16[16,1792]{1,0:T(8,128)(2,1)S(1)} %get-tuple-element.41), channel_id=1, source_target_pairs={{0,2},{1,3},{2,0},{3,1},{4,6},{5,7},{6,4},{7,5},{8,10},{9,11},{10,... | collective-permute-start | bytes 172040 | tf_op jit(solution)/shard_map/ppermute | solution.py:24
  26.0 3.0 %collective-permute-start.17 = (bf16[16,1792]{1,0:T(8,128)(2,1)S(1)}, bf16[16,1792]{1,0:T(8,128)(2,1)S(1)}, u32[]{:S(2)}, u32[]{:S(2)}) collective-permute-start(bf16[16,1792]{1,0:T(8,128)(2,1)S(1)} %get-tuple-element.47), channel_id=1, source_target_pairs={{0,14},{1,15},{2,12},{3,13},{4,10},{5,11},{6,8},{7,9},{8,6},{9,7},... | collective-permute-start | bytes 172040 | tf_op jit(solution)/shard_map/ppermute | solution.py:34
  29.0 0.0 collective-permute-done.10.arrived_ref
  29.0 1.0 %collective-permute-start.16 = (bf16[16,1792]{1,0:T(8,128)(2,1)S(1)}, bf16[16,1792]{1,0:T(8,128)(2,1)S(1)}, u32[]{:S(2)}, u32[]{:S(2)}) collective-permute-start(bf16[16,1792]{1,0:T(8,128)(2,1)S(1)} %get-tuple-element.46), channel_id=1, source_target_pairs={{0,12},{4,8},{8,4},{12,0},{1,13},{5,9},{9,5},{13,1},{2,14},{6,10},... | collective-permute-start | bytes 172040 | tf_op jit(solution)/shard_map/ppermute | solution.py:24
  30.0 0.0 collective-permute-done.13.arrived_ref
  30.0 0.6 %collective-permute-start.14 = (bf16[16,1792]{1,0:T(8,128)(2,1)S(1)}, bf16[16,1792]{1,0:T(8,128)(2,1)S(1)}, u32[]{:S(2)}, u32[]{:S(2)}) collective-permute-start(bf16[16,1792]{1,0:T(8,128)(2,1)S(1)} %get-tuple-element.44), channel_id=1, source_target_pairs={{0,4},{4,0},{8,12},{12,8},{1,5},{5,1},{9,13},{13,9},{2,6},{6,2},{1... | collective-permute-start | bytes 172040 | tf_op jit(solution)/shard_map/ppermute | solution.py:24
  30.6 3.0 %collective-permute-start.15 = (bf16[16,1792]{1,0:T(8,128)(2,1)S(1)}, bf16[16,1792]{1,0:T(8,128)(2,1)S(1)}, u32[]{:S(2)}, u32[]{:S(2)}) collective-permute-start(bf16[16,1792]{1,0:T(8,128)(2,1)S(1)} %get-tuple-element.45), channel_id=1, source_target_pairs={{0,8},{4,12},{8,0},{12,4},{1,9},{5,13},{9,1},{13,5},{2,10},{6,14},... | collective-permute-start | bytes 172040 | tf_op jit(solution)/shard_map/ppermute | solution.py:24
  33.6 2.0 %attend.1 = bf16[64,512]{1,0:T(8,128)(2,1)} custom-call(s32[4,4]{1,0:T(4,128)} %dest_ref.1, s32[16]{0:T(128)} %len_ref.1, bf16[64,576]{1,0:T(8,128)(2,1)} %bitcast.10, bf16[32,2176]{1,0:T(8,128)(2,1)S(1)} %join.6.refs_2_.refs_1_.refs_0_, bf16[32,2176]{1,0:T(8,128)(2,1)S(1)} %join.7.refs_2_.refs_1_, bf16[32,2176]{1,0:T(8,128)(2,1)S(1)} %collective-permute-done.3.refs_2_, ...), custom_call_target="tpu_custom_call" | custom-call | flops 234881024 | bytes 3670016 | tf_op jit(solution)/shard_map/attend/pallas_call | solution.py:464
  35.5 0.0 collective-permute-done.12.arrived_ref
  35.6 0.0 collective-permute-done.17.refs_4_
  35.6 0.0 collective-permute-done.16.refs_3_
  35.6 0.0 collective-permute-done.14.refs_1_
  35.6 0.9 %collective-permute-done.15.refs_2_ = bf16[16,1792]{1,0:T(8,128)(2,1)S(1)} collective-permute-done((bf16[16,1792]{1,0:T(8,128)(2,1)S(1)}, bf16[16,1792]{1,0:T(8,128)(2,1)S(1)}, u32[]{:S(2)}, u32[]{:S(2)}) %collective-permute-start.15) | collective-permute-done | bytes 57376 | tf_op jit(solution)/shard_map/ppermute | solution.py:24
  36.5 1.2 %combine.1 = bf16[256,1792]{1,0:T(8,128)(2,1)} custom-call(bf16[256,128]{1,0:T(8,128)(2,1)S(1)} %get-tuple-element.25.refs_2_.table_ref, bf16[16,1792]{1,0:T(8,128)(2,1)S(1)} %total.6.refs_0_, bf16[16,1792]{1,0:T(8,128)(2,1)S(1)} %collective-permute-done.14.refs_1_, bf16[16,1792]{1,0:T(8,128)(2,1)S(1)} %collective-permute-done.15.refs_2_, ...), custom_call_target="tpu_custom_call" | custom-call | flops 117440512 | bytes 917504 | tf_op jit(solution)/shard_map/combine/pallas_call | solution.py:381
  (11 shorter events, 0.2 us)
Async XLA Ops:
  2.2 11.9 %collective-permute-start.6 = (bf16[16,2176]{1,0:T(8,128)(2,1)S(1)}, bf16[16,2176]{1,0:T(8,128)(2,1)S(1)}, u32[]{:S(2)}, u32[]{:S(2)}) collective-permute-start(bf16[16,2176]{1,0:T(8,128)(2,1)S(1)} %get-tuple-element.29), channel_id=1, source_target_pairs={{0,6},{1,7},{2,4},{3,5},{4,2},{5,3},{6,0},{7,1},{8,14},{9,15},{10,... | collective-permute-start | bytes 208904 | tf_op jit(solution)/shard_map/ppermute | solution.py:34
  6.2 7.9 %collective-permute-start.1 = (bf16[16,2176]{1,0:T(8,128)(2,1)S(1)}, bf16[16,2176]{1,0:T(8,128)(2,1)S(1)}, u32[]{:S(2)}, u32[]{:S(2)}) collective-permute-start(bf16[16,2176]{1,0:T(8,128)(2,1)S(1)} %get-tuple-element.30), channel_id=1, source_target_pairs={{0,8},{4,12},{8,0},{12,4},{1,9},{5,13},{9,1},{13,5},{2,10},{6,14},... | collective-permute-start | bytes 208904 | tf_op jit(solution)/shard_map/ppermute | solution.py:24
  8.8 6.2 %collective-permute-start.2 = (bf16[16,2176]{1,0:T(8,128)(2,1)S(1)}, bf16[16,2176]{1,0:T(8,128)(2,1)S(1)}, u32[]{:S(2)}, u32[]{:S(2)}) collective-permute-start(bf16[16,2176]{1,0:T(8,128)(2,1)S(1)} %get-tuple-element.31), channel_id=1, source_target_pairs={{0,12},{4,8},{8,4},{12,0},{1,13},{5,9},{9,5},{13,1},{2,14},{6,10},... | collective-permute-start | bytes 208904 | tf_op jit(solution)/shard_map/ppermute | solution.py:24
  9.0 6.0 %collective-permute-start = (bf16[16,2176]{1,0:T(8,128)(2,1)S(1)}, bf16[16,2176]{1,0:T(8,128)(2,1)S(1)}, u32[]{:S(2)}, u32[]{:S(2)}) collective-permute-start(bf16[16,2176]{1,0:T(8,128)(2,1)S(1)} %get-tuple-element.29), channel_id=1, source_target_pairs={{0,4},{4,0},{8,12},{12,8},{1,5},{5,1},{9,13},{13,9},{2,6},{6,2},{1... | collective-permute-start | bytes 208904 | tf_op jit(solution)/shard_map/ppermute | solution.py:24
  9.7 5.4 %collective-permute-start.5 = (bf16[16,2176]{1,0:T(8,128)(2,1)S(1)}, bf16[16,2176]{1,0:T(8,128)(2,1)S(1)}, u32[]{:S(2)}, u32[]{:S(2)}) collective-permute-start(bf16[16,2176]{1,0:T(8,128)(2,1)S(1)} %get-tuple-element.28.refs_0_), channel_id=1, source_target_pairs={{0,2},{1,3},{2,0},{3,1},{4,6},{5,7},{6,4},{7,5},{8,10},{9,11},{10,... | collective-permute-start | bytes 208904 | tf_op jit(solution)/shard_map/ppermute | solution.py:24
  15.1 5.1 %collective-permute-start.7 = (bf16[32,2176]{1,0:T(8,128)(2,1)S(1)}, bf16[32,2176]{1,0:T(8,128)(2,1)S(1)}, u32[]{:S(2)}, u32[]{:S(2)}) collective-permute-start(bf16[32,2176]{1,0:T(8,128)(2,1)S(1)} %tie.2), channel_id=1, source_target_pairs={{0,2},{1,3},{2,0},{3,1},{4,6},{5,7},{6,4},{7,5},{8,10},{9,11},{10,... | collective-permute-start | bytes 417800 | tf_op jit(solution)/shard_map/ppermute | solution.py:24
  15.8 4.4 %collective-permute-start.3 = (bf16[32,2176]{1,0:T(8,128)(2,1)S(1)}, bf16[32,2176]{1,0:T(8,128)(2,1)S(1)}, u32[]{:S(2)}, u32[]{:S(2)}) collective-permute-start(bf16[32,2176]{1,0:T(8,128)(2,1)S(1)} %join.6.refs_2_.refs_1_.refs_0_), channel_id=1, source_target_pairs={{0,1},{1,0},{2,3},{3,2},{4,5},{5,4},{6,7},{7,6},{8,9},{9,8},{10,11... | collective-permute-start | bytes 417800 | tf_op jit(solution)/shard_map/ppermute | solution.py:24
  15.8 5.2 %collective-permute-start.8 = (bf16[32,2176]{1,0:T(8,128)(2,1)S(1)}, bf16[32,2176]{1,0:T(8,128)(2,1)S(1)}, u32[]{:S(2)}, u32[]{:S(2)}) collective-permute-start(bf16[32,2176]{1,0:T(8,128)(2,1)S(1)} %join.9.refs_4_), channel_id=1, source_target_pairs={{0,1},{1,0},{2,3},{3,2},{4,5},{5,4},{6,7},{7,6},{8,9},{9,8},{10,11... | collective-permute-start | bytes 417800 | tf_op jit(solution)/shard_map/ppermute | solution.py:24
  16.3 3.9 %collective-permute-start.4 = (bf16[32,2176]{1,0:T(8,128)(2,1)S(1)}, bf16[32,2176]{1,0:T(8,128)(2,1)S(1)}, u32[]{:S(2)}, u32[]{:S(2)}) collective-permute-start(bf16[32,2176]{1,0:T(8,128)(2,1)S(1)} %join.7.refs_2_.refs_1_), channel_id=1, source_target_pairs={{0,1},{1,0},{2,3},{3,2},{4,5},{5,4},{6,7},{7,6},{8,9},{9,8},{10,11... | collective-permute-start | bytes 417800 | tf_op jit(solution)/shard_map/ppermute | solution.py:24
  20.2 1.4 %collective-permute-start.9 = (bf16[32,2176]{1,0:T(8,128)(2,1)S(1)}, bf16[32,2176]{1,0:T(8,128)(2,1)S(1)}, u32[]{:S(2)}, u32[]{:S(2)}) collective-permute-start(bf16[32,2176]{1,0:T(8,128)(2,1)S(1)} %tie.3.refs_5_), channel_id=1, source_target_pairs={{0,1},{1,0},{2,3},{3,2},{4,5},{5,4},{6,7},{7,6},{8,9},{9,8},{10,11... | collective-permute-start | bytes 417800 | tf_op jit(solution)/shard_map/ppermute | solution.py:24
  22.3 1.5 %collective-permute-start.11 = (bf16[64,1792]{1,0:T(8,128)(2,1)S(1)}, bf16[64,1792]{1,0:T(8,128)(2,1)S(1)}, u32[]{:S(2)}, u32[]{:S(2)}) collective-permute-start(bf16[64,1792]{1,0:T(8,128)(2,1)S(1)} %get-tuple-element.40), channel_id=1, source_target_pairs={{0,1},{1,0},{2,3},{3,2},{4,5},{5,4},{6,7},{7,6},{8,9},{9,8},{10,11... | collective-permute-start | bytes 688136 | tf_op jit(solution)/shard_map/ppermute | solution.py:24
  22.8 6.2 %collective-permute-start.10 = (bf16[64,1792]{1,0:T(8,128)(2,1)S(1)}, bf16[64,1792]{1,0:T(8,128)(2,1)S(1)}, u32[]{:S(2)}, u32[]{:S(2)}) collective-permute-start(bf16[64,1792]{1,0:T(8,128)(2,1)S(1)} %down.3), channel_id=1, source_target_pairs={{0,1},{1,0},{2,3},{3,2},{4,5},{5,4},{6,7},{7,6},{8,9},{9,8},{10,11... | collective-permute-start | bytes 688136 | tf_op jit(solution)/shard_map/ppermute | solution.py:24
  23.9 6.1 %collective-permute-start.13 = (bf16[32,1792]{1,0:T(8,128)(2,1)S(1)}, bf16[32,1792]{1,0:T(8,128)(2,1)S(1)}, u32[]{:S(2)}, u32[]{:S(2)}) collective-permute-start(bf16[32,1792]{1,0:T(8,128)(2,1)S(1)} %get-tuple-element.43), channel_id=1, source_target_pairs={{0,2},{1,3},{2,0},{3,1},{4,6},{5,7},{6,4},{7,5},{8,10},{9,11},{10,... | collective-permute-start | bytes 344072 | tf_op jit(solution)/shard_map/ppermute | solution.py:24
  24.6 11.0 %collective-permute-start.12 = (bf16[16,1792]{1,0:T(8,128)(2,1)S(1)}, bf16[16,1792]{1,0:T(8,128)(2,1)S(1)}, u32[]{:S(2)}, u32[]{:S(2)}) collective-permute-start(bf16[16,1792]{1,0:T(8,128)(2,1)S(1)} %get-tuple-element.41), channel_id=1, source_target_pairs={{0,2},{1,3},{2,0},{3,1},{4,6},{5,7},{6,4},{7,5},{8,10},{9,11},{10,... | collective-permute-start | bytes 172040 | tf_op jit(solution)/shard_map/ppermute | solution.py:24
  26.0 9.6 %collective-permute-start.17 = (bf16[16,1792]{1,0:T(8,128)(2,1)S(1)}, bf16[16,1792]{1,0:T(8,128)(2,1)S(1)}, u32[]{:S(2)}, u32[]{:S(2)}) collective-permute-start(bf16[16,1792]{1,0:T(8,128)(2,1)S(1)} %get-tuple-element.47), channel_id=1, source_target_pairs={{0,14},{1,15},{2,12},{3,13},{4,10},{5,11},{6,8},{7,9},{8,6},{9,7},... | collective-permute-start | bytes 172040 | tf_op jit(solution)/shard_map/ppermute | solution.py:34
  29.0 6.5 %collective-permute-start.16 = (bf16[16,1792]{1,0:T(8,128)(2,1)S(1)}, bf16[16,1792]{1,0:T(8,128)(2,1)S(1)}, u32[]{:S(2)}, u32[]{:S(2)}) collective-permute-start(bf16[16,1792]{1,0:T(8,128)(2,1)S(1)} %get-tuple-element.46), channel_id=1, source_target_pairs={{0,12},{4,8},{8,4},{12,0},{1,13},{5,9},{9,5},{13,1},{2,14},{6,10},... | collective-permute-start | bytes 172040 | tf_op jit(solution)/shard_map/ppermute | solution.py:24
  30.0 5.6 %collective-permute-start.14 = (bf16[16,1792]{1,0:T(8,128)(2,1)S(1)}, bf16[16,1792]{1,0:T(8,128)(2,1)S(1)}, u32[]{:S(2)}, u32[]{:S(2)}) collective-permute-start(bf16[16,1792]{1,0:T(8,128)(2,1)S(1)} %get-tuple-element.44), channel_id=1, source_target_pairs={{0,4},{4,0},{8,12},{12,8},{1,5},{5,1},{9,13},{13,9},{2,6},{6,2},{1... | collective-permute-start | bytes 172040 | tf_op jit(solution)/shard_map/ppermute | solution.py:24
  30.6 5.9 %collective-permute-start.15 = (bf16[16,1792]{1,0:T(8,128)(2,1)S(1)}, bf16[16,1792]{1,0:T(8,128)(2,1)S(1)}, u32[]{:S(2)}, u32[]{:S(2)}) collective-permute-start(bf16[16,1792]{1,0:T(8,128)(2,1)S(1)} %get-tuple-element.45), channel_id=1, source_target_pairs={{0,8},{4,12},{8,0},{12,4},{1,9},{5,13},{9,1},{13,5},{2,10},{6,14},... | collective-permute-start | bytes 172040 | tf_op jit(solution)/shard_map/ppermute | solution.py:24

commit v7 on v6

--- a/solution.py
+++ b/solution.py
@@ -132,8 +132,15 @@
 
 
 def fetch_kernel(ep_count, count, skip, *refs):
-    sources, outs, sems = refs[:count], refs[skip:-1], refs[-1]
+    routing = refs[-4:-1] if ep_count else ()
+    sources, outs, sems = refs[:count], refs[skip : -1 - len(routing)], refs[-1]
     cuts, copies = sems.shape[1], []
+    small = [
+        pltpu.make_async_copy(refs[count + i], routing[i], routing[2].at[i])
+        for i in range(2 if routing else 0)
+    ]
+    for copy in small:
+        copy.start()
     for i in range(count):
         rows = sources[i].shape[0] // cuts
         for c in range(cuts):
@@ -144,8 +151,9 @@
     for copy in copies:
         copy.start()
     if len(outs) > count:
-        ids_ref, gates_ref = refs[count : count + 2]
-        outs[-1][...] = gate_table(ids_ref[...], gates_ref[...], ep_count)
+        for copy in small:
+            copy.wait()
+        outs[-1][...] = gate_table(routing[0][...], routing[1][...], ep_count)
     for copy in copies:
         copy.wait()
 
@@ -153,15 +161,16 @@
 def fetch(arrays, after=(), routing=(), ep_count=0):
     operands = [in_hbm(a) for a in [*arrays, *routing]]
     out_shape = [pltpu.VMEM(a.shape, a.dtype) for a in arrays]
-    table = []
+    table, scratch = [], []
     if routing:
+        scratch = [pltpu.VMEM(a.shape, a.dtype) for a in routing] + [pltpu.SemaphoreType.DMA((2,))]
         table = [jax.ShapeDtypeStruct((routing[0].shape[1], 2 * ep_count * CAP), bf16)]
     return pl.pallas_call(
         functools.partial(fetch_kernel, ep_count, len(arrays), len(operands) + len(after)),
         out_shape=out_shape + table,
-        in_specs=[HBM] * len(arrays) + [VMEM] * len(routing) + [ANY] * len(after),
+        in_specs=[HBM] * len(operands) + [ANY] * len(after),
         out_specs=[VMEM] * len(out_shape + table),
-        scratch_shapes=[pltpu.SemaphoreType.DMA((len(arrays), 4))],
+        scratch_shapes=scratch + [pltpu.SemaphoreType.DMA((len(arrays), 4))],
         compiler_params=params(table * 4, 1 << 20),
         cost_estimate=cost(0, 0),
         name="fetch",
@@ -430,9 +439,9 @@
     rest = join([arrived[d] for d in staged], [table])
 
     pieces = {0: [join([arrived[d] for d in [0, *direct]], [rest])], bit: [join(over, [rest])]}
-    pieces[bit] += [swap(tie(rest, pieces[0] + over[1:]), "pd", bit)]
+    pieces[bit] += [swap(tie(rest, pieces[0]), "pd", bit)]
     pieces[0] += [join([arrived[d] for d in staged], pieces[0])]
-    (w_down,) = fetch([down_weight[0]], pieces[0])
+    (w_down,) = fetch([down_weight[0]], [*pieces[0], *over[1:]])
     spread(pieces, 0, bit // 2)
     sums = gate_up([0], width, w_gate, w_up, pieces)
     pieces[bit][-1] = tie(pieces[bit][-1], [sums[0], w_down])

time: 38 us -> 37.8 us (level)
  waiting for transfers between devices: 3.82 us -> 4.86 us
  Pallas kernels: 13.5 us -> 12.8 us
  starting transfers between devices: 19.6 us -> 19.1 us
    ppermute x16, waiting for transfers between devices: 3.81 us -> 4.85 us  [swap(): return lax.ppermute(value, axis, [(i, i ^ mask) for i in range(count)])]
    pallas_call x2, Pallas kernels: 5.93 us -> 5.25 us  [fetch(): pl.pallas_call(functools.partial(fetch_kernel, ep_count, len(arrays), len...]
    ppermute x2, starting transfers between devices: 7.03 us -> 6.64 us  [swap_both(): return lax.ppermute(value, ('ep', 'pd'), pairs)]
  transfers between devices with their start and end apart: 18 -> 18, of which waited for: 5 -> 6; matrix products, arithmetic and copies ran while one was open for 0% -> 0% of each run, Pallas kernels for 27% -> 25%
where the time goes in v7:
time: 37.8 us; the launch traced here: 37.5 us
  starting transfers between devices  19.1 us (51%)
  Pallas kernels  12.8 us (34%)
  waiting for transfers between devices  4.86 us (13%)
  between operations  0.8 us (2%)
    ppermute x16, starting transfers between devices, swap(): return lax.ppermute(value, axis, [(i, i ^ mask) for i in range(count)])  12.4 us
    ppermute x2, starting transfers between devices, swap_both(): return lax.ppermute(value, ('ep', 'pd'), pairs)  6.64 us
    pallas_call x2, Pallas kernels, fetch(): pl.pallas_call(functools.partial(fetch_kernel, ep_count, len(arrays), len...  5.25 us
    ppermute x16, waiting for transfers between devices, swap(): return lax.ppermute(value, axis, [(i, i ^ mask) for i in range(count)])  4.85 us
    pallas_call x1, Pallas kernels, on_device(): pl.pallas_call(functools.partial(attend_kernel, order, pd_count, width),...  1.96 us
    pallas_call x1, Pallas kernels, route(): pl.pallas_call(functools.partial(route_kernel, ep_count), out_shape=out_s...  1.56 us
    pallas_call x1, Pallas kernels, mix(): pl.pallas_call(functools.partial(combine_kernel, cuts, [len(block) for bl...  1.22 us
    pallas_call x2, Pallas kernels, gate_up(): pl.pallas_call(functools.partial(gate_up_kernel, masks, width, bool(befor...  1.21 us
  transfers between devices with their start and end apart: 18, of which 6 were waited for; matrix products, arithmetic and copies ran while one was open for 0% of the time, Pallas kernels for 25%

profile of v7, /device:TPU:0, one launch (start us, length us, event | category | flops | bytes accessed | tf_op | source)
XLA Modules:
  0.0 37.5 jit_solution(4103845033146158314)
XLA Ops:
  0.6 1.6 %route.1 = (bf16[16,2176]{1,0:T(8,128)(2,1)S(1)}, bf16[16,2176]{1,0:T(8,128)(2,1)S(1)}, bf16[16,2176]{1,0:T(8,128)(2,1)S(1)}, bf16[16,2176]{1,0:T(8,128)(2,1)S(1)}) custom-call(s32[8,256]{1,0:T(8,128)} %bitcast.12, s32[4,4]{1,0:T(4,128)} %dest_ref.1, bf16[4,8,576]{2,1,0:T(8,128)(2,1)} %refs_2_.1, bf16[256,1792]{1,0:T(8,128)(2,1)} %refs_3_.1), custom_call_target="tpu_custom_call" | custom-call | flops 117440512 | bytes 917504 | tf_op jit(solution)/shard_map/route/pallas_call | solution.py:108
  2.2 4.0 %collective-permute-start.3 = (bf16[16,2176]{1,0:T(8,128)(2,1)S(1)}, bf16[16,2176]{1,0:T(8,128)(2,1)S(1)}, u32[]{:S(2)}, u32[]{:S(2)}) collective-permute-start(bf16[16,2176]{1,0:T(8,128)(2,1)S(1)} %get-tuple-element.29), channel_id=1, source_target_pairs={{0,6},{1,7},{2,4},{3,5},{4,2},{5,3},{6,0},{7,1},{8,14},{9,15},{10,... | collective-permute-start | bytes 208904 | tf_op jit(solution)/shard_map/ppermute | solution.py:34
  6.2 2.6 %collective-permute-start.1 = (bf16[16,2176]{1,0:T(8,128)(2,1)S(1)}, bf16[16,2176]{1,0:T(8,128)(2,1)S(1)}, u32[]{:S(2)}, u32[]{:S(2)}) collective-permute-start(bf16[16,2176]{1,0:T(8,128)(2,1)S(1)} %get-tuple-element.30), channel_id=1, source_target_pairs={{0,8},{4,12},{8,0},{12,4},{1,9},{5,13},{9,1},{13,5},{2,10},{6,14},... | collective-permute-start | bytes 208904 | tf_op jit(solution)/shard_map/ppermute | solution.py:24
  8.8 0.2 collective-permute-start.2
  9.0 0.7 %collective-permute-start = (bf16[16,2176]{1,0:T(8,128)(2,1)S(1)}, bf16[16,2176]{1,0:T(8,128)(2,1)S(1)}, u32[]{:S(2)}, u32[]{:S(2)}) collective-permute-start(bf16[16,2176]{1,0:T(8,128)(2,1)S(1)} %get-tuple-element.29), channel_id=1, source_target_pairs={{0,4},{4,0},{8,12},{12,8},{1,5},{5,1},{9,13},{13,9},{2,6},{6,2},{1... | collective-permute-start | bytes 208904 | tf_op jit(solution)/shard_map/ppermute | solution.py:24
  9.7 0.5 %collective-permute-start.6 = (bf16[16,2176]{1,0:T(8,128)(2,1)S(1)}, bf16[16,2176]{1,0:T(8,128)(2,1)S(1)}, u32[]{:S(2)}, u32[]{:S(2)}) collective-permute-start(bf16[16,2176]{1,0:T(8,128)(2,1)S(1)} %get-tuple-element.28.refs_0_), channel_id=1, source_target_pairs={{0,2},{1,3},{2,0},{3,1},{4,6},{5,7},{6,4},{7,5},{8,10},{9,11},{10,... | collective-permute-start | bytes 208904 | tf_op jit(solution)/shard_map/ppermute | solution.py:24
  10.2 3.2 %fetch.2 = (bf16[7168,256]{1,0:T(8,128)(2,1)S(1)}, bf16[7168,256]{1,0:T(8,128)(2,1)S(1)}, bf16[256,128]{1,0:T(8,128)(2,1)S(1)}) custom-call(bf16[7168,256]{1,0:T(8,128)(2,1)} %bitcast.7, bf16[7168,256]{1,0:T(8,128)(2,1)} %bitcast.8, s32[8,256]{1,0:T(8,128)} %bitcast.13, f32[8,256]{1,0:T(8,128)} %bitcast.14), custom_call_target="tpu_custom_call" | custom-call | tf_op jit(solution)/shard_map/fetch/pallas_call | solution.py:168
  13.4 0.0 collective-permute-done.3.refs_0_
  13.5 0.3 collective-permute-done.1.refs_0_
  13.7 1.3 %collective-permute-done.2.refs_1_ = bf16[16,2176]{1,0:T(8,128)(2,1)S(1)} collective-permute-done((bf16[16,2176]{1,0:T(8,128)(2,1)S(1)}, bf16[16,2176]{1,0:T(8,128)(2,1)S(1)}, u32[]{:S(2)}, u32[]{:S(2)}) %collective-permute-start.2) | collective-permute-done | bytes 69664 | tf_op jit(solution)/shard_map/ppermute | solution.py:24
  15.0 0.0 collective-permute-done.refs_1_
  15.1 0.0 collective-permute-done.6.refs_0_
  15.1 0.6 %collective-permute-start.7 = (bf16[32,2176]{1,0:T(8,128)(2,1)S(1)}, bf16[32,2176]{1,0:T(8,128)(2,1)S(1)}, u32[]{:S(2)}, u32[]{:S(2)}) collective-permute-start(bf16[32,2176]{1,0:T(8,128)(2,1)S(1)} %tie.2), channel_id=1, source_target_pairs={{0,2},{1,3},{2,0},{3,1},{4,6},{5,7},{6,4},{7,5},{8,10},{9,11},{10,... | collective-permute-start | bytes 417800 | tf_op jit(solution)/shard_map/ppermute | solution.py:24
  15.7 0.0 collective-permute-start.4
  15.7 0.5 %collective-permute-start.8 = (bf16[32,2176]{1,0:T(8,128)(2,1)S(1)}, bf16[32,2176]{1,0:T(8,128)(2,1)S(1)}, u32[]{:S(2)}, u32[]{:S(2)}) collective-permute-start(bf16[32,2176]{1,0:T(8,128)(2,1)S(1)} %join.9.refs_4_), channel_id=1, source_target_pairs={{0,1},{1,0},{2,3},{3,2},{4,5},{5,4},{6,7},{7,6},{8,9},{9,8},{10,11... | collective-permute-start | bytes 417800 | tf_op jit(solution)/shard_map/ppermute | solution.py:24
  16.2 0.1 collective-permute-start.5
  16.3 2.0 %fetch.3.refs_2_.down_ref = bf16[256,7168]{1,0:T(8,128)(2,1)S(1)} custom-call(bf16[256,7168]{1,0:T(8,128)(2,1)} %bitcast.9, bf16[32,2176]{1,0:T(8,128)(2,1)S(1)} %join.6.refs_2_.refs_1_.refs_0_, bf16[32,2176]{1,0:T(8,128)(2,1)S(1)} %join.7.refs_2_.refs_1_, bf16[16,2176]{1,0:T(8,128)(2,1)S(1)} %join.8.refs_3_.refs_1_), custom_call_target="tpu_custom_call" | custom-call | tf_op jit(solution)/shard_map/fetch/pallas_call | solution.py:168
  18.4 0.5 %gate_up.2 = (f32[64,256]{1,0:T(8,128)S(1)}, f32[64,256]{1,0:T(8,128)S(1)}) custom-call(bf16[7168,256]{1,0:T(8,128)(2,1)S(1)} %get-tuple-element.26.gate_ref, bf16[7168,256]{1,0:T(8,128)(2,1)S(1)} %get-tuple-element.27.up_ref, bf16[32,2176]{1,0:T(8,128)(2,1)S(1)} %join.6.refs_2_.refs_1_.refs_0_, bf16[32,2176]{1,0:T(8,128)(2,1)S(1)} %join.7.refs_2_.refs_1_), custom_call_target="tpu_custom_call" | custom-call | tf_op jit(solution)/shard_map/gate_up/pallas_call | solution.py:263
  18.8 1.4 %collective-permute-done.7.refs_0_ = bf16[32,2176]{1,0:T(8,128)(2,1)S(1)} collective-permute-done((bf16[32,2176]{1,0:T(8,128)(2,1)S(1)}, bf16[32,2176]{1,0:T(8,128)(2,1)S(1)}, u32[]{:S(2)}, u32[]{:S(2)}) %collective-permute-start.7) | collective-permute-done | bytes 139296 | tf_op jit(solution)/shard_map/ppermute | solution.py:24
  20.2 0.0 collective-permute-start.9
  20.2 0.0 collective-permute-done.5.refs_3_
  20.2 0.0 collective-permute-done.4.refs_2_
  20.2 0.8 %gate_up.3 = (f32[64,256]{1,0:T(8,128)S(1)}, f32[64,256]{1,0:T(8,128)S(1)}) custom-call(bf16[7168,256]{1,0:T(8,128)(2,1)S(1)} %get-tuple-element.26.gate_ref, bf16[7168,256]{1,0:T(8,128)(2,1)S(1)} %get-tuple-element.27.up_ref, f32[64,256]{1,0:T(8,128)S(1)} %get-tuple-element.32.refs_1_.refs_0_, f32[64,256]{1,0:T(8,128)S(1)} %get-tuple-element.33.refs_1_, ...), custom_call_target="tpu_custom_call" | custom-call | tf_op jit(solution)/shard_map/gate_up/pallas_call | solution.py:263
  21.0 0.0 collective-permute-done.8.refs_2_.refs_6_
  21.0 0.6 %collective-permute-done.9.refs_3_.refs_7_ = bf16[32,2176]{1,0:T(8,128)(2,1)S(1)} collective-permute-done((bf16[32,2176]{1,0:T(8,128)(2,1)S(1)}, bf16[32,2176]{1,0:T(8,128)(2,1)S(1)}, u32[]{:S(2)}, u32[]{:S(2)}) %collective-permute-start.9) | collective-permute-done | bytes 139296 | tf_op jit(solution)/shard_map/ppermute | solution.py:24
  21.6 0.7 %hidden.1 = (bf16[64,256]{1,0:T(8,128)(2,1)S(1)}, bf16[64,1792]{1,0:T(8,128)(2,1)S(1)}) custom-call(bf16[7168,256]{1,0:T(8,128)(2,1)S(1)} %get-tuple-element.26.gate_ref, bf16[7168,256]{1,0:T(8,128)(2,1)S(1)} %get-tuple-element.27.up_ref, bf16[256,7168]{1,0:T(8,128)(2,1)S(1)} %fetch.3.refs_2_.down_ref, f32[64,256]{1,0:T(8,128)S(1)} %get-tuple-element.34.refs_0_, ...), custom_call_target="tpu_custom_call" | custom-call | tf_op jit(solution)/shard_map/hidden/pallas_call | solution.py:291
  22.3 0.2 collective-permute-start.11
  22.5 0.3 down.3
  22.8 0.4 %collective-permute-start.10 = (bf16[64,1792]{1,0:T(8,128)(2,1)S(1)}, bf16[64,1792]{1,0:T(8,128)(2,1)S(1)}, u32[]{:S(2)}, u32[]{:S(2)}) collective-permute-start(bf16[64,1792]{1,0:T(8,128)(2,1)S(1)} %down.3), channel_id=1, source_target_pairs={{0,1},{1,0},{2,3},{3,2},{4,5},{5,4},{6,7},{7,6},{8,9},{9,8},{10,11... | collective-permute-start | bytes 688136 | tf_op jit(solution)/shard_map/ppermute | solution.py:24
  23.2 0.5 %down.2 = (f32[64,1792]{1,0:T(8,128)S(1)}, f32[64,1792]{1,0:T(8,128)S(1)}) custom-call(bf16[64,256]{1,0:T(8,128)(2,1)S(1)} %get-tuple-element.36.hidden_ref, bf16[256,7168]{1,0:T(8,128)(2,1)S(1)} %fetch.3.refs_2_.down_ref), custom_call_target="tpu_custom_call" | custom-call | flops 234881024 | bytes 3670016 | tf_op jit(solution)/shard_map/down/pallas_call | solution.py:312
  23.6 0.2 collective-permute-done.11.arrived_ref
  23.9 0.6 %collective-permute-start.13 = (bf16[32,1792]{1,0:T(8,128)(2,1)S(1)}, bf16[32,1792]{1,0:T(8,128)(2,1)S(1)}, u32[]{:S(2)}, u32[]{:S(2)}) collective-permute-start(bf16[32,1792]{1,0:T(8,128)(2,1)S(1)} %get-tuple-element.43), channel_id=1, source_target_pairs={{0,2},{1,3},{2,0},{3,1},{4,6},{5,7},{6,4},{7,5},{8,10},{9,11},{10,... | collective-permute-start | bytes 344072 | tf_op jit(solution)/shard_map/ppermute | solution.py:24
  24.5 1.5 %collective-permute-start.12 = (bf16[16,1792]{1,0:T(8,128)(2,1)S(1)}, bf16[16,1792]{1,0:T(8,128)(2,1)S(1)}, u32[]{:S(2)}, u32[]{:S(2)}) collective-permute-start(bf16[16,1792]{1,0:T(8,128)(2,1)S(1)} %get-tuple-element.41), channel_id=1, source_target_pairs={{0,2},{1,3},{2,0},{3,1},{4,6},{5,7},{6,4},{7,5},{8,10},{9,11},{10,... | collective-permute-start | bytes 172040 | tf_op jit(solution)/shard_map/ppermute | solution.py:24
  26.0 2.6 %collective-permute-start.17 = (bf16[16,1792]{1,0:T(8,128)(2,1)S(1)}, bf16[16,1792]{1,0:T(8,128)(2,1)S(1)}, u32[]{:S(2)}, u32[]{:S(2)}) collective-permute-start(bf16[16,1792]{1,0:T(8,128)(2,1)S(1)} %get-tuple-element.47), channel_id=1, source_target_pairs={{0,14},{1,15},{2,12},{3,13},{4,10},{5,11},{6,8},{7,9},{8,6},{9,7},... | collective-permute-start | bytes 172040 | tf_op jit(solution)/shard_map/ppermute | solution.py:34
  28.6 0.0 collective-permute-done.10.arrived_ref
  28.6 1.2 %collective-permute-start.16 = (bf16[16,1792]{1,0:T(8,128)(2,1)S(1)}, bf16[16,1792]{1,0:T(8,128)(2,1)S(1)}, u32[]{:S(2)}, u32[]{:S(2)}) collective-permute-start(bf16[16,1792]{1,0:T(8,128)(2,1)S(1)} %get-tuple-element.46), channel_id=1, source_target_pairs={{0,12},{4,8},{8,4},{12,0},{1,13},{5,9},{9,5},{13,1},{2,14},{6,10},... | collective-permute-start | bytes 172040 | tf_op jit(solution)/shard_map/ppermute | solution.py:24
  29.9 0.0 collective-permute-done.13.arrived_ref
  29.9 1.3 %collective-permute-start.14 = (bf16[16,1792]{1,0:T(8,128)(2,1)S(1)}, bf16[16,1792]{1,0:T(8,128)(2,1)S(1)}, u32[]{:S(2)}, u32[]{:S(2)}) collective-permute-start(bf16[16,1792]{1,0:T(8,128)(2,1)S(1)} %get-tuple-element.44), channel_id=1, source_target_pairs={{0,4},{4,0},{8,12},{12,8},{1,5},{5,1},{9,13},{13,9},{2,6},{6,2},{1... | collective-permute-start | bytes 172040 | tf_op jit(solution)/shard_map/ppermute | solution.py:24
  31.2 1.9 %collective-permute-start.15 = (bf16[16,1792]{1,0:T(8,128)(2,1)S(1)}, bf16[16,1792]{1,0:T(8,128)(2,1)S(1)}, u32[]{:S(2)}, u32[]{:S(2)}) collective-permute-start(bf16[16,1792]{1,0:T(8,128)(2,1)S(1)} %get-tuple-element.45), channel_id=1, source_target_pairs={{0,8},{4,12},{8,0},{12,4},{1,9},{5,13},{9,1},{13,5},{2,10},{6,14},... | collective-permute-start | bytes 172040 | tf_op jit(solution)/shard_map/ppermute | solution.py:24
  33.2 2.0 %attend.1 = bf16[64,512]{1,0:T(8,128)(2,1)} custom-call(s32[4,4]{1,0:T(4,128)} %dest_ref.1, s32[16]{0:T(128)} %len_ref.1, bf16[64,576]{1,0:T(8,128)(2,1)} %bitcast.10, bf16[32,2176]{1,0:T(8,128)(2,1)S(1)} %join.6.refs_2_.refs_1_.refs_0_, bf16[32,2176]{1,0:T(8,128)(2,1)S(1)} %join.7.refs_2_.refs_1_, bf16[32,2176]{1,0:T(8,128)(2,1)S(1)} %collective-permute-done.4.refs_2_, ...), custom_call_target="tpu_custom_call" | custom-call | flops 234881024 | bytes 3670016 | tf_op jit(solution)/shard_map/attend/pallas_call | solution.py:473
  35.1 0.0 collective-permute-done.12.arrived_ref
  35.2 0.0 collective-permute-done.17.refs_4_
  35.2 0.0 collective-permute-done.16.refs_3_
  35.2 0.0 collective-permute-done.14.refs_1_
  35.2 1.1 %collective-permute-done.15.refs_2_ = bf16[16,1792]{1,0:T(8,128)(2,1)S(1)} collective-permute-done((bf16[16,1792]{1,0:T(8,128)(2,1)S(1)}, bf16[16,1792]{1,0:T(8,128)(2,1)S(1)}, u32[]{:S(2)}, u32[]{:S(2)}) %collective-permute-start.15) | collective-permute-done | bytes 57376 | tf_op jit(solution)/shard_map/ppermute | solution.py:24
  36.3 1.2 %combine.1 = bf16[256,1792]{1,0:T(8,128)(2,1)} custom-call(bf16[256,128]{1,0:T(8,128)(2,1)S(1)} %get-tuple-element.25.refs_2_.table_ref, bf16[16,1792]{1,0:T(8,128)(2,1)S(1)} %total.6.refs_0_, bf16[16,1792]{1,0:T(8,128)(2,1)S(1)} %collective-permute-done.14.refs_1_, bf16[16,1792]{1,0:T(8,128)(2,1)S(1)} %collective-permute-done.15.refs_2_, ...), custom_call_target="tpu_custom_call" | custom-call | flops 117440512 | bytes 917504 | tf_op jit(solution)/shard_map/combine/pallas_call | solution.py:390
  (11 shorter events, 0.2 us)
Async XLA Ops:
  2.2 11.3 %collective-permute-start.3 = (bf16[16,2176]{1,0:T(8,128)(2,1)S(1)}, bf16[16,2176]{1,0:T(8,128)(2,1)S(1)}, u32[]{:S(2)}, u32[]{:S(2)}) collective-permute-start(bf16[16,2176]{1,0:T(8,128)(2,1)S(1)} %get-tuple-element.29), channel_id=1, source_target_pairs={{0,6},{1,7},{2,4},{3,5},{4,2},{5,3},{6,0},{7,1},{8,14},{9,15},{10,... | collective-permute-start | bytes 208904 | tf_op jit(solution)/shard_map/ppermute | solution.py:34
  6.2 7.5 %collective-permute-start.1 = (bf16[16,2176]{1,0:T(8,128)(2,1)S(1)}, bf16[16,2176]{1,0:T(8,128)(2,1)S(1)}, u32[]{:S(2)}, u32[]{:S(2)}) collective-permute-start(bf16[16,2176]{1,0:T(8,128)(2,1)S(1)} %get-tuple-element.30), channel_id=1, source_target_pairs={{0,8},{4,12},{8,0},{12,4},{1,9},{5,13},{9,1},{13,5},{2,10},{6,14},... | collective-permute-start | bytes 208904 | tf_op jit(solution)/shard_map/ppermute | solution.py:24
  8.8 6.2 %collective-permute-start.2 = (bf16[16,2176]{1,0:T(8,128)(2,1)S(1)}, bf16[16,2176]{1,0:T(8,128)(2,1)S(1)}, u32[]{:S(2)}, u32[]{:S(2)}) collective-permute-start(bf16[16,2176]{1,0:T(8,128)(2,1)S(1)} %get-tuple-element.31), channel_id=1, source_target_pairs={{0,12},{4,8},{8,4},{12,0},{1,13},{5,9},{9,5},{13,1},{2,14},{6,10},... | collective-permute-start | bytes 208904 | tf_op jit(solution)/shard_map/ppermute | solution.py:24
  9.0 6.0 %collective-permute-start = (bf16[16,2176]{1,0:T(8,128)(2,1)S(1)}, bf16[16,2176]{1,0:T(8,128)(2,1)S(1)}, u32[]{:S(2)}, u32[]{:S(2)}) collective-permute-start(bf16[16,2176]{1,0:T(8,128)(2,1)S(1)} %get-tuple-element.29), channel_id=1, source_target_pairs={{0,4},{4,0},{8,12},{12,8},{1,5},{5,1},{9,13},{13,9},{2,6},{6,2},{1... | collective-permute-start | bytes 208904 | tf_op jit(solution)/shard_map/ppermute | solution.py:24
  9.7 5.4 %collective-permute-start.6 = (bf16[16,2176]{1,0:T(8,128)(2,1)S(1)}, bf16[16,2176]{1,0:T(8,128)(2,1)S(1)}, u32[]{:S(2)}, u32[]{:S(2)}) collective-permute-start(bf16[16,2176]{1,0:T(8,128)(2,1)S(1)} %get-tuple-element.28.refs_0_), channel_id=1, source_target_pairs={{0,2},{1,3},{2,0},{3,1},{4,6},{5,7},{6,4},{7,5},{8,10},{9,11},{10,... | collective-permute-start | bytes 208904 | tf_op jit(solution)/shard_map/ppermute | solution.py:24
  15.1 5.1 %collective-permute-start.7 = (bf16[32,2176]{1,0:T(8,128)(2,1)S(1)}, bf16[32,2176]{1,0:T(8,128)(2,1)S(1)}, u32[]{:S(2)}, u32[]{:S(2)}) collective-permute-start(bf16[32,2176]{1,0:T(8,128)(2,1)S(1)} %tie.2), channel_id=1, source_target_pairs={{0,2},{1,3},{2,0},{3,1},{4,6},{5,7},{6,4},{7,5},{8,10},{9,11},{10,... | collective-permute-start | bytes 417800 | tf_op jit(solution)/shard_map/ppermute | solution.py:24
  15.7 4.5 %collective-permute-start.4 = (bf16[32,2176]{1,0:T(8,128)(2,1)S(1)}, bf16[32,2176]{1,0:T(8,128)(2,1)S(1)}, u32[]{:S(2)}, u32[]{:S(2)}) collective-permute-start(bf16[32,2176]{1,0:T(8,128)(2,1)S(1)} %join.6.refs_2_.refs_1_.refs_0_), channel_id=1, source_target_pairs={{0,1},{1,0},{2,3},{3,2},{4,5},{5,4},{6,7},{7,6},{8,9},{9,8},{10,11... | collective-permute-start | bytes 417800 | tf_op jit(solution)/shard_map/ppermute | solution.py:24
  15.7 5.3 %collective-permute-start.8 = (bf16[32,2176]{1,0:T(8,128)(2,1)S(1)}, bf16[32,2176]{1,0:T(8,128)(2,1)S(1)}, u32[]{:S(2)}, u32[]{:S(2)}) collective-permute-start(bf16[32,2176]{1,0:T(8,128)(2,1)S(1)} %join.9.refs_4_), channel_id=1, source_target_pairs={{0,1},{1,0},{2,3},{3,2},{4,5},{5,4},{6,7},{7,6},{8,9},{9,8},{10,11... | collective-permute-start | bytes 417800 | tf_op jit(solution)/shard_map/ppermute | solution.py:24
  16.2 4.0 %collective-permute-start.5 = (bf16[32,2176]{1,0:T(8,128)(2,1)S(1)}, bf16[32,2176]{1,0:T(8,128)(2,1)S(1)}, u32[]{:S(2)}, u32[]{:S(2)}) collective-permute-start(bf16[32,2176]{1,0:T(8,128)(2,1)S(1)} %join.7.refs_2_.refs_1_), channel_id=1, source_target_pairs={{0,1},{1,0},{2,3},{3,2},{4,5},{5,4},{6,7},{7,6},{8,9},{9,8},{10,11... | collective-permute-start | bytes 417800 | tf_op jit(solution)/shard_map/ppermute | solution.py:24
  20.2 1.4 %collective-permute-start.9 = (bf16[32,2176]{1,0:T(8,128)(2,1)S(1)}, bf16[32,2176]{1,0:T(8,128)(2,1)S(1)}, u32[]{:S(2)}, u32[]{:S(2)}) collective-permute-start(bf16[32,2176]{1,0:T(8,128)(2,1)S(1)} %tie.3.refs_5_), channel_id=1, source_target_pairs={{0,1},{1,0},{2,3},{3,2},{4,5},{5,4},{6,7},{7,6},{8,9},{9,8},{10,11... | collective-permute-start | bytes 417800 | tf_op jit(solution)/shard_map/ppermute | solution.py:24
  22.3 1.5 %collective-permute-start.11 = (bf16[64,1792]{1,0:T(8,128)(2,1)S(1)}, bf16[64,1792]{1,0:T(8,128)(2,1)S(1)}, u32[]{:S(2)}, u32[]{:S(2)}) collective-permute-start(bf16[64,1792]{1,0:T(8,128)(2,1)S(1)} %get-tuple-element.40), channel_id=1, source_target_pairs={{0,1},{1,0},{2,3},{3,2},{4,5},{5,4},{6,7},{7,6},{8,9},{9,8},{10,11... | collective-permute-start | bytes 688136 | tf_op jit(solution)/shard_map/ppermute | solution.py:24
  22.8 5.8 %collective-permute-start.10 = (bf16[64,1792]{1,0:T(8,128)(2,1)S(1)}, bf16[64,1792]{1,0:T(8,128)(2,1)S(1)}, u32[]{:S(2)}, u32[]{:S(2)}) collective-permute-start(bf16[64,1792]{1,0:T(8,128)(2,1)S(1)} %down.3), channel_id=1, source_target_pairs={{0,1},{1,0},{2,3},{3,2},{4,5},{5,4},{6,7},{7,6},{8,9},{9,8},{10,11... | collective-permute-start | bytes 688136 | tf_op jit(solution)/shard_map/ppermute | solution.py:24
  23.9 6.0 %collective-permute-start.13 = (bf16[32,1792]{1,0:T(8,128)(2,1)S(1)}, bf16[32,1792]{1,0:T(8,128)(2,1)S(1)}, u32[]{:S(2)}, u32[]{:S(2)}) collective-permute-start(bf16[32,1792]{1,0:T(8,128)(2,1)S(1)} %get-tuple-element.43), channel_id=1, source_target_pairs={{0,2},{1,3},{2,0},{3,1},{4,6},{5,7},{6,4},{7,5},{8,10},{9,11},{10,... | collective-permute-start | bytes 344072 | tf_op jit(solution)/shard_map/ppermute | solution.py:24
  24.5 10.7 %collective-permute-start.12 = (bf16[16,1792]{1,0:T(8,128)(2,1)S(1)}, bf16[16,1792]{1,0:T(8,128)(2,1)S(1)}, u32[]{:S(2)}, u32[]{:S(2)}) collective-permute-start(bf16[16,1792]{1,0:T(8,128)(2,1)S(1)} %get-tuple-element.41), channel_id=1, source_target_pairs={{0,2},{1,3},{2,0},{3,1},{4,6},{5,7},{6,4},{7,5},{8,10},{9,11},{10,... | collective-permute-start | bytes 172040 | tf_op jit(solution)/shard_map/ppermute | solution.py:24
  26.0 9.2 %collective-permute-start.17 = (bf16[16,1792]{1,0:T(8,128)(2,1)S(1)}, bf16[16,1792]{1,0:T(8,128)(2,1)S(1)}, u32[]{:S(2)}, u32[]{:S(2)}) collective-permute-start(bf16[16,1792]{1,0:T(8,128)(2,1)S(1)} %get-tuple-element.47), channel_id=1, source_target_pairs={{0,14},{1,15},{2,12},{3,13},{4,10},{5,11},{6,8},{7,9},{8,6},{9,7},... | collective-permute-start | bytes 172040 | tf_op jit(solution)/shard_map/ppermute | solution.py:34
  28.6 6.5 %collective-permute-start.16 = (bf16[16,1792]{1,0:T(8,128)(2,1)S(1)}, bf16[16,1792]{1,0:T(8,128)(2,1)S(1)}, u32[]{:S(2)}, u32[]{:S(2)}) collective-permute-start(bf16[16,1792]{1,0:T(8,128)(2,1)S(1)} %get-tuple-element.46), channel_id=1, source_target_pairs={{0,12},{4,8},{8,4},{12,0},{1,13},{5,9},{9,5},{13,1},{2,14},{6,10},... | collective-permute-start | bytes 172040 | tf_op jit(solution)/shard_map/ppermute | solution.py:24
  29.9 5.3 %collective-permute-start.14 = (bf16[16,1792]{1,0:T(8,128)(2,1)S(1)}, bf16[16,1792]{1,0:T(8,128)(2,1)S(1)}, u32[]{:S(2)}, u32[]{:S(2)}) collective-permute-start(bf16[16,1792]{1,0:T(8,128)(2,1)S(1)} %get-tuple-element.44), channel_id=1, source_target_pairs={{0,4},{4,0},{8,12},{12,8},{1,5},{5,1},{9,13},{13,9},{2,6},{6,2},{1... | collective-permute-start | bytes 172040 | tf_op jit(solution)/shard_map/ppermute | solution.py:24
  31.2 5.1 %collective-permute-start.15 = (bf16[16,1792]{1,0:T(8,128)(2,1)S(1)}, bf16[16,1792]{1,0:T(8,128)(2,1)S(1)}, u32[]{:S(2)}, u32[]{:S(2)}) collective-permute-start(bf16[16,1792]{1,0:T(8,128)(2,1)S(1)} %get-tuple-element.45), channel_id=1, source_target_pairs={{0,8},{4,12},{8,0},{12,4},{1,9},{5,13},{9,1},{13,5},{2,10},{6,14},... | collective-permute-start | bytes 172040 | tf_op jit(solution)/shard_map/ppermute | solution.py:24

commit v8 on v7

--- a/solution.py
+++ b/solution.py
@@ -72,7 +72,13 @@
 def route_kernel(ep_count, *refs):
     sources, blocks = refs[:4], refs[4 : 4 + ep_count]
     held, sems = refs[4 + ep_count : -1], refs[-1]
-    copies = [pltpu.make_async_copy(sources[i], held[i], sems.at[i]) for i in range(4)]
+    copies = [pltpu.make_async_copy(sources[i], held[i], sems.at[i]) for i in range(3)]
+    half = held[3].shape[1] // 2
+    for i in range(2):
+        at = pl.ds(i * half, half)
+        copies.append(
+            pltpu.make_async_copy(sources[3].at[:, at], held[3].at[:, at], sems.at[3 + i])
+        )
     for copy in copies:
         copy.start()
     ids_ref, dest_ref, cache_ref, tokens_ref = held
@@ -93,10 +99,12 @@
         above = jnp.concatenate([kept[:, :first], jnp.zeros((part, wide - first), f32)], axis=1)
         below = jnp.concatenate([kept[:, first:], jnp.zeros((part, wide - second), f32)], axis=1)
         blocks[d][:, width:] = jnp.concatenate([above, below], axis=0).astype(bf16)
-    copies[3].wait()
-    rows = jnp.dot(dispatch, tokens_ref[...], preferred_element_type=f32)
-    for d in range(ep_count):
-        blocks[d][:, :width] = rows[d * CAP : (d + 1) * CAP].astype(bf16)
+    for i in range(2):
+        at = pl.ds(i * half, half)
+        copies[3 + i].wait()
+        rows = jnp.dot(dispatch, tokens_ref[:, at], preferred_element_type=f32)
+        for d in range(ep_count):
+            blocks[d][:, at] = rows[d * CAP : (d + 1) * CAP].astype(bf16)
 
 
 def route(ids, tokens, cache_rows, destination, ep_count):
@@ -111,7 +119,7 @@
         in_specs=[HBM] * 4,
         out_specs=[VMEM] * ep_count,
         scratch_shapes=[p(a.shape, a.dtype) for p, a in zip(places, sources)]
-        + [pltpu.SemaphoreType.DMA((4,))],
+        + [pltpu.SemaphoreType.DMA((5,))],
         compiler_params=params(sources * 2 + out_shape * 2),
         cost_estimate=cost(4 * ep_count * CAP * tokens.size, 2 * tokens.size),
         name="route",
@@ -386,7 +394,7 @@
 def mix(table, blocks):
     operands = [part for block in blocks for part in block]
     mixed = jax.ShapeDtypeStruct((table.shape[0], operands[0].shape[1]), bf16)
-    cuts = 2 if mixed.shape[1] % 256 == 0 else 1
+    cuts = 7 if mixed.shape[1] % 896 == 0 else 1
     return pl.pallas_call(
         functools.partial(combine_kernel, cuts, [len(block) for block in blocks]),
         out_shape=mixed,

time: 37.8 us -> 37.7 us (level)
  no operation moved by 1% of the time
where the time goes in v8:
time: 37.7 us; the launch traced here: 37.5 us
  starting transfers between devices  19.1 us (51%)
  Pallas kernels  12.8 us (34%)
  waiting for transfers between devices  4.86 us (13%)
  between operations  0.8 us (2%)
    ppermute x16, starting transfers between devices, swap(): return lax.ppermute(value, axis, [(i, i ^ mask) for i in range(count)])  12.4 us
    ppermute x2, starting transfers between devices, swap_both(): return lax.ppermute(value, ('ep', 'pd'), pairs)  6.64 us
    pallas_call x2, Pallas kernels, fetch(): pl.pallas_call(functools.partial(fetch_kernel, ep_count, len(arrays), len...  5.25 us
    ppermute x16, waiting for transfers between devices, swap(): return lax.ppermute(value, axis, [(i, i ^ mask) for i in range(count)])  4.85 us
    pallas_call x1, Pallas kernels, on_device(): pl.pallas_call(functools.partial(attend_kernel, order, pd_count, width),...  1.96 us
    pallas_call x1, Pallas kernels, route(): pl.pallas_call(functools.partial(route_kernel, ep_count), out_shape=out_s...  1.53 us
    pallas_call x2, Pallas kernels, gate_up(): pl.pallas_call(functools.partial(gate_up_kernel, masks, width, bool(befor...  1.21 us
    pallas_call x1, Pallas kernels, mix(): pl.pallas_call(functools.partial(combine_kernel, cuts, [len(block) for bl...  1.18 us
  transfers between devices with their start and end apart: 18, of which 6 were waited for; matrix products, arithmetic and copies ran while one was open for 0% of the time, Pallas kernels for 25%

profile of v8, /device:TPU:0, one launch (start us, length us, event | category | flops | bytes accessed | tf_op | source)
XLA Modules:
  0.0 37.5 jit_solution(2061659879089436388)
XLA Ops:
  0.6 1.5 %route.1 = (bf16[16,2176]{1,0:T(8,128)(2,1)S(1)}, bf16[16,2176]{1,0:T(8,128)(2,1)S(1)}, bf16[16,2176]{1,0:T(8,128)(2,1)S(1)}, bf16[16,2176]{1,0:T(8,128)(2,1)S(1)}) custom-call(s32[8,256]{1,0:T(8,128)} %bitcast.12, s32[4,4]{1,0:T(4,128)} %dest_ref.1, bf16[4,8,576]{2,1,0:T(8,128)(2,1)} %refs_2_.1, bf16[256,1792]{1,0:T(8,128)(2,1)} %refs_3_.1), custom_call_target="tpu_custom_call" | custom-call | flops 117440512 | bytes 917504 | tf_op jit(solution)/shard_map/route/pallas_call | solution.py:116
  2.2 4.0 %collective-permute-start.3 = (bf16[16,2176]{1,0:T(8,128)(2,1)S(1)}, bf16[16,2176]{1,0:T(8,128)(2,1)S(1)}, u32[]{:S(2)}, u32[]{:S(2)}) collective-permute-start(bf16[16,2176]{1,0:T(8,128)(2,1)S(1)} %get-tuple-element.29), channel_id=1, source_target_pairs={{0,6},{1,7},{2,4},{3,5},{4,2},{5,3},{6,0},{7,1},{8,14},{9,15},{10,... | collective-permute-start | bytes 208904 | tf_op jit(solution)/shard_map/ppermute | solution.py:34
  6.2 2.6 %collective-permute-start.1 = (bf16[16,2176]{1,0:T(8,128)(2,1)S(1)}, bf16[16,2176]{1,0:T(8,128)(2,1)S(1)}, u32[]{:S(2)}, u32[]{:S(2)}) collective-permute-start(bf16[16,2176]{1,0:T(8,128)(2,1)S(1)} %get-tuple-element.30), channel_id=1, source_target_pairs={{0,8},{4,12},{8,0},{12,4},{1,9},{5,13},{9,1},{13,5},{2,10},{6,14},... | collective-permute-start | bytes 208904 | tf_op jit(solution)/shard_map/ppermute | solution.py:24
  8.8 0.2 collective-permute-start.2
  9.0 0.7 %collective-permute-start = (bf16[16,2176]{1,0:T(8,128)(2,1)S(1)}, bf16[16,2176]{1,0:T(8,128)(2,1)S(1)}, u32[]{:S(2)}, u32[]{:S(2)}) collective-permute-start(bf16[16,2176]{1,0:T(8,128)(2,1)S(1)} %get-tuple-element.29), channel_id=1, source_target_pairs={{0,4},{4,0},{8,12},{12,8},{1,5},{5,1},{9,13},{13,9},{2,6},{6,2},{1... | collective-permute-start | bytes 208904 | tf_op jit(solution)/shard_map/ppermute | solution.py:24
  9.7 0.5 %collective-permute-start.6 = (bf16[16,2176]{1,0:T(8,128)(2,1)S(1)}, bf16[16,2176]{1,0:T(8,128)(2,1)S(1)}, u32[]{:S(2)}, u32[]{:S(2)}) collective-permute-start(bf16[16,2176]{1,0:T(8,128)(2,1)S(1)} %get-tuple-element.28.refs_0_), channel_id=1, source_target_pairs={{0,2},{1,3},{2,0},{3,1},{4,6},{5,7},{6,4},{7,5},{8,10},{9,11},{10,... | collective-permute-start | bytes 208904 | tf_op jit(solution)/shard_map/ppermute | solution.py:24
  10.2 3.2 %fetch.2 = (bf16[7168,256]{1,0:T(8,128)(2,1)S(1)}, bf16[7168,256]{1,0:T(8,128)(2,1)S(1)}, bf16[256,128]{1,0:T(8,128)(2,1)S(1)}) custom-call(bf16[7168,256]{1,0:T(8,128)(2,1)} %bitcast.7, bf16[7168,256]{1,0:T(8,128)(2,1)} %bitcast.8, s32[8,256]{1,0:T(8,128)} %bitcast.13, f32[8,256]{1,0:T(8,128)} %bitcast.14), custom_call_target="tpu_custom_call" | custom-call | tf_op jit(solution)/shard_map/fetch/pallas_call | solution.py:176
  13.4 0.0 collective-permute-done.3.refs_0_
  13.4 0.3 collective-permute-done.1.refs_0_
  13.7 1.3 %collective-permute-done.2.refs_1_ = bf16[16,2176]{1,0:T(8,128)(2,1)S(1)} collective-permute-done((bf16[16,2176]{1,0:T(8,128)(2,1)S(1)}, bf16[16,2176]{1,0:T(8,128)(2,1)S(1)}, u32[]{:S(2)}, u32[]{:S(2)}) %collective-permute-start.2) | collective-permute-done | bytes 69664 | tf_op jit(solution)/shard_map/ppermute | solution.py:24
  15.0 0.0 collective-permute-done.refs_1_
  15.0 0.0 collective-permute-done.6.refs_0_
  15.1 0.6 %collective-permute-start.7 = (bf16[32,2176]{1,0:T(8,128)(2,1)S(1)}, bf16[32,2176]{1,0:T(8,128)(2,1)S(1)}, u32[]{:S(2)}, u32[]{:S(2)}) collective-permute-start(bf16[32,2176]{1,0:T(8,128)(2,1)S(1)} %tie.2), channel_id=1, source_target_pairs={{0,2},{1,3},{2,0},{3,1},{4,6},{5,7},{6,4},{7,5},{8,10},{9,11},{10,... | collective-permute-start | bytes 417800 | tf_op jit(solution)/shard_map/ppermute | solution.py:24
  15.7 0.0 collective-permute-start.4
  15.7 0.5 %collective-permute-start.8 = (bf16[32,2176]{1,0:T(8,128)(2,1)S(1)}, bf16[32,2176]{1,0:T(8,128)(2,1)S(1)}, u32[]{:S(2)}, u32[]{:S(2)}) collective-permute-start(bf16[32,2176]{1,0:T(8,128)(2,1)S(1)} %join.9.refs_4_), channel_id=1, source_target_pairs={{0,1},{1,0},{2,3},{3,2},{4,5},{5,4},{6,7},{7,6},{8,9},{9,8},{10,11... | collective-permute-start | bytes 417800 | tf_op jit(solution)/shard_map/ppermute | solution.py:24
  16.2 0.1 collective-permute-start.5
  16.3 2.0 %fetch.3.refs_2_.down_ref = bf16[256,7168]{1,0:T(8,128)(2,1)S(1)} custom-call(bf16[256,7168]{1,0:T(8,128)(2,1)} %bitcast.9, bf16[32,2176]{1,0:T(8,128)(2,1)S(1)} %join.6.refs_2_.refs_1_.refs_0_, bf16[32,2176]{1,0:T(8,128)(2,1)S(1)} %join.7.refs_2_.refs_1_, bf16[16,2176]{1,0:T(8,128)(2,1)S(1)} %join.8.refs_3_.refs_1_), custom_call_target="tpu_custom_call" | custom-call | tf_op jit(solution)/shard_map/fetch/pallas_call | solution.py:176
  18.3 0.4 %gate_up.2 = (f32[64,256]{1,0:T(8,128)S(1)}, f32[64,256]{1,0:T(8,128)S(1)}) custom-call(bf16[7168,256]{1,0:T(8,128)(2,1)S(1)} %get-tuple-element.26.gate_ref, bf16[7168,256]{1,0:T(8,128)(2,1)S(1)} %get-tuple-element.27.up_ref, bf16[32,2176]{1,0:T(8,128)(2,1)S(1)} %join.6.refs_2_.refs_1_.refs_0_, bf16[32,2176]{1,0:T(8,128)(2,1)S(1)} %join.7.refs_2_.refs_1_), custom_call_target="tpu_custom_call" | custom-call | tf_op jit(solution)/shard_map/gate_up/pallas_call | solution.py:271
  18.8 1.4 %collective-permute-done.7.refs_0_ = bf16[32,2176]{1,0:T(8,128)(2,1)S(1)} collective-permute-done((bf16[32,2176]{1,0:T(8,128)(2,1)S(1)}, bf16[32,2176]{1,0:T(8,128)(2,1)S(1)}, u32[]{:S(2)}, u32[]{:S(2)}) %collective-permute-start.7) | collective-permute-done | bytes 139296 | tf_op jit(solution)/shard_map/ppermute | solution.py:24
  20.2 0.0 collective-permute-start.9
  20.2 0.0 collective-permute-done.5.refs_3_
  20.2 0.0 collective-permute-done.4.refs_2_
  20.2 0.8 %gate_up.3 = (f32[64,256]{1,0:T(8,128)S(1)}, f32[64,256]{1,0:T(8,128)S(1)}) custom-call(bf16[7168,256]{1,0:T(8,128)(2,1)S(1)} %get-tuple-element.26.gate_ref, bf16[7168,256]{1,0:T(8,128)(2,1)S(1)} %get-tuple-element.27.up_ref, f32[64,256]{1,0:T(8,128)S(1)} %get-tuple-element.32.refs_1_.refs_0_, f32[64,256]{1,0:T(8,128)S(1)} %get-tuple-element.33.refs_1_, ...), custom_call_target="tpu_custom_call" | custom-call | tf_op jit(solution)/shard_map/gate_up/pallas_call | solution.py:271
  21.0 0.0 collective-permute-done.8.refs_2_.refs_6_
  21.0 0.6 %collective-permute-done.9.refs_3_.refs_7_ = bf16[32,2176]{1,0:T(8,128)(2,1)S(1)} collective-permute-done((bf16[32,2176]{1,0:T(8,128)(2,1)S(1)}, bf16[32,2176]{1,0:T(8,128)(2,1)S(1)}, u32[]{:S(2)}, u32[]{:S(2)}) %collective-permute-start.9) | collective-permute-done | bytes 139296 | tf_op jit(solution)/shard_map/ppermute | solution.py:24
  21.6 0.7 %hidden.1 = (bf16[64,256]{1,0:T(8,128)(2,1)S(1)}, bf16[64,1792]{1,0:T(8,128)(2,1)S(1)}) custom-call(bf16[7168,256]{1,0:T(8,128)(2,1)S(1)} %get-tuple-element.26.gate_ref, bf16[7168,256]{1,0:T(8,128)(2,1)S(1)} %get-tuple-element.27.up_ref, bf16[256,7168]{1,0:T(8,128)(2,1)S(1)} %fetch.3.refs_2_.down_ref, f32[64,256]{1,0:T(8,128)S(1)} %get-tuple-element.34.refs_0_, ...), custom_call_target="tpu_custom_call" | custom-call | tf_op jit(solution)/shard_map/hidden/pallas_call | solution.py:299
  22.3 0.2 collective-permute-start.11
  22.5 0.3 down.3
  22.7 0.4 %collective-permute-start.10 = (bf16[64,1792]{1,0:T(8,128)(2,1)S(1)}, bf16[64,1792]{1,0:T(8,128)(2,1)S(1)}, u32[]{:S(2)}, u32[]{:S(2)}) collective-permute-start(bf16[64,1792]{1,0:T(8,128)(2,1)S(1)} %down.3), channel_id=1, source_target_pairs={{0,1},{1,0},{2,3},{3,2},{4,5},{5,4},{6,7},{7,6},{8,9},{9,8},{10,11... | collective-permute-start | bytes 688136 | tf_op jit(solution)/shard_map/ppermute | solution.py:24
  23.2 0.5 %down.2 = (f32[64,1792]{1,0:T(8,128)S(1)}, f32[64,1792]{1,0:T(8,128)S(1)}) custom-call(bf16[64,256]{1,0:T(8,128)(2,1)S(1)} %get-tuple-element.36.hidden_ref, bf16[256,7168]{1,0:T(8,128)(2,1)S(1)} %fetch.3.refs_2_.down_ref), custom_call_target="tpu_custom_call" | custom-call | flops 234881024 | bytes 3670016 | tf_op jit(solution)/shard_map/down/pallas_call | solution.py:320
  23.6 0.2 collective-permute-done.11.arrived_ref
  23.8 0.6 %collective-permute-start.13 = (bf16[32,1792]{1,0:T(8,128)(2,1)S(1)}, bf16[32,1792]{1,0:T(8,128)(2,1)S(1)}, u32[]{:S(2)}, u32[]{:S(2)}) collective-permute-start(bf16[32,1792]{1,0:T(8,128)(2,1)S(1)} %get-tuple-element.43), channel_id=1, source_target_pairs={{0,2},{1,3},{2,0},{3,1},{4,6},{5,7},{6,4},{7,5},{8,10},{9,11},{10,... | collective-permute-start | bytes 344072 | tf_op jit(solution)/shard_map/ppermute | solution.py:24
  24.4 1.5 %collective-permute-start.12 = (bf16[16,1792]{1,0:T(8,128)(2,1)S(1)}, bf16[16,1792]{1,0:T(8,128)(2,1)S(1)}, u32[]{:S(2)}, u32[]{:S(2)}) collective-permute-start(bf16[16,1792]{1,0:T(8,128)(2,1)S(1)} %get-tuple-element.41), channel_id=1, source_target_pairs={{0,2},{1,3},{2,0},{3,1},{4,6},{5,7},{6,4},{7,5},{8,10},{9,11},{10,... | collective-permute-start | bytes 172040 | tf_op jit(solution)/shard_map/ppermute | solution.py:24
  25.9 2.6 %collective-permute-start.17 = (bf16[16,1792]{1,0:T(8,128)(2,1)S(1)}, bf16[16,1792]{1,0:T(8,128)(2,1)S(1)}, u32[]{:S(2)}, u32[]{:S(2)}) collective-permute-start(bf16[16,1792]{1,0:T(8,128)(2,1)S(1)} %get-tuple-element.47), channel_id=1, source_target_pairs={{0,14},{1,15},{2,12},{3,13},{4,10},{5,11},{6,8},{7,9},{8,6},{9,7},... | collective-permute-start | bytes 172040 | tf_op jit(solution)/shard_map/ppermute | solution.py:34
  28.6 0.0 collective-permute-done.10.arrived_ref
  28.6 1.2 %collective-permute-start.16 = (bf16[16,1792]{1,0:T(8,128)(2,1)S(1)}, bf16[16,1792]{1,0:T(8,128)(2,1)S(1)}, u32[]{:S(2)}, u32[]{:S(2)}) collective-permute-start(bf16[16,1792]{1,0:T(8,128)(2,1)S(1)} %get-tuple-element.46), channel_id=1, source_target_pairs={{0,12},{4,8},{8,4},{12,0},{1,13},{5,9},{9,5},{13,1},{2,14},{6,10},... | collective-permute-start | bytes 172040 | tf_op jit(solution)/shard_map/ppermute | solution.py:24
  29.8 0.0 collective-permute-done.13.arrived_ref
  29.9 1.3 %collective-permute-start.14 = (bf16[16,1792]{1,0:T(8,128)(2,1)S(1)}, bf16[16,1792]{1,0:T(8,128)(2,1)S(1)}, u32[]{:S(2)}, u32[]{:S(2)}) collective-permute-start(bf16[16,1792]{1,0:T(8,128)(2,1)S(1)} %get-tuple-element.44), channel_id=1, source_target_pairs={{0,4},{4,0},{8,12},{12,8},{1,5},{5,1},{9,13},{13,9},{2,6},{6,2},{1... | collective-permute-start | bytes 172040 | tf_op jit(solution)/shard_map/ppermute | solution.py:24
  31.2 2.0 %collective-permute-start.15 = (bf16[16,1792]{1,0:T(8,128)(2,1)S(1)}, bf16[16,1792]{1,0:T(8,128)(2,1)S(1)}, u32[]{:S(2)}, u32[]{:S(2)}) collective-permute-start(bf16[16,1792]{1,0:T(8,128)(2,1)S(1)} %get-tuple-element.45), channel_id=1, source_target_pairs={{0,8},{4,12},{8,0},{12,4},{1,9},{5,13},{9,1},{13,5},{2,10},{6,14},... | collective-permute-start | bytes 172040 | tf_op jit(solution)/shard_map/ppermute | solution.py:24
  33.2 2.0 %attend.1 = bf16[64,512]{1,0:T(8,128)(2,1)} custom-call(s32[4,4]{1,0:T(4,128)} %dest_ref.1, s32[16]{0:T(128)} %len_ref.1, bf16[64,576]{1,0:T(8,128)(2,1)} %bitcast.10, bf16[32,2176]{1,0:T(8,128)(2,1)S(1)} %join.6.refs_2_.refs_1_.refs_0_, bf16[32,2176]{1,0:T(8,128)(2,1)S(1)} %join.7.refs_2_.refs_1_, bf16[32,2176]{1,0:T(8,128)(2,1)S(1)} %collective-permute-done.4.refs_2_, ...), custom_call_target="tpu_custom_call" | custom-call | flops 234881024 | bytes 3670016 | tf_op jit(solution)/shard_map/attend/pallas_call | solution.py:481
  35.1 0.0 collective-permute-done.12.arrived_ref
  35.1 0.0 collective-permute-done.17.refs_4_
  35.1 0.0 collective-permute-done.16.refs_3_
  35.2 0.0 collective-permute-done.14.refs_1_
  35.2 1.1 %collective-permute-done.15.refs_2_ = bf16[16,1792]{1,0:T(8,128)(2,1)S(1)} collective-permute-done((bf16[16,1792]{1,0:T(8,128)(2,1)S(1)}, bf16[16,1792]{1,0:T(8,128)(2,1)S(1)}, u32[]{:S(2)}, u32[]{:S(2)}) %collective-permute-start.15) | collective-permute-done | bytes 57376 | tf_op jit(solution)/shard_map/ppermute | solution.py:24
  36.3 1.2 %combine.1 = bf16[256,1792]{1,0:T(8,128)(2,1)} custom-call(bf16[256,128]{1,0:T(8,128)(2,1)S(1)} %get-tuple-element.25.refs_2_.table_ref, bf16[16,1792]{1,0:T(8,128)(2,1)S(1)} %total.6.refs_0_, bf16[16,1792]{1,0:T(8,128)(2,1)S(1)} %collective-permute-done.14.refs_1_, bf16[16,1792]{1,0:T(8,128)(2,1)S(1)} %collective-permute-done.15.refs_2_, ...), custom_call_target="tpu_custom_call" | custom-call | flops 117440512 | bytes 917504 | tf_op jit(solution)/shard_map/combine/pallas_call | solution.py:398
  (11 shorter events, 0.2 us)
Async XLA Ops:
  2.2 11.3 %collective-permute-start.3 = (bf16[16,2176]{1,0:T(8,128)(2,1)S(1)}, bf16[16,2176]{1,0:T(8,128)(2,1)S(1)}, u32[]{:S(2)}, u32[]{:S(2)}) collective-permute-start(bf16[16,2176]{1,0:T(8,128)(2,1)S(1)} %get-tuple-element.29), channel_id=1, source_target_pairs={{0,6},{1,7},{2,4},{3,5},{4,2},{5,3},{6,0},{7,1},{8,14},{9,15},{10,... | collective-permute-start | bytes 208904 | tf_op jit(solution)/shard_map/ppermute | solution.py:34
  6.2 7.5 %collective-permute-start.1 = (bf16[16,2176]{1,0:T(8,128)(2,1)S(1)}, bf16[16,2176]{1,0:T(8,128)(2,1)S(1)}, u32[]{:S(2)}, u32[]{:S(2)}) collective-permute-start(bf16[16,2176]{1,0:T(8,128)(2,1)S(1)} %get-tuple-element.30), channel_id=1, source_target_pairs={{0,8},{4,12},{8,0},{12,4},{1,9},{5,13},{9,1},{13,5},{2,10},{6,14},... | collective-permute-start | bytes 208904 | tf_op jit(solution)/shard_map/ppermute | solution.py:24
  8.8 6.2 %collective-permute-start.2 = (bf16[16,2176]{1,0:T(8,128)(2,1)S(1)}, bf16[16,2176]{1,0:T(8,128)(2,1)S(1)}, u32[]{:S(2)}, u32[]{:S(2)}) collective-permute-start(bf16[16,2176]{1,0:T(8,128)(2,1)S(1)} %get-tuple-element.31), channel_id=1, source_target_pairs={{0,12},{4,8},{8,4},{12,0},{1,13},{5,9},{9,5},{13,1},{2,14},{6,10},... | collective-permute-start | bytes 208904 | tf_op jit(solution)/shard_map/ppermute | solution.py:24
  9.0 6.0 %collective-permute-start = (bf16[16,2176]{1,0:T(8,128)(2,1)S(1)}, bf16[16,2176]{1,0:T(8,128)(2,1)S(1)}, u32[]{:S(2)}, u32[]{:S(2)}) collective-permute-start(bf16[16,2176]{1,0:T(8,128)(2,1)S(1)} %get-tuple-element.29), channel_id=1, source_target_pairs={{0,4},{4,0},{8,12},{12,8},{1,5},{5,1},{9,13},{13,9},{2,6},{6,2},{1... | collective-permute-start | bytes 208904 | tf_op jit(solution)/shard_map/ppermute | solution.py:24
  9.7 5.4 %collective-permute-start.6 = (bf16[16,2176]{1,0:T(8,128)(2,1)S(1)}, bf16[16,2176]{1,0:T(8,128)(2,1)S(1)}, u32[]{:S(2)}, u32[]{:S(2)}) collective-permute-start(bf16[16,2176]{1,0:T(8,128)(2,1)S(1)} %get-tuple-element.28.refs_0_), channel_id=1, source_target_pairs={{0,2},{1,3},{2,0},{3,1},{4,6},{5,7},{6,4},{7,5},{8,10},{9,11},{10,... | collective-permute-start | bytes 208904 | tf_op jit(solution)/shard_map/ppermute | solution.py:24
  15.1 5.1 %collective-permute-start.7 = (bf16[32,2176]{1,0:T(8,128)(2,1)S(1)}, bf16[32,2176]{1,0:T(8,128)(2,1)S(1)}, u32[]{:S(2)}, u32[]{:S(2)}) collective-permute-start(bf16[32,2176]{1,0:T(8,128)(2,1)S(1)} %tie.2), channel_id=1, source_target_pairs={{0,2},{1,3},{2,0},{3,1},{4,6},{5,7},{6,4},{7,5},{8,10},{9,11},{10,... | collective-permute-start | bytes 417800 | tf_op jit(solution)/shard_map/ppermute | solution.py:24
  15.7 4.5 %collective-permute-start.4 = (bf16[32,2176]{1,0:T(8,128)(2,1)S(1)}, bf16[32,2176]{1,0:T(8,128)(2,1)S(1)}, u32[]{:S(2)}, u32[]{:S(2)}) collective-permute-start(bf16[32,2176]{1,0:T(8,128)(2,1)S(1)} %join.6.refs_2_.refs_1_.refs_0_), channel_id=1, source_target_pairs={{0,1},{1,0},{2,3},{3,2},{4,5},{5,4},{6,7},{7,6},{8,9},{9,8},{10,11... | collective-permute-start | bytes 417800 | tf_op jit(solution)/shard_map/ppermute | solution.py:24
  15.7 5.3 %collective-permute-start.8 = (bf16[32,2176]{1,0:T(8,128)(2,1)S(1)}, bf16[32,2176]{1,0:T(8,128)(2,1)S(1)}, u32[]{:S(2)}, u32[]{:S(2)}) collective-permute-start(bf16[32,2176]{1,0:T(8,128)(2,1)S(1)} %join.9.refs_4_), channel_id=1, source_target_pairs={{0,1},{1,0},{2,3},{3,2},{4,5},{5,4},{6,7},{7,6},{8,9},{9,8},{10,11... | collective-permute-start | bytes 417800 | tf_op jit(solution)/shard_map/ppermute | solution.py:24
  16.2 4.0 %collective-permute-start.5 = (bf16[32,2176]{1,0:T(8,128)(2,1)S(1)}, bf16[32,2176]{1,0:T(8,128)(2,1)S(1)}, u32[]{:S(2)}, u32[]{:S(2)}) collective-permute-start(bf16[32,2176]{1,0:T(8,128)(2,1)S(1)} %join.7.refs_2_.refs_1_), channel_id=1, source_target_pairs={{0,1},{1,0},{2,3},{3,2},{4,5},{5,4},{6,7},{7,6},{8,9},{9,8},{10,11... | collective-permute-start | bytes 417800 | tf_op jit(solution)/shard_map/ppermute | solution.py:24
  20.2 1.4 %collective-permute-start.9 = (bf16[32,2176]{1,0:T(8,128)(2,1)S(1)}, bf16[32,2176]{1,0:T(8,128)(2,1)S(1)}, u32[]{:S(2)}, u32[]{:S(2)}) collective-permute-start(bf16[32,2176]{1,0:T(8,128)(2,1)S(1)} %tie.3.refs_5_), channel_id=1, source_target_pairs={{0,1},{1,0},{2,3},{3,2},{4,5},{5,4},{6,7},{7,6},{8,9},{9,8},{10,11... | collective-permute-start | bytes 417800 | tf_op jit(solution)/shard_map/ppermute | solution.py:24
  22.3 1.5 %collective-permute-start.11 = (bf16[64,1792]{1,0:T(8,128)(2,1)S(1)}, bf16[64,1792]{1,0:T(8,128)(2,1)S(1)}, u32[]{:S(2)}, u32[]{:S(2)}) collective-permute-start(bf16[64,1792]{1,0:T(8,128)(2,1)S(1)} %get-tuple-element.40), channel_id=1, source_target_pairs={{0,1},{1,0},{2,3},{3,2},{4,5},{5,4},{6,7},{7,6},{8,9},{9,8},{10,11... | collective-permute-start | bytes 688136 | tf_op jit(solution)/shard_map/ppermute | solution.py:24
  22.7 5.8 %collective-permute-start.10 = (bf16[64,1792]{1,0:T(8,128)(2,1)S(1)}, bf16[64,1792]{1,0:T(8,128)(2,1)S(1)}, u32[]{:S(2)}, u32[]{:S(2)}) collective-permute-start(bf16[64,1792]{1,0:T(8,128)(2,1)S(1)} %down.3), channel_id=1, source_target_pairs={{0,1},{1,0},{2,3},{3,2},{4,5},{5,4},{6,7},{7,6},{8,9},{9,8},{10,11... | collective-permute-start | bytes 688136 | tf_op jit(solution)/shard_map/ppermute | solution.py:24
  23.8 6.0 %collective-permute-start.13 = (bf16[32,1792]{1,0:T(8,128)(2,1)S(1)}, bf16[32,1792]{1,0:T(8,128)(2,1)S(1)}, u32[]{:S(2)}, u32[]{:S(2)}) collective-permute-start(bf16[32,1792]{1,0:T(8,128)(2,1)S(1)} %get-tuple-element.43), channel_id=1, source_target_pairs={{0,2},{1,3},{2,0},{3,1},{4,6},{5,7},{6,4},{7,5},{8,10},{9,11},{10,... | collective-permute-start | bytes 344072 | tf_op jit(solution)/shard_map/ppermute | solution.py:24
  24.4 10.7 %collective-permute-start.12 = (bf16[16,1792]{1,0:T(8,128)(2,1)S(1)}, bf16[16,1792]{1,0:T(8,128)(2,1)S(1)}, u32[]{:S(2)}, u32[]{:S(2)}) collective-permute-start(bf16[16,1792]{1,0:T(8,128)(2,1)S(1)} %get-tuple-element.41), channel_id=1, source_target_pairs={{0,2},{1,3},{2,0},{3,1},{4,6},{5,7},{6,4},{7,5},{8,10},{9,11},{10,... | collective-permute-start | bytes 172040 | tf_op jit(solution)/shard_map/ppermute | solution.py:24
  25.9 9.2 %collective-permute-start.17 = (bf16[16,1792]{1,0:T(8,128)(2,1)S(1)}, bf16[16,1792]{1,0:T(8,128)(2,1)S(1)}, u32[]{:S(2)}, u32[]{:S(2)}) collective-permute-start(bf16[16,1792]{1,0:T(8,128)(2,1)S(1)} %get-tuple-element.47), channel_id=1, source_target_pairs={{0,14},{1,15},{2,12},{3,13},{4,10},{5,11},{6,8},{7,9},{8,6},{9,7},... | collective-permute-start | bytes 172040 | tf_op jit(solution)/shard_map/ppermute | solution.py:34
  28.6 6.5 %collective-permute-start.16 = (bf16[16,1792]{1,0:T(8,128)(2,1)S(1)}, bf16[16,1792]{1,0:T(8,128)(2,1)S(1)}, u32[]{:S(2)}, u32[]{:S(2)}) collective-permute-start(bf16[16,1792]{1,0:T(8,128)(2,1)S(1)} %get-tuple-element.46), channel_id=1, source_target_pairs={{0,12},{4,8},{8,4},{12,0},{1,13},{5,9},{9,5},{13,1},{2,14},{6,10},... | collective-permute-start | bytes 172040 | tf_op jit(solution)/shard_map/ppermute | solution.py:24
  29.9 5.3 %collective-permute-start.14 = (bf16[16,1792]{1,0:T(8,128)(2,1)S(1)}, bf16[16,1792]{1,0:T(8,128)(2,1)S(1)}, u32[]{:S(2)}, u32[]{:S(2)}) collective-permute-start(bf16[16,1792]{1,0:T(8,128)(2,1)S(1)} %get-tuple-element.44), channel_id=1, source_target_pairs={{0,4},{4,0},{8,12},{12,8},{1,5},{5,1},{9,13},{13,9},{2,6},{6,2},{1... | collective-permute-start | bytes 172040 | tf_op jit(solution)/shard_map/ppermute | solution.py:24
  31.2 5.1 %collective-permute-start.15 = (bf16[16,1792]{1,0:T(8,128)(2,1)S(1)}, bf16[16,1792]{1,0:T(8,128)(2,1)S(1)}, u32[]{:S(2)}, u32[]{:S(2)}) collective-permute-start(bf16[16,1792]{1,0:T(8,128)(2,1)S(1)} %get-tuple-element.45), channel_id=1, source_target_pairs={{0,8},{4,12},{8,0},{12,4},{1,9},{5,13},{9,1},{13,5},{2,10},{6,14},... | collective-permute-start | bytes 172040 | tf_op jit(solution)/shard_map/ppermute | solution.py:24
